TPU v7x, 512 devices: a whole 4x8x8 slice. The times are simulated.
512 devices in a mesh: chan: 64 (over z_hi, y, x), freq: 8 (over z_lo, core).
Axes of the slice: x: 4, y: 8, z: 8 (z_hi: 2, z_lo: 4; z = z_hi * 4 + z_lo), core: 2. Of those that a mesh axis runs over, the one named last changes fastest.
Arguments:
- spectra: bfloat16 [16384, 64, 128], P('chan', 'freq'), may hold values from -6 to 6
- half_width: int32 [16384], P('chan'), may hold values from 1 to 4, as said below
- partners: int32 [3, 64], replicated, may hold values from 0 to 63, as said below
Outputs:
- correlations: bfloat16 [8, 4, 16384, 256], P('freq', None, 'chan')
Inputs may be any that keep to these rules, and one draw needn't show every extreme that they name: partners[r, i] = i XOR m_r, where the 3 round masks m_r are distinct and lie in 1 .. 63. `half_width`: some channel has exactly 4.
All inputs are finite; a program needn't handle non-finite values.
Results may differ from a plain program's by a relative error of at most 0.017.
Values may be sent and summed in bfloat16 or wider, within the bound.
No kernel may reach another device: no remote copies, remote signals or barrier semaphores. Data moves between devices by JAX's collectives and lax.ppermute only.
A program may use at most 64 MiB of HBM per device.

v0:
```python
import jax
import jax.numpy as jnp
from jax import lax
from jax.sharding import PartitionSpec as P

HMAX = 4
ROUNDS = 3
LAG_DEV = 1


def with_halo(array, sides, width):
    for axis, dim in sides:
        size, length = (lax.axis_size(axis), array.shape[dim])
        up = [(i, (i + 1) % size) for i in range(size - 1)]
        down = [(j, i) for i, j in up]
        last = lax.slice_in_dim(array, length - width, length, axis=dim)
        first = lax.slice_in_dim(array, 0, width, axis=dim)
        before = lax.ppermute(last, axis, up)
        after = lax.ppermute(first, axis, down)
        array = jnp.concatenate([before, array, after], axis=dim)
    return array


def partner(block, axis, bit):
    count = lax.axis_size(axis)
    route = []
    for low in range(count):
        high = low | 1 << bit
        if high != low and high < count:
            route += [(low, high), (high, low)]
    return lax.ppermute(block, axis, route)


def whiten_padded(spectra, padded, half_width):
    seg_count = spectra.shape[-1] // 2
    bin_count = spectra.shape[1]
    widened = padded.astype(jnp.float32)
    powers = widened[..., :seg_count] ** 2 + widened[..., seg_count:] ** 2
    window_sum = jnp.zeros((spectra.shape[0], bin_count, seg_count), jnp.float32)
    for offset in range(-HMAX, HMAX + 1):
        window = powers[:, HMAX + offset : HMAX + offset + bin_count]
        window_sum = window_sum + jnp.where(
            abs(offset) <= half_width[:, None, None], window, jnp.float32(0.0)
        )
    smooth = window_sum / (2 * half_width + 1).astype(jnp.float32)[:, None, None]
    inverse = lax.rsqrt(jnp.maximum(smooth, jnp.float32(0.5)))
    return (spectra.astype(jnp.float32) * jnp.concatenate([inverse, inverse], -1)).astype(
        jnp.bfloat16
    )


def cross_pair(left_block, right_block):
    seg_count = left_block.shape[-1] // 2
    turned = jnp.concatenate([left_block[..., seg_count:], -left_block[..., :seg_count]], -1)
    real_part = jnp.einsum(
        "agk,bgk->gab", left_block, right_block, preferred_element_type=jnp.float32
    )
    imag_part = jnp.einsum("agk,bgk->gab", turned, right_block, preferred_element_type=jnp.float32)
    return (real_part, imag_part)


def lag_terms(real_part, imag_part, cosine, sine_table):
    result = jnp.einsum("gab,gl->lab", real_part, cosine, precision=lax.Precision.HIGHEST)
    return result - jnp.einsum(
        "gab,gl->lab", imag_part, sine_table, precision=lax.Precision.HIGHEST
    )


def shards(spectra, half_width, partners):
    freq_count = lax.axis_size("freq")
    bin_dev = spectra.shape[1]
    bin_count = bin_dev * freq_count
    lag_count = LAG_DEV * freq_count
    seg_count = spectra.shape[-1] // 2
    padded = with_halo(spectra, (("freq", 1),), HMAX)
    white = whiten_padded(spectra, padded, half_width)
    bin_global = (lax.axis_index("freq") * bin_dev + jnp.arange(bin_dev, dtype=jnp.int32)).astype(
        jnp.float32
    )
    lag_index = jnp.arange(lag_count, dtype=jnp.float32)
    theta = 2.0 * jnp.pi * bin_global[:, None] * lag_index[None, :] / bin_count
    factor = 1.0 / jnp.sqrt(jnp.float32(seg_count * bin_count))
    cosine = jnp.cos(theta) * factor
    sine_table = jnp.sin(theta) * factor
    block_index = lax.axis_index("chan")
    bit_count = lax.axis_size("chan").bit_length() - 1
    partner_blocks = [white]
    for round_index in range(ROUNDS):
        round_mask = jnp.bitwise_xor(partners[round_index, block_index], block_index)
        current = white
        bit_order = list(range(bit_count))
        for bit_number in bit_order:
            arrived = partner(current, "chan", bit_number)
            current = jnp.where(round_mask >> bit_number & 1 == 1, arrived, current)
        partner_blocks.append(current)
    results = []
    for partner_block in partner_blocks:
        real_part, imag_part = cross_pair(white, partner_block)

        def pair_terms(first_lag, lag_rows, real_part=real_part, imag_part=imag_part):
            return lag_terms(real_part, imag_part, cosine, sine_table)

        results.append(
            lax.psum_scatter(
                pair_terms(jnp.int32(0), LAG_DEV * lax.axis_size("freq")).astype(jnp.bfloat16),
                "freq",
                scatter_dimension=0,
                tiled=True,
            ).astype(jnp.float32)
        )
    return jnp.stack(results, 1).astype(jnp.bfloat16)


def solution(mesh):
    return jax.shard_map(
        shards,
        mesh=mesh,
        in_specs=(P("chan", "freq", None), P("chan"), P()),
        out_specs=P("freq", None, "chan", None),
        check_vma=False,
    )
```

profile of v0, /device:TPU:1, one launch (start us, length us, event | category | flops | bytes accessed | tf_op | source)
XLA Modules:
  0.0 349.2 jit_solution(14058983762538551212)
XLA Ops:
  7.7 8.8 %collective-permute-start.1 = (bf16[256,4,128]{2,0,1:T(8,128)(2,1)S(1)}, bf16[256,4,128]{2,0,1:T(8,128)(2,1)S(1)}, u32[]{:S(2)}, u32[]{:S(2)}) collective-permute-start(bf16[256,4,128]{2,0,1:T(8,128)(2,1)S(1)} %get-tuple-element.11), channel_id=1, source_target_pairs={{1,0},{2,1},{3,2},{4,3},{5,4},{6,5},{7,6},{9,8},{10,9},{11,10},{12... | collective-permute-start | bytes 786440 | tf_op jit(solution)/shard_map/ppermute | solution.py:19
  18.5 3.2 collective-permute-done
  28.8 9.8 %collective-permute-done.2 = bf16[256,8,128]{2,0,1:T(8,128)(2,1)S(1)} collective-permute-done((bf16[256,8,128]{2,0,1:T(8,128)(2,1)S(1)}, bf16[256,8,128]{2,0,1:T(8,128)(2,1)S(1)}, u32[]{:S(2)}, u32[]{:S(2)}) %collective-permute-start.2) | collective-permute-done | bytes 524320 | tf_op jit(solution)/shard_map/ppermute | solution.py:31
  41.7 14.3 %collective-permute-done.13 = bf16[256,8,128]{2,0,1:T(8,128)(2,1)S(1)} collective-permute-done((bf16[256,8,128]{2,0,1:T(8,128)(2,1)S(1)}, bf16[256,8,128]{2,0,1:T(8,128)(2,1)S(1)}, u32[]{:S(2)}, u32[]{:S(2)}) %collective-permute-start.13) | collective-permute-done | bytes 524320 | tf_op jit(solution)/shard_map/ppermute | solution.py:31
  58.4 2.9 fusion.13
  63.2 7.8 %collective-permute-done.14 = bf16[256,8,128]{2,0,1:T(8,128)(2,1)S(1)} collective-permute-done((bf16[256,8,128]{2,0,1:T(8,128)(2,1)S(1)}, bf16[256,8,128]{2,0,1:T(8,128)(2,1)S(1)}, u32[]{:S(2)}, u32[]{:S(2)}) %collective-permute-start.14) | collective-permute-done | bytes 524320 | tf_op jit(solution)/shard_map/ppermute | solution.py:31
  71.1 1.9 collective-permute-start.15
  73.0 3.0 subtract_convert_fusion.3
  79.3 2.2 collective-permute-start.9
  81.6 17.5 %collective-permute-done.15 = bf16[256,8,128]{2,0,1:T(8,128)(2,1)} collective-permute-done((bf16[256,8,128]{2,0,1:T(8,128)(2,1)S(1)}, bf16[256,8,128]{2,0,1:T(8,128)(2,1)}, u32[]{:S(2)}, u32[]{:S(2)}) %collective-permute-start.15) | collective-permute-done | bytes 524320 | tf_op jit(solution)/shard_map/ppermute | solution.py:31
  104.1 11.1 %collective-permute-done.9 = bf16[256,8,128]{2,0,1:T(8,128)(2,1)S(1)} collective-permute-done((bf16[256,8,128]{2,0,1:T(8,128)(2,1)S(1)}, bf16[256,8,128]{2,0,1:T(8,128)(2,1)S(1)}, u32[]{:S(2)}, u32[]{:S(2)}) %collective-permute-start.9) | collective-permute-done | bytes 524320 | tf_op jit(solution)/shard_map/ppermute | solution.py:31
  117.2 6.7 %collective-permute-done.16 = bf16[256,8,128]{2,0,1:T(8,128)(2,1)S(1)} collective-permute-done((bf16[256,8,128]{2,0,1:T(8,128)(2,1)S(1)}, bf16[256,8,128]{2,0,1:T(8,128)(2,1)S(1)}, u32[]{:S(2)}, u32[]{:S(2)}) %collective-permute-start.16) | collective-permute-done | bytes 524320 | tf_op jit(solution)/shard_map/ppermute | solution.py:31
  124.0 3.9 %collective-permute-start.17 = (bf16[256,8,128]{2,0,1:T(8,128)(2,1)S(1)}, bf16[256,8,128]{2,0,1:T(8,128)(2,1)S(1)}, u32[]{:S(2)}, u32[]{:S(2)}) collective-permute-start(bf16[256,8,128]{2,0,1:T(8,128)(2,1)S(1)} %broadcast_select_fusion.4), channel_id=1, source_target_pairs={{0,256},{256,0},{8,264},{264,8},{16,272},{272,16},{24,280},{280,24... | collective-permute-start | bytes 1572872 | tf_op jit(solution)/shard_map/ppermute | solution.py:31
  128.0 15.5 %collective-permute-done.4 = bf16[256,8,128]{2,0,1:T(8,128)(2,1)S(1)} collective-permute-done((bf16[256,8,128]{2,0,1:T(8,128)(2,1)S(1)}, bf16[256,8,128]{2,0,1:T(8,128)(2,1)S(1)}, u32[]{:S(2)}, u32[]{:S(2)}) %collective-permute-start.4) | collective-permute-done | bytes 524320 | tf_op jit(solution)/shard_map/ppermute | solution.py:31
  143.5 7.9 %collective-permute-start.5 = (bf16[256,8,128]{2,0,1:T(8,128)(2,1)S(1)}, bf16[256,8,128]{2,0,1:T(8,128)(2,1)}, u32[]{:S(2)}, u32[]{:S(2)}) collective-permute-start(bf16[256,8,128]{2,0,1:T(8,128)(2,1)S(1)} %broadcast_select_fusion.14), channel_id=1, source_target_pairs={{0,64},{64,0},{8,72},{72,8},{16,80},{80,16},{24,88},{88,24},{32,96... | collective-permute-start | bytes 1572872 | tf_op jit(solution)/shard_map/ppermute | solution.py:31
  151.7 4.1 %collective-permute-start.11 = (bf16[256,8,128]{2,0,1:T(8,128)(2,1)S(1)}, bf16[256,8,128]{2,0,1:T(8,128)(2,1)S(1)}, u32[]{:S(2)}, u32[]{:S(2)}) collective-permute-start(bf16[256,8,128]{2,0,1:T(8,128)(2,1)S(1)} %broadcast_select_fusion.9), channel_id=1, source_target_pairs={{0,128},{128,0},{8,136},{136,8},{16,144},{144,16},{24,152},{152,24... | collective-permute-start | bytes 1572872 | tf_op jit(solution)/shard_map/ppermute | solution.py:31
  156.2 2.9 fusion.1
  159.6 3.0 subtract_convert_fusion
  163.8 23.9 %collective-permute-done.11 = bf16[256,8,128]{2,0,1:T(8,128)(2,1)S(1)} collective-permute-done((bf16[256,8,128]{2,0,1:T(8,128)(2,1)S(1)}, bf16[256,8,128]{2,0,1:T(8,128)(2,1)S(1)}, u32[]{:S(2)}, u32[]{:S(2)}) %collective-permute-start.11) | collective-permute-done | bytes 524320 | tf_op jit(solution)/shard_map/ppermute | solution.py:31
  187.8 5.9 %collective-permute-start.12 = (bf16[256,8,128]{2,0,1:T(8,128)(2,1)S(1)}, bf16[256,8,128]{2,0,1:T(8,128)(2,1)S(1)}, u32[]{:S(2)}, u32[]{:S(2)}) collective-permute-start(bf16[256,8,128]{2,0,1:T(8,128)(2,1)S(1)} %broadcast_select_fusion.10), channel_id=1, source_target_pairs={{0,256},{256,0},{8,264},{264,8},{16,272},{272,16},{24,280},{280,24... | collective-permute-start | bytes 1572872 | tf_op jit(solution)/shard_map/ppermute | solution.py:31
  193.7 3.7 %collective-permute-done.5 = bf16[256,8,128]{2,0,1:T(8,128)(2,1)} collective-permute-done((bf16[256,8,128]{2,0,1:T(8,128)(2,1)S(1)}, bf16[256,8,128]{2,0,1:T(8,128)(2,1)}, u32[]{:S(2)}, u32[]{:S(2)}) %collective-permute-start.5) | collective-permute-done | bytes 524320 | tf_op jit(solution)/shard_map/ppermute | solution.py:31
  198.5 6.0 %collective-permute-start.6 = (bf16[256,8,128]{2,0,1:T(8,128)(2,1)S(1)}, bf16[256,8,128]{2,0,1:T(8,128)(2,1)S(1)}, u32[]{:S(2)}, u32[]{:S(2)}) collective-permute-start(bf16[256,8,128]{2,0,1:T(8,128)(2,1)S(1)} %broadcast_select_fusion.15), channel_id=1, source_target_pairs={{0,128},{128,0},{8,136},{136,8},{16,144},{144,16},{24,152},{152,24... | collective-permute-start | bytes 1572872 | tf_op jit(solution)/shard_map/ppermute | solution.py:31
  204.5 15.0 %collective-permute-done.12 = bf16[256,8,128]{2,0,1:T(8,128)(2,1)S(1)} collective-permute-done((bf16[256,8,128]{2,0,1:T(8,128)(2,1)S(1)}, bf16[256,8,128]{2,0,1:T(8,128)(2,1)S(1)}, u32[]{:S(2)}, u32[]{:S(2)}) %collective-permute-start.12) | collective-permute-done | bytes 524320 | tf_op jit(solution)/shard_map/ppermute | solution.py:31
  220.0 2.9 fusion.5
  223.3 3.0 subtract_convert_fusion.1
  227.7 4.3 %collective-permute-start.7 = (bf16[256,8,128]{2,0,1:T(8,128)(2,1)S(1)}, bf16[256,8,128]{2,0,1:T(8,128)(2,1)S(1)}, u32[]{:S(2)}, u32[]{:S(2)}) collective-permute-start(bf16[256,8,128]{2,0,1:T(8,128)(2,1)S(1)} %broadcast_select_fusion.16), channel_id=1, source_target_pairs={{0,256},{256,0},{8,264},{264,8},{16,272},{272,16},{24,280},{280,24... | collective-permute-start | bytes 1572872 | tf_op jit(solution)/shard_map/ppermute | solution.py:31
  232.0 20.2 %collective-permute-done.7 = bf16[256,8,128]{2,0,1:T(8,128)(2,1)S(1)} collective-permute-done((bf16[256,8,128]{2,0,1:T(8,128)(2,1)S(1)}, bf16[256,8,128]{2,0,1:T(8,128)(2,1)S(1)}, u32[]{:S(2)}, u32[]{:S(2)}) %collective-permute-start.7) | collective-permute-done | bytes 524320 | tf_op jit(solution)/shard_map/ppermute | solution.py:31
  253.1 2.9 fusion.9
  256.0 3.0 subtract_convert_fusion.2
  260.3 38.6 %reduce-scatter.9.cloned.1.call-done = bf16[1,256,256]{2,1,0:T(8,128)(2,1)} async-done(((bf16[8,256,256]{2,1,0:T(8,128)(2,1)}), bf16[1,256,256]{2,1,0:T(8,128)(2,1)}) %reduce-scatter.9.cloned.1.call-update) | async-done | bytes 131088 | tf_op jit(solution)/shard_map/reduce_scatter | solution.py:104
  298.9 41.9 %reduce-scatter.7.cloned.1.call-done = bf16[1,256,256]{2,1,0:T(8,128)(2,1)} async-done(((bf16[8,256,256]{2,1,0:T(8,128)(2,1)}), bf16[1,256,256]{2,1,0:T(8,128)(2,1)}) %reduce-scatter.7.cloned.1.call-update) | async-done | bytes 131088 | tf_op jit(solution)/shard_map/reduce_scatter | solution.py:104
  340.7 2.0 pad_maximum_fusion.1
  (68 shorter events, 33.7 us)
Async XLA Ops:
  6.5 11.9 %copy-start.1 = (s32[256]{0:T(256)S(1)}, s32[256]{0:T(256)}, u32[]{:S(2)}) copy-start(s32[256]{0:T(256)} %param.4) | copy-start | bytes 3076
  6.5 253.7 %reduce-scatter.5.cloned.1.call-start = ((), (), s32[]{:S(2)}) async-start(), calls=%async_computation.4 | async-start | bytes 1179648 | tf_op jit(solution)/shard_map/reduce_scatter | solution.py:104
  7.7 10.8 %collective-permute-start.1 = (bf16[256,4,128]{2,0,1:T(8,128)(2,1)S(1)}, bf16[256,4,128]{2,0,1:T(8,128)(2,1)S(1)}, u32[]{:S(2)}, u32[]{:S(2)}) collective-permute-start(bf16[256,4,128]{2,0,1:T(8,128)(2,1)S(1)} %get-tuple-element.11), channel_id=1, source_target_pairs={{1,0},{2,1},{3,2},{4,3},{5,4},{6,5},{7,6},{9,8},{10,9},{11,10},{12... | collective-permute-start | bytes 786440 | tf_op jit(solution)/shard_map/ppermute | solution.py:19
  16.5 5.2 %collective-permute-start = (bf16[256,4,128]{2,0,1:T(8,128)(2,1)S(1)}, bf16[256,4,128]{2,0,1:T(8,128)(2,1)S(1)}, u32[]{:S(2)}, u32[]{:S(2)}) collective-permute-start(bf16[256,4,128]{2,0,1:T(8,128)(2,1)S(1)} %get-tuple-element.10), channel_id=1, source_target_pairs={{0,1},{1,2},{2,3},{3,4},{4,5},{5,6},{6,7},{8,9},{9,10},{10,11},{11... | collective-permute-start | bytes 786440 | tf_op jit(solution)/shard_map/ppermute | solution.py:18
  22.5 1.5 copy-start
  24.0 2.3 copy-start.2
  24.3 14.3 %collective-permute-start.2 = (bf16[256,8,128]{2,0,1:T(8,128)(2,1)S(1)}, bf16[256,8,128]{2,0,1:T(8,128)(2,1)S(1)}, u32[]{:S(2)}, u32[]{:S(2)}) collective-permute-start(bf16[256,8,128]{2,0,1:T(8,128)(2,1)S(1)} %fusion.36), channel_id=1, source_target_pairs={{0,8},{8,0},{16,24},{24,16},{32,40},{40,32},{48,56},{56,48},{64,72... | collective-permute-start | bytes 1572872 | tf_op jit(solution)/shard_map/ppermute | solution.py:31
  38.8 17.2 %collective-permute-start.13 = (bf16[256,8,128]{2,0,1:T(8,128)(2,1)S(1)}, bf16[256,8,128]{2,0,1:T(8,128)(2,1)S(1)}, u32[]{:S(2)}, u32[]{:S(2)}) collective-permute-start(bf16[256,8,128]{2,0,1:T(8,128)(2,1)S(1)} %get-tuple-element.6), channel_id=1, source_target_pairs={{0,16},{16,0},{8,24},{24,8},{32,48},{48,32},{40,56},{56,40},{64,80... | collective-permute-start | bytes 1572872 | tf_op jit(solution)/shard_map/ppermute | solution.py:31
  56.0 15.0 %collective-permute-start.14 = (bf16[256,8,128]{2,0,1:T(8,128)(2,1)S(1)}, bf16[256,8,128]{2,0,1:T(8,128)(2,1)S(1)}, u32[]{:S(2)}, u32[]{:S(2)}) collective-permute-start(bf16[256,8,128]{2,0,1:T(8,128)(2,1)S(1)} %broadcast_select_fusion.1), channel_id=1, source_target_pairs={{0,32},{32,0},{8,40},{40,8},{16,48},{48,16},{24,56},{56,24},{64,96... | collective-permute-start | bytes 1572872 | tf_op jit(solution)/shard_map/ppermute | solution.py:31
  61.3 18.0 %collective-permute-start.8 = (bf16[256,8,128]{2,0,1:T(8,128)(2,1)S(1)}, bf16[256,8,128]{2,0,1:T(8,128)(2,1)S(1)}, u32[]{:S(2)}, u32[]{:S(2)}) collective-permute-start(bf16[256,8,128]{2,0,1:T(8,128)(2,1)S(1)} %get-tuple-element.7), channel_id=1, source_target_pairs={{0,16},{16,0},{8,24},{24,8},{32,48},{48,32},{40,56},{56,40},{64,80... | collective-permute-start | bytes 1572872 | tf_op jit(solution)/shard_map/ppermute | solution.py:31
  71.1 28.0 %collective-permute-start.15 = (bf16[256,8,128]{2,0,1:T(8,128)(2,1)S(1)}, bf16[256,8,128]{2,0,1:T(8,128)(2,1)}, u32[]{:S(2)}, u32[]{:S(2)}) collective-permute-start(bf16[256,8,128]{2,0,1:T(8,128)(2,1)S(1)} %broadcast_select_fusion.2), channel_id=1, source_target_pairs={{0,64},{64,0},{8,72},{72,8},{16,80},{80,16},{24,88},{88,24},{32,96... | collective-permute-start | bytes 1572872 | tf_op jit(solution)/shard_map/ppermute | solution.py:31
  77.3 183.0 %reduce-scatter.11.cloned.1.call-start = ((), (), s32[]{:S(2)}) async-start(), calls=%async_computation.7 | async-start | bytes 1179648 | tf_op jit(solution)/shard_map/reduce_scatter | solution.py:104
  77.3 24.8 %collective-permute-start.3 = (bf16[256,8,128]{2,0,1:T(8,128)(2,1)S(1)}, bf16[256,8,128]{2,0,1:T(8,128)(2,1)S(1)}, u32[]{:S(2)}, u32[]{:S(2)}) collective-permute-start(bf16[256,8,128]{2,0,1:T(8,128)(2,1)S(1)} %get-tuple-element.5), channel_id=1, source_target_pairs={{0,16},{16,0},{8,24},{24,8},{32,48},{48,32},{40,56},{56,40},{64,80... | collective-permute-start | bytes 1572872 | tf_op jit(solution)/shard_map/ppermute | solution.py:31
  79.3 35.9 %collective-permute-start.9 = (bf16[256,8,128]{2,0,1:T(8,128)(2,1)S(1)}, bf16[256,8,128]{2,0,1:T(8,128)(2,1)S(1)}, u32[]{:S(2)}, u32[]{:S(2)}) collective-permute-start(bf16[256,8,128]{2,0,1:T(8,128)(2,1)S(1)} %broadcast_select_fusion.7), channel_id=1, source_target_pairs={{0,32},{32,0},{8,40},{40,8},{16,48},{48,16},{24,56},{56,24},{64,96... | collective-permute-start | bytes 1572872 | tf_op jit(solution)/shard_map/ppermute | solution.py:31
  100.2 23.8 %collective-permute-start.16 = (bf16[256,8,128]{2,0,1:T(8,128)(2,1)S(1)}, bf16[256,8,128]{2,0,1:T(8,128)(2,1)S(1)}, u32[]{:S(2)}, u32[]{:S(2)}) collective-permute-start(bf16[256,8,128]{2,0,1:T(8,128)(2,1)S(1)} %broadcast_select_fusion.3), channel_id=1, source_target_pairs={{0,128},{128,0},{8,136},{136,8},{16,144},{144,16},{24,152},{152,24... | collective-permute-start | bytes 1572872 | tf_op jit(solution)/shard_map/ppermute | solution.py:31
  102.2 41.3 %collective-permute-start.4 = (bf16[256,8,128]{2,0,1:T(8,128)(2,1)S(1)}, bf16[256,8,128]{2,0,1:T(8,128)(2,1)S(1)}, u32[]{:S(2)}, u32[]{:S(2)}) collective-permute-start(bf16[256,8,128]{2,0,1:T(8,128)(2,1)S(1)} %broadcast_select_fusion.13), channel_id=1, source_target_pairs={{0,32},{32,0},{8,40},{40,8},{16,48},{48,16},{24,56},{56,24},{64,96... | collective-permute-start | bytes 1572872 | tf_op jit(solution)/shard_map/ppermute | solution.py:31
  115.3 36.3 %collective-permute-start.10 = (bf16[256,8,128]{2,0,1:T(8,128)(2,1)S(1)}, bf16[256,8,128]{2,0,1:T(8,128)(2,1)S(1)}, u32[]{:S(2)}, u32[]{:S(2)}) collective-permute-start(bf16[256,8,128]{2,0,1:T(8,128)(2,1)S(1)} %broadcast_select_fusion.8), channel_id=1, source_target_pairs={{0,64},{64,0},{8,72},{72,8},{16,80},{80,16},{24,88},{88,24},{32,96... | collective-permute-start | bytes 1572872 | tf_op jit(solution)/shard_map/ppermute | solution.py:31
  124.0 31.8 %collective-permute-start.17 = (bf16[256,8,128]{2,0,1:T(8,128)(2,1)S(1)}, bf16[256,8,128]{2,0,1:T(8,128)(2,1)S(1)}, u32[]{:S(2)}, u32[]{:S(2)}) collective-permute-start(bf16[256,8,128]{2,0,1:T(8,128)(2,1)S(1)} %broadcast_select_fusion.4), channel_id=1, source_target_pairs={{0,256},{256,0},{8,264},{264,8},{16,272},{272,16},{24,280},{280,24... | collective-permute-start | bytes 1572872 | tf_op jit(solution)/shard_map/ppermute | solution.py:31
  143.5 53.9 %collective-permute-start.5 = (bf16[256,8,128]{2,0,1:T(8,128)(2,1)S(1)}, bf16[256,8,128]{2,0,1:T(8,128)(2,1)}, u32[]{:S(2)}, u32[]{:S(2)}) collective-permute-start(bf16[256,8,128]{2,0,1:T(8,128)(2,1)S(1)} %broadcast_select_fusion.14), channel_id=1, source_target_pairs={{0,64},{64,0},{8,72},{72,8},{16,80},{80,16},{24,88},{88,24},{32,96... | collective-permute-start | bytes 1572872 | tf_op jit(solution)/shard_map/ppermute | solution.py:31
  151.7 36.0 %collective-permute-start.11 = (bf16[256,8,128]{2,0,1:T(8,128)(2,1)S(1)}, bf16[256,8,128]{2,0,1:T(8,128)(2,1)S(1)}, u32[]{:S(2)}, u32[]{:S(2)}) collective-permute-start(bf16[256,8,128]{2,0,1:T(8,128)(2,1)S(1)} %broadcast_select_fusion.9), channel_id=1, source_target_pairs={{0,128},{128,0},{8,136},{136,8},{16,144},{144,16},{24,152},{152,24... | collective-permute-start | bytes 1572872 | tf_op jit(solution)/shard_map/ppermute | solution.py:31
  163.8 135.1 %reduce-scatter.9.cloned.1.call-start = ((), (), s32[]{:S(2)}) async-start(), calls=%async_computation.6 | async-start | bytes 1179648 | tf_op jit(solution)/shard_map/reduce_scatter | solution.py:104
  187.8 31.8 %collective-permute-start.12 = (bf16[256,8,128]{2,0,1:T(8,128)(2,1)S(1)}, bf16[256,8,128]{2,0,1:T(8,128)(2,1)S(1)}, u32[]{:S(2)}, u32[]{:S(2)}) collective-permute-start(bf16[256,8,128]{2,0,1:T(8,128)(2,1)S(1)} %broadcast_select_fusion.10), channel_id=1, source_target_pairs={{0,256},{256,0},{8,264},{264,8},{16,272},{272,16},{24,280},{280,24... | collective-permute-start | bytes 1572872 | tf_op jit(solution)/shard_map/ppermute | solution.py:31
  198.5 29.1 %collective-permute-start.6 = (bf16[256,8,128]{2,0,1:T(8,128)(2,1)S(1)}, bf16[256,8,128]{2,0,1:T(8,128)(2,1)S(1)}, u32[]{:S(2)}, u32[]{:S(2)}) collective-permute-start(bf16[256,8,128]{2,0,1:T(8,128)(2,1)S(1)} %broadcast_select_fusion.15), channel_id=1, source_target_pairs={{0,128},{128,0},{8,136},{136,8},{16,144},{144,16},{24,152},{152,24... | collective-permute-start | bytes 1572872 | tf_op jit(solution)/shard_map/ppermute | solution.py:31
  227.6 113.1 %reduce-scatter.7.cloned.1.call-start = ((), (), s32[]{:S(2)}) async-start(), calls=%async_computation.5 | async-start | bytes 1179648 | tf_op jit(solution)/shard_map/reduce_scatter | solution.py:104
  227.7 24.5 %collective-permute-start.7 = (bf16[256,8,128]{2,0,1:T(8,128)(2,1)S(1)}, bf16[256,8,128]{2,0,1:T(8,128)(2,1)S(1)}, u32[]{:S(2)}, u32[]{:S(2)}) collective-permute-start(bf16[256,8,128]{2,0,1:T(8,128)(2,1)S(1)} %broadcast_select_fusion.16), channel_id=1, source_target_pairs={{0,256},{256,0},{8,264},{264,8},{16,272},{272,16},{24,280},{280,24... | collective-permute-start | bytes 1572872 | tf_op jit(solution)/shard_map/ppermute | solution.py:31
Sparse Core Ops, SparseCore 0:
  77.4 37.1 reduce-scatter.4
  163.9 77.0 reduce-scatter.10
  243.9 54.9 reduce-scatter.8
  301.5 39.1 reduce-scatter.6
where the time goes:
time: 354 us; the launch traced here: 349 us
  waiting for transfers between devices  230 us (65%)
  starting transfers between devices  62.5 us (18%)
  matrix products  27.1 us (8%)
  between operations  15.5 us (4%)
  other arithmetic  7.88 us (2%)
  local copies, waits for them, and re-layouts  6.57 us (2%)
    ppermute x16, waiting for transfers between devices, partner(): return lax.ppermute(block, axis, route)  146 us
    reduce_scatter x4, waiting for transfers between devices, shards(): lax.psum_scatter(pair_terms(jnp.int32(0), LAG_DEV * lax.axis_size('freq')...  80.5 us
    ppermute x16, starting transfers between devices, partner(): return lax.ppermute(block, axis, route)  51.7 us
    dot_general x4, matrix products, lag_terms(): jnp.einsum('gab,gl->lab', real_part, cosine, precision=lax.Precision.HIGH...  12 us
    dot_general x4, matrix products, lag_terms(): jnp.einsum('gab,gl->lab', imag_part, sine_table, precision=lax.Precision....  11.5 us
    ppermute x1, starting transfers between devices, with_halo(): after = lax.ppermute(first, axis, down)  8.79 us
  transfers between devices with their start and end apart: 22, of which 15 were waited for; matrix products, arithmetic and copies ran while one was open for 10% of the time, Pallas kernels for 0%

commit v1 on v0

v1 whole, which is shorter than its diff:
```python
import functools

import jax
import jax.numpy as jnp
import numpy as np
from jax import lax
from jax.experimental import pallas as pl
from jax.experimental.pallas import tpu as pltpu
from jax.sharding import PartitionSpec as P

HMAX = 4
ROUNDS = 3
CORES = 2
ROWS = 16
ORDER = (0, 2, 1, 3)
NEAR = 4


def tables(freq_count, bin_dev, seg_count):
    chips = freq_count // CORES
    bin_count = freq_count * bin_dev
    out = np.zeros((freq_count, 2 * chips, CORES * bin_dev, 2 * seg_count), np.float32)
    sign = np.where(np.arange(2 * seg_count) < seg_count, -1.0, 1.0)
    for index in range(freq_count):
        chip, core = index // CORES, index % CORES
        bins = np.concatenate(
            [index * bin_dev + np.arange(bin_dev), (index ^ 1) * bin_dev + np.arange(bin_dev)]
        )
        for d in range(chips):
            lag = (chip ^ ORDER[d]) * CORES + core
            theta = 2.0 * np.pi * ((bins * lag) % bin_count) / bin_count
            factor = 1.0 / np.sqrt(seg_count * bin_count)
            out[index, d] = np.cos(theta)[:, None] * factor
            out[index, chips + d] = np.sin(theta)[:, None] * factor * sign
    return out.reshape(freq_count, 2 * chips, -1)


def whiten_kernel(bin_dev, width, x_ref, low_ref, high_ref, half_ref, out_ref):
    half = width // 2

    def block(ref, rows, index):
        return ref[rows, index * width : (index + 1) * width].astype(jnp.float32)

    def step(i, carry):
        rows = pl.ds(pl.multiple_of(i * ROWS, ROWS), ROWS)
        own = [block(x_ref, rows, g) for g in range(bin_dev)]
        wide = [block(low_ref, rows, g) for g in range(HMAX)]
        wide += own
        wide += [block(high_ref, rows, g) for g in range(HMAX)]
        power = []
        for value in wide:
            square = value * value
            power.append(square + pltpu.roll(square, half, 1))
        hw = half_ref[rows, :]
        scale = 1.0 / (2.0 * hw + 1.0)
        for g in range(bin_dev):
            centre = g + HMAX
            total = power[centre]
            for k in range(1, HMAX + 1):
                both = power[centre - k] + power[centre + k]
                total = total + (both if k == 1 else jnp.where(hw >= k, both, 0.0))
            smooth = jnp.maximum(total * scale, 0.5)
            out_ref[rows, g * width : (g + 1) * width] = (own[g] * lax.rsqrt(smooth)).astype(
                jnp.bfloat16
            )
        return carry

    lax.fori_loop(0, x_ref.shape[0] // ROWS, step, 0)


def whiten(x, low, high, half_wide, bin_dev):
    return pl.pallas_call(
        functools.partial(whiten_kernel, bin_dev, x.shape[1] // bin_dev),
        out_shape=jax.ShapeDtypeStruct(x.shape, jnp.bfloat16),
        compiler_params=pltpu.CompilerParams(vmem_limit_bytes=16 << 20),
        name="whiten",
    )(x, low, high, half_wide)


NT = (((1,), (1,)), ((), ()))


def correlate(turned_ref, blocks, out_ref):
    def step(d, carry):
        for j, (mine_ref, other_ref) in enumerate(blocks):
            span = mine_ref.shape[1]
            total = lax.dot_general(
                turned_ref[d, :, :span], mine_ref[...], NT, preferred_element_type=jnp.float32
            )
            total += lax.dot_general(
                turned_ref[d, :, span:], other_ref[...], NT, preferred_element_type=jnp.float32
            )
            out_ref[d, j] = total.astype(jnp.bfloat16)
        return carry

    lax.fori_loop(0, turned_ref.shape[0], step, 0)


def first_kernel(width, mine_ref, other_ref, table_ref, turned_ref, out_ref):
    rows_all, span = mine_ref.shape
    chips = turned_ref.shape[0]
    for part, ref in enumerate((mine_ref, other_ref)):

        def turn(g, carry, part=part, ref=ref):
            lanes = pl.ds(pl.multiple_of(g * width, width), width)
            to = pl.ds(pl.multiple_of(part * span + g * width, width), width)
            wide = [jnp.broadcast_to(table_ref[k : k + 1, to], (ROWS, width)) for k in range(2 * chips)]

            def step(i, inner):
                rows = pl.ds(pl.multiple_of(i * ROWS, ROWS), ROWS)
                value = ref[rows, lanes].astype(jnp.float32)
                swapped = pltpu.roll(value, width // 2, 1)
                for d in range(chips):
                    turned_ref[d, rows, to] = (value * wide[d] + swapped * wide[chips + d]).astype(
                        jnp.bfloat16
                    )
                return inner

            return lax.fori_loop(0, rows_all // ROWS, step, carry, unroll=8)

        lax.fori_loop(0, span // width, turn, 0)
    correlate(turned_ref, [(mine_ref, other_ref)], out_ref)


def first_pair(mine, other, table, width):
    rows, span = mine.shape
    chips = table.shape[0] // 2
    return pl.pallas_call(
        functools.partial(first_kernel, width),
        out_shape=[
            jax.ShapeDtypeStruct((chips, rows, 2 * span), jnp.bfloat16),
            jax.ShapeDtypeStruct((chips, 1, rows, rows), jnp.bfloat16),
        ],
        compiler_params=pltpu.CompilerParams(vmem_limit_bytes=20 << 20),
        name="first_pair",
    )(mine, other, table)


def pairs_kernel(turned_ref, *refs):
    correlate(turned_ref, list(zip(refs[:-1:2], refs[1:-1:2])), refs[-1])


def next_pairs(turned, *halves):
    rows = halves[0].shape[0]
    return pl.pallas_call(
        pairs_kernel,
        out_shape=jax.ShapeDtypeStruct(
            (turned.shape[0], len(halves) // 2, rows, rows), jnp.bfloat16
        ),
        compiler_params=pltpu.CompilerParams(vmem_limit_bytes=20 << 20),
        cost_estimate=pl.CostEstimate(
            flops=2 * len(halves) * turned.size * rows, bytes_accessed=2 * turned.size, transcendentals=0
        ),
        name="next_pairs",
    )(turned, *halves)


def swap_cores(block, size):
    return lax.ppermute(block, "freq", [(i, i ^ 1) for i in range(size)])


def scatter(partial, size):
    kept = partial.shape[0] // 2
    beside = [(i, i ^ CORES) for i in range(size)]
    across = [(i, i ^ (2 * CORES)) for i in range(size)]
    arrived = lax.ppermute(partial[kept:], "freq", beside).astype(jnp.float32)
    passing = (partial[1].astype(jnp.float32) + arrived[1]).astype(jnp.bfloat16)
    passed = lax.ppermute(passing, "freq", across).astype(jnp.float32)
    return (partial[0].astype(jnp.float32) + arrived[0] + passed).astype(jnp.bfloat16)


def exchange(block, mask, count):
    if mask == 0:
        return block
    return lax.ppermute(block, "chan", [(i, i ^ mask) for i in range(count)])


def far_side(left, right, count):
    half = left.shape[0] // 2
    return exchange(left[:half], 3, count), exchange(right[half:], 1, count)


def pick_kernel(mask_ref, own, left, right, low_part, high_part, *refs):
    outs, sems = refs[:-1], refs[-1]
    half = own.shape[0] // 2
    for r, out in enumerate(outs):
        near = mask_ref[r, 0] & (NEAR - 1)
        lower, upper = out.at[pl.ds(0, half)], out.at[pl.ds(half, half)]
        for value, block in ((0, own), (1, left), (3, right)):

            @pl.when(near == value)
            def _(block=block, lower=lower, upper=upper, r=r):
                pltpu.make_async_copy(block.at[pl.ds(0, half)], lower, sems.at[r, 0]).start()
                pltpu.make_async_copy(block.at[pl.ds(half, half)], upper, sems.at[r, 1]).start()

        @pl.when(near == 2)
        def _(lower=lower, upper=upper, r=r):
            pltpu.make_async_copy(low_part, lower, sems.at[r, 0]).start()
            pltpu.make_async_copy(high_part, upper, sems.at[r, 1]).start()

    for r, out in enumerate(outs):
        pltpu.make_async_copy(low_part, out.at[pl.ds(0, half)], sems.at[r, 0]).wait()
        pltpu.make_async_copy(high_part, out.at[pl.ds(half, half)], sems.at[r, 1]).wait()


def pick(partners, own, *pieces):
    return pl.pallas_call(
        pick_kernel,
        in_specs=[pl.BlockSpec(memory_space=pltpu.SMEM)]
        + [pl.BlockSpec(memory_space=pl.ANY)] * (1 + len(pieces)),
        out_specs=[pl.BlockSpec(memory_space=pl.ANY)] * ROUNDS,
        out_shape=[jax.ShapeDtypeStruct(own.shape, own.dtype)] * ROUNDS,
        scratch_shapes=[pltpu.SemaphoreType.DMA((ROUNDS, 2))],
        compiler_params=pltpu.CompilerParams(vmem_limit_bytes=1 << 20),
        name="pick",
    )(partners, own, *pieces)


def shards(spectra, half_width, partners):
    freq_count = lax.axis_size("freq")
    chan_count = lax.axis_size("chan")
    channels, bin_dev, width = spectra.shape
    far_count = chan_count // NEAR
    x = spectra.reshape(channels, bin_dev * width)
    edge = HMAX * width
    up = [(i, i + 1) for i in range(freq_count - 1)]
    down = [(i + 1, i) for i in range(freq_count - 1)]
    low = lax.ppermute(x[:, -edge:], "freq", up)
    high = lax.ppermute(x[:, :edge], "freq", down)
    half_wide = jnp.broadcast_to(half_width.astype(jnp.float32)[:, None], (channels, width))
    table = lax.dynamic_index_in_dim(
        jnp.asarray(tables(freq_count, bin_dev, width // 2)),
        lax.axis_index("freq"),
        0,
        keepdims=False,
    )
    white = whiten(x, low, high, half_wide, bin_dev)
    left, right = exchange(white, 1, chan_count), exchange(white, 3, chan_count)
    other = swap_cores(white, freq_count)
    turned, partial = first_pair(white, other, table, width)
    left, right, partial = lax.optimization_barrier((left, right, partial))
    picked = pick(partners, white, left, right, *far_side(left, right, chan_count))
    far = partners[:, 0] >> (NEAR.bit_length() - 1)
    *picked, partial = lax.optimization_barrier((*picked, partial))

    def first_stage(mask):
        def run(block, partial):
            return exchange(block, mask * NEAR, chan_count), scatter(partial, freq_count)

        return run

    def second_stage(mask):
        def run(block, held):
            return exchange(block, mask * NEAR, chan_count), swap_cores(held, freq_count)

        return run

    def last_stage(mask):
        def run(block, held, partial):
            arriving = exchange(block, mask * NEAR, chan_count)
            return arriving, swap_cores(held, freq_count), scatter(partial, freq_count)

        return run

    def stage(make, r, *operands):
        return lax.switch(far[r], [make(k) for k in range(far_count)], *operands)

    block_0, sum_own = stage(first_stage, 0, picked[0], partial)
    block_1, other_0 = stage(second_stage, 1, picked[1], block_0)
    partial = next_pairs(turned, block_0, other_0)
    block_2, other_1, sum_0 = stage(last_stage, 2, picked[2], block_1, partial)
    sum_1 = scatter(next_pairs(turned, block_1, other_1), freq_count)
    partial = next_pairs(turned, block_2, swap_cores(block_2, freq_count))
    return jnp.concatenate([sum_own, sum_0, sum_1, scatter(partial, freq_count)])[None]


def solution(mesh):
    return jax.shard_map(
        shards,
        mesh=mesh,
        in_specs=(P("chan", "freq", None), P("chan"), P()),
        out_specs=P("freq", None, "chan", None),
        check_vma=False,
    )
```

time: 354 us -> 191 us (0.54); the launches traced: 349 us -> 190 us
  waiting for transfers between devices: 230 us -> 80.7 us
  matrix products: 27.1 us -> 0 us
  starting transfers between devices: 62.5 us -> 79.8 us
  Pallas kernels: 0 us -> 16.9 us
  between operations: 15.5 us -> 2.13 us
  other arithmetic: 7.88 us -> 2.03 us
    reduce_scatter x4 -> x0, waiting for transfers between devices: 80.5 us -> none  [shards(): lax.psum_scatter(pair_terms(jnp.int32(0), LAG_DEV * lax.axis_size('freq')...]
    ppermute x18 -> x21, waiting for transfers between devices: 149 us -> 80.7 us  [the longest x4 40.6 us: scatter(): passed = lax.ppermute(passing, 'freq', across).astype(jnp.float32)]
    dot_general x16 -> x0, matrix products: 27.1 us -> none  [the longest x4 12 us: lag_terms(): jnp.einsum('gab,gl->lab', real_part, cosine, precision=lax.Precision.HIGH...]
    ppermute x18 -> x21, starting transfers between devices: 62.4 us -> 79.8 us  [the longest x7 33.8 us: exchange(): return lax.ppermute(block, 'chan', [(i, i ^ mask) for i in range(count)])]
    pallas_call x0 -> x6, Pallas kernels: none -> 16.9 us  [the longest x3 7.88 us: next_pairs(): pl.pallas_call(pairs_kernel, out_shape=jax.ShapeDtypeStruct((turned.shape...]
    unnamed x7 -> x11, local copies, waits for them, and re-layouts: 1.14 us -> 6.35 us
    convert_element_type x4 -> x0, local copies, waits for them, and re-layouts: 4.75 us -> none  [shards(): pair_terms(jnp.int32(0), LAG_DEV * lax.axis_size('freq'))]
  transfers between devices with their start and end apart: 22 -> 21, of which waited for: 15 -> 13; matrix products, arithmetic and copies ran while one was open for 10% -> 1% of each run, Pallas kernels for 0% -> 5%
where the time goes in v1:
time: 191 us; the launch traced here: 190 us
  waiting for transfers between devices  80.7 us (42%)
  starting transfers between devices  79.8 us (42%)
  Pallas kernels  16.9 us (9%)
  local copies, waits for them, and re-layouts  8.01 us (4%)
  between operations  2.13 us (1%)
  other arithmetic  2.03 us (1%)
    ppermute x4, waiting for transfers between devices, scatter(): passed = lax.ppermute(passing, 'freq', across).astype(jnp.float32)  40.6 us
    ppermute x7, starting transfers between devices, exchange(): return lax.ppermute(block, 'chan', [(i, i ^ mask) for i in range(count)])  33.8 us
    ppermute x7, waiting for transfers between devices, exchange(): return lax.ppermute(block, 'chan', [(i, i ^ mask) for i in range(count)])  31.6 us
    ppermute x4, starting transfers between devices, scatter(): passed = lax.ppermute(passing, 'freq', across).astype(jnp.float32)  12.6 us
    ppermute x4, starting transfers between devices, swap_cores(): return lax.ppermute(block, 'freq', [(i, i ^ 1) for i in range(size)])  12.1 us
    ppermute x4, starting transfers between devices, scatter(): arrived = lax.ppermute(partial[kept:], 'freq', beside).astype(jnp.float32)  11.2 us
    pallas_call x3, Pallas kernels, next_pairs(): pl.pallas_call(pairs_kernel, out_shape=jax.ShapeDtypeStruct((turned.shape...  7.88 us
    unnamed x11, local copies, waits for them, and re-layouts  6.35 us
  transfers between devices with their start and end apart: 21, of which 13 were waited for; matrix products, arithmetic and copies ran while one was open for 1% of the time, Pallas kernels for 5%

profile of v1, /device:TPU:1, one launch (start us, length us, event | category | flops | bytes accessed | tf_op | source)
XLA Modules:
  0.0 190.0 jit_solution(13084436340392981946)
XLA Ops:
  1.2 5.4 %collective-permute-start.141 = (bf16[256,512]{1,0:T(8,128)(2,1)S(1)}, bf16[256,512]{1,0:T(8,128)(2,1)S(1)}, u32[]{:S(2)}, u32[]{:S(2)}) collective-permute-start(bf16[256,512]{1,0:T(8,128)(2,1)S(1)} %get-tuple-element.407), channel_id=1, source_target_pairs={{0,1},{1,2},{2,3},{3,4},{4,5},{5,6},{6,7},{8,9},{9,10},{10,11},{11... | collective-permute-start | bytes 786440 | tf_op jit(solution)/shard_map/ppermute | solution.py:228
  6.6 4.7 %collective-permute-start.142 = (bf16[256,512]{1,0:T(8,128)(2,1)S(1)}, bf16[256,512]{1,0:T(8,128)(2,1)S(1)}, u32[]{:S(2)}, u32[]{:S(2)}) collective-permute-start(bf16[256,512]{1,0:T(8,128)(2,1)S(1)} %get-tuple-element.406), channel_id=1, source_target_pairs={{1,0},{2,1},{3,2},{4,3},{5,4},{6,5},{7,6},{9,8},{10,9},{11,10},{12... | collective-permute-start | bytes 786440 | tf_op jit(solution)/shard_map/ppermute | solution.py:229
  12.0 2.3 %collective-permute-done.142.high_ref = bf16[256,512]{1,0:T(8,128)(2,1)S(1)} collective-permute-done((bf16[256,512]{1,0:T(8,128)(2,1)S(1)}, bf16[256,512]{1,0:T(8,128)(2,1)S(1)}, u32[]{:S(2)}, u32[]{:S(2)}) %collective-permute-start.142) | collective-permute-done | bytes 262176 | tf_op jit(solution)/shard_map/ppermute | solution.py:229
  18.3 3.1 %collective-permute-start.143 = (bf16[256,1024]{1,0:T(8,128)(2,1)S(1)}, bf16[256,1024]{1,0:T(8,128)(2,1)S(1)}, u32[]{:S(2)}, u32[]{:S(2)}) collective-permute-start(bf16[256,1024]{1,0:T(8,128)(2,1)S(1)} %whiten.1.mine_ref.own), channel_id=1, source_target_pairs={{0,8},{8,0},{16,24},{24,16},{32,40},{40,32},{48,56},{56,48},{64,72... | collective-permute-start | bytes 1572872 | tf_op jit(solution)/shard_map/ppermute | solution.py:175
  21.4 3.7 %collective-permute-start.144 = (bf16[256,1024]{1,0:T(8,128)(2,1)S(1)}, bf16[256,1024]{1,0:T(8,128)(2,1)S(1)}, u32[]{:S(2)}, u32[]{:S(2)}) collective-permute-start(bf16[256,1024]{1,0:T(8,128)(2,1)S(1)} %whiten.1.mine_ref.own), channel_id=1, source_target_pairs={{0,24},{8,16},{16,8},{24,0},{32,56},{40,48},{48,40},{56,32},{64,88... | collective-permute-start | bytes 1572872 | tf_op jit(solution)/shard_map/ppermute | solution.py:175
  26.0 5.6 %first_pair.1 = (bf16[4,256,2048]{2,1,0:T(8,128)(2,1)S(1)}, bf16[4,1,256,256]{3,2,1,0:T(8,128)(2,1)S(1)}) custom-call(bf16[256,1024]{1,0:T(8,128)(2,1)S(1)} %whiten.1.mine_ref.own, bf16[256,1024]{1,0:T(8,128)(2,1)S(1)} %collective-permute-done.145.other_ref, f32[8,2048]{1,0:T(8,128)S(1)} %dynamic-slice_bitcast_fusion.table_ref), custom_call_target="tpu_custom_call" | custom-call | tf_op jit(solution)/shard_map/first_pair/pallas_call | solution.py:128
  33.2 4.0 %collective-permute-done.144.right = bf16[256,1024]{1,0:T(8,128)(2,1)S(1)} collective-permute-done((bf16[256,1024]{1,0:T(8,128)(2,1)S(1)}, bf16[256,1024]{1,0:T(8,128)(2,1)S(1)}, u32[]{:S(2)}, u32[]{:S(2)}) %collective-permute-start.144) | collective-permute-done | bytes 524320 | tf_op jit(solution)/shard_map/ppermute | solution.py:175
  37.2 3.7 %collective-permute-start.146 = (bf16[128,1024]{1,0:T(8,128)(2,1)S(1)}, bf16[128,1024]{1,0:T(8,128)(2,1)S(1)}, u32[]{:S(2)}, u32[]{:S(2)}) collective-permute-start(bf16[128,1024]{1,0:T(8,128)(2,1)S(1)} %slice.541), channel_id=1, source_target_pairs={{0,24},{8,16},{16,8},{24,0},{32,56},{40,48},{48,40},{56,32},{64,88... | collective-permute-start | bytes 786440 | tf_op jit(solution)/shard_map/ppermute | solution.py:175
  46.5 2.3 %collective-permute-done.147.high_part = bf16[128,1024]{1,0:T(8,128)(2,1)S(1)} collective-permute-done((bf16[128,1024]{1,0:T(8,128)(2,1)S(1)}, bf16[128,1024]{1,0:T(8,128)(2,1)S(1)}, u32[]{:S(2)}, u32[]{:S(2)}) %collective-permute-start.147) | collective-permute-done | bytes 262176 | tf_op jit(solution)/shard_map/ppermute | solution.py:175
  50.2 33.8 %conditional.10 = (bf16[256,1024]{1,0:T(8,128)(2,1)}, bf16[1,256,256]{2,1,0:T(8,128)(2,1)S(1)}) conditional(s32[]{:T(128)} %bitcast.64, (bf16[4,1,256,256]{3,2,1,0:T(8,128)(2,1)S(1)}, bf16[256,1024]{1,0:T(8,128)(2,1)}) %tuple.333, (bf16[256,1024]{1,0:T(8,128)(2,1)}, ...), branch_computations={%region_0.1_spmd, %region_1.2_spmd, %region_2.3_spmd, %region_3.4_... | conditional | flops 655360 | bytes 7209096
  50.3 4.0 %collective-permute-start.49 = (bf16[2,1,256,256]{3,2,1,0:T(8,128)(2,1)S(1)}, bf16[2,1,256,256]{3,2,1,0:T(8,128)(2,1)S(1)}, u32[]{:S(2)}, u32[]{:S(2)}) collective-permute-start(bf16[2,1,256,256]{3,2,1,0:T(8,128)(2,1)S(1)} %slice.390), channel_id=1, source_target_pairs={{0,2},{1,3},{2,0},{3,1},{4,6},{5,7},{6,4},{7,5},{8,10},{9,11},{10,... | collective-permute-start | bytes 786440 | tf_op jit(solution)/shard_map/cond/branch_6_fun/ppermute | solution.py:166
  54.3 5.9 %collective-permute-start.48 = (bf16[256,1024]{1,0:T(8,128)(2,1)}, bf16[256,1024]{1,0:T(8,128)(2,1)S(1)}, u32[]{:S(2)}, u32[]{:S(2)}) collective-permute-start(bf16[256,1024]{1,0:T(8,128)(2,1)} %get-tuple-element.259), channel_id=1, source_target_pairs={{0,192},{8,200},{16,208},{24,216},{32,224},{40,232},{48,240},{56,2... | collective-permute-start | bytes 1572872 | tf_op jit(solution)/shard_map/cond/branch_6_fun/ppermute | solution.py:175
  60.2 4.8 %collective-permute-start.50 = (bf16[1,256,256]{2,1,0:T(8,128)(2,1)S(1)}, bf16[1,256,256]{2,1,0:T(8,128)(2,1)S(1)}, u32[]{:S(2)}, u32[]{:S(2)}) collective-permute-start(bf16[1,256,256]{2,1,0:T(8,128)(2,1)S(1)} %fusion.34), channel_id=1, source_target_pairs={{0,4},{1,5},{2,6},{3,7},{4,0},{5,1},{6,2},{7,3},{8,12},{9,13},{10,... | collective-permute-start | bytes 393224 | tf_op jit(solution)/shard_map/cond/branch_6_fun/ppermute | solution.py:168
  65.0 4.0 %collective-permute-done.50 = bf16[1,256,256]{2,1,0:T(8,128)(2,1)S(1)} collective-permute-done((bf16[1,256,256]{2,1,0:T(8,128)(2,1)S(1)}, bf16[1,256,256]{2,1,0:T(8,128)(2,1)S(1)}, u32[]{:S(2)}, u32[]{:S(2)}) %collective-permute-start.50) | collective-permute-done | bytes 131104 | tf_op jit(solution)/shard_map/cond/branch_6_fun/ppermute | solution.py:168
  69.1 14.1 %collective-permute-done.48 = bf16[256,1024]{1,0:T(8,128)(2,1)S(1)} collective-permute-done((bf16[256,1024]{1,0:T(8,128)(2,1)}, bf16[256,1024]{1,0:T(8,128)(2,1)S(1)}, u32[]{:S(2)}, u32[]{:S(2)}) %collective-permute-start.48) | collective-permute-done | bytes 524320 | tf_op jit(solution)/shard_map/cond/branch_6_fun/ppermute | solution.py:175
  84.0 15.0 %conditional.8 = (bf16[256,1024]{1,0:T(8,128)(2,1)S(1)}, bf16[256,1024]{1,0:T(8,128)(2,1)}) conditional(s32[]{:T(128)} %bitcast.67, (bf16[256,1024]{1,0:T(8,128)(2,1)}, bf16[256,1024]{1,0:T(8,128)(2,1)S(1)}) %tuple.335, (bf16[256,1024]{1,0:T(8,128)(2,1)S(1)}, bf16[256,1024]{1,0:T(8,128)(2,1)}) %tuple.336, ...), branch_computations={%region_16.17_spmd, %region_17.18_spmd, %region_18.19_spmd, %regio... | conditional | bytes 5242976 | solution.py:266
  84.0 3.2 %collective-permute-start.1 = (bf16[256,1024]{1,0:T(8,128)(2,1)S(1)}, bf16[256,1024]{1,0:T(8,128)(2,1)S(1)}, u32[]{:S(2)}, u32[]{:S(2)}) collective-permute-start(bf16[256,1024]{1,0:T(8,128)(2,1)S(1)} %get-tuple-element.281), channel_id=1, source_target_pairs={{0,32},{8,40},{16,48},{24,56},{32,0},{40,8},{48,16},{56,24},{64,96... | collective-permute-start | bytes 1572872 | tf_op jit(solution)/shard_map/cond/branch_1_fun/ppermute | solution.py:175
  87.2 3.1 %collective-permute-start.2 = (bf16[256,1024]{1,0:T(8,128)(2,1)}, bf16[256,1024]{1,0:T(8,128)(2,1)}, u32[]{:S(2)}, u32[]{:S(2)}) collective-permute-start(bf16[256,1024]{1,0:T(8,128)(2,1)} %get-tuple-element.282), channel_id=1, source_target_pairs={{0,1},{1,0},{2,3},{3,2},{4,5},{5,4},{6,7},{7,6},{8,9},{9,8},{10,11... | collective-permute-start | bytes 1572872 | tf_op jit(solution)/shard_map/cond/branch_1_fun/ppermute | solution.py:159
  90.2 8.5 %collective-permute-done.1 = bf16[256,1024]{1,0:T(8,128)(2,1)S(1)} collective-permute-done((bf16[256,1024]{1,0:T(8,128)(2,1)S(1)}, bf16[256,1024]{1,0:T(8,128)(2,1)S(1)}, u32[]{:S(2)}, u32[]{:S(2)}) %collective-permute-start.1) | collective-permute-done | bytes 524320 | tf_op jit(solution)/shard_map/cond/branch_1_fun/ppermute | solution.py:175
  101.2 3.1 %next_pairs.3 = bf16[4,1,256,256]{3,2,1,0:T(8,128)(2,1)S(1)} custom-call(bf16[4,256,2048]{2,1,0:T(8,128)(2,1)S(1)} %copy-done.2, bf16[256,1024]{1,0:T(8,128)(2,1)} %get-tuple-element.388.refs_0_, bf16[256,1024]{1,0:T(8,128)(2,1)} %get-tuple-element.392.refs_1_), custom_call_target="tpu_custom_call" | custom-call | flops 2147483648 | bytes 4194304 | tf_op jit(solution)/shard_map/next_pairs/pallas_call | solution.py:145
  104.3 50.9 %conditional.11 = (bf16[256,1024]{1,0:T(8,128)(2,1)S(1)}, bf16[256,1024]{1,0:T(8,128)(2,1)}, bf16[1,256,256]{2,1,0:T(8,128)(2,1)S(1)}) conditional(s32[]{:T(128)} %bitcast.66, (bf16[256,1024]{1,0:T(8,128)(2,1)S(1)}, bf16[4,1,256,256]{3,2,1,0:T(8,128)(2,1)S(1)}, bf16[256,1024]{1,0:T(8,128)(2,1)S(1)}) %tuple.337, ...), branch_computations={%region_32.33_spmd, %region_33.34_spmd, %region_34.35_spmd, %regio... | conditional | flops 655360 | bytes 9306296
  106.3 12.3 %collective-permute-start.129 = (bf16[256,1024]{1,0:T(8,128)(2,1)S(1)}, bf16[256,1024]{1,0:T(8,128)(2,1)S(1)}, u32[]{:S(2)}, u32[]{:S(2)}) collective-permute-start(bf16[256,1024]{1,0:T(8,128)(2,1)S(1)} %get-tuple-element.350), channel_id=1, source_target_pairs={{0,416},{8,424},{16,432},{24,440},{32,384},{40,392},{48,400},{56,4... | collective-permute-start | bytes 1572872 | tf_op jit(solution)/shard_map/cond/branch_13_fun/ppermute | solution.py:175
  118.6 4.7 %collective-permute-start.130 = (bf16[256,1024]{1,0:T(8,128)(2,1)S(1)}, bf16[256,1024]{1,0:T(8,128)(2,1)}, u32[]{:S(2)}, u32[]{:S(2)}) collective-permute-start(bf16[256,1024]{1,0:T(8,128)(2,1)S(1)} %get-tuple-element.351), channel_id=1, source_target_pairs={{0,1},{1,0},{2,3},{3,2},{4,5},{5,4},{6,7},{7,6},{8,9},{9,8},{10,11... | collective-permute-start | bytes 1572872 | tf_op jit(solution)/shard_map/cond/branch_13_fun/ppermute | solution.py:159
  123.4 4.0 %collective-permute-start.132 = (bf16[1,256,256]{2,1,0:T(8,128)(2,1)S(1)}, bf16[1,256,256]{2,1,0:T(8,128)(2,1)S(1)}, u32[]{:S(2)}, u32[]{:S(2)}) collective-permute-start(bf16[1,256,256]{2,1,0:T(8,128)(2,1)S(1)} %fusion.149), channel_id=1, source_target_pairs={{0,4},{1,5},{2,6},{3,7},{4,0},{5,1},{6,2},{7,3},{8,12},{9,13},{10,... | collective-permute-start | bytes 393224 | tf_op jit(solution)/shard_map/cond/branch_13_fun/ppermute | solution.py:168
  127.4 27.6 %collective-permute-done.132 = bf16[1,256,256]{2,1,0:T(8,128)(2,1)S(1)} collective-permute-done((bf16[1,256,256]{2,1,0:T(8,128)(2,1)S(1)}, bf16[1,256,256]{2,1,0:T(8,128)(2,1)S(1)}, u32[]{:S(2)}, u32[]{:S(2)}) %collective-permute-start.132) | collective-permute-done | bytes 131104 | tf_op jit(solution)/shard_map/cond/branch_13_fun/ppermute | solution.py:168
  155.2 2.3 %collective-permute-start.150 = (bf16[256,1024]{1,0:T(8,128)(2,1)S(1)}, bf16[256,1024]{1,0:T(8,128)(2,1)S(1)}, u32[]{:S(2)}, u32[]{:S(2)}) collective-permute-start(bf16[256,1024]{1,0:T(8,128)(2,1)S(1)} %get-tuple-element.396.refs_0_), channel_id=1, source_target_pairs={{0,1},{1,0},{2,3},{3,2},{4,5},{5,4},{6,7},{7,6},{8,9},{9,8},{10,11... | collective-permute-start | bytes 1572872 | tf_op jit(solution)/shard_map/ppermute | solution.py:159
  159.7 2.9 %next_pairs.4 = bf16[4,1,256,256]{3,2,1,0:T(8,128)(2,1)S(1)} custom-call(bf16[4,256,2048]{2,1,0:T(8,128)(2,1)S(1)} %copy-done.3, bf16[256,1024]{1,0:T(8,128)(2,1)S(1)} %get-tuple-element.390.refs_0_, bf16[256,1024]{1,0:T(8,128)(2,1)} %get-tuple-element.395.refs_1_), custom_call_target="tpu_custom_call" | custom-call | flops 2147483648 | bytes 4194304 | tf_op jit(solution)/shard_map/next_pairs/pallas_call | solution.py:145
  166.5 3.4 %collective-permute-start.151 = (bf16[2,1,256,256]{3,2,1,0:T(8,128)(2,1)S(1)}, bf16[2,1,256,256]{3,2,1,0:T(8,128)(2,1)S(1)}, u32[]{:S(2)}, u32[]{:S(2)}) collective-permute-start(bf16[2,1,256,256]{3,2,1,0:T(8,128)(2,1)S(1)} %slice.627), channel_id=1, source_target_pairs={{0,2},{1,3},{2,0},{3,1},{4,6},{5,7},{6,4},{7,5},{8,10},{9,11},{10,... | collective-permute-start | bytes 786440 | tf_op jit(solution)/shard_map/ppermute | solution.py:166
  169.9 2.5 %collective-permute-done.148 = bf16[2,1,256,256]{3,2,1,0:T(8,128)(2,1)S(1)} collective-permute-done((bf16[2,1,256,256]{3,2,1,0:T(8,128)(2,1)S(1)}, bf16[2,1,256,256]{3,2,1,0:T(8,128)(2,1)S(1)}, u32[]{:S(2)}, u32[]{:S(2)}) %collective-permute-start.148) | collective-permute-done | bytes 262176 | tf_op jit(solution)/shard_map/ppermute | solution.py:166
  174.4 3.6 %collective-permute-done.151 = bf16[2,1,256,256]{3,2,1,0:T(8,128)(2,1)S(1)} collective-permute-done((bf16[2,1,256,256]{3,2,1,0:T(8,128)(2,1)S(1)}, bf16[2,1,256,256]{3,2,1,0:T(8,128)(2,1)S(1)}, u32[]{:S(2)}, u32[]{:S(2)}) %collective-permute-start.151) | collective-permute-done | bytes 262176 | tf_op jit(solution)/shard_map/ppermute | solution.py:166
  180.1 4.8 %collective-permute-done.149 = bf16[1,256,256]{2,1,0:T(8,128)(2,1)S(1)} collective-permute-done((bf16[1,256,256]{2,1,0:T(8,128)(2,1)S(1)}, bf16[1,256,256]{2,1,0:T(8,128)(2,1)S(1)}, u32[]{:S(2)}, u32[]{:S(2)}) %collective-permute-start.149) | collective-permute-done | bytes 131104 | tf_op jit(solution)/shard_map/ppermute | solution.py:168
  184.9 4.2 %collective-permute-done.152 = bf16[1,256,256]{2,1,0:T(8,128)(2,1)S(1)} collective-permute-done((bf16[1,256,256]{2,1,0:T(8,128)(2,1)S(1)}, bf16[1,256,256]{2,1,0:T(8,128)(2,1)S(1)}, u32[]{:S(2)}, u32[]{:S(2)}) %collective-permute-start.152) | collective-permute-done | bytes 131104 | tf_op jit(solution)/shard_map/ppermute | solution.py:168
  (56 shorter events, 29.6 us)
Async XLA Ops:
  0.0 42.9 %copy-start = (s32[3,64]{1,0:T(4,128)S(1)}, s32[3,64]{1,0:T(4,128)}, u32[]{:S(2)}) copy-start(s32[3,64]{1,0:T(4,128)} %mask_ref.1) | copy-start | bytes 2308
  1.2 10.8 %collective-permute-start.141 = (bf16[256,512]{1,0:T(8,128)(2,1)S(1)}, bf16[256,512]{1,0:T(8,128)(2,1)S(1)}, u32[]{:S(2)}, u32[]{:S(2)}) collective-permute-start(bf16[256,512]{1,0:T(8,128)(2,1)S(1)} %get-tuple-element.407), channel_id=1, source_target_pairs={{0,1},{1,2},{2,3},{3,4},{4,5},{5,6},{6,7},{8,9},{9,10},{10,11},{11... | collective-permute-start | bytes 786440 | tf_op jit(solution)/shard_map/ppermute | solution.py:228
  6.6 7.7 %collective-permute-start.142 = (bf16[256,512]{1,0:T(8,128)(2,1)S(1)}, bf16[256,512]{1,0:T(8,128)(2,1)S(1)}, u32[]{:S(2)}, u32[]{:S(2)}) collective-permute-start(bf16[256,512]{1,0:T(8,128)(2,1)S(1)} %get-tuple-element.406), channel_id=1, source_target_pairs={{1,0},{2,1},{3,2},{4,3},{5,4},{6,5},{7,6},{9,8},{10,9},{11,10},{12... | collective-permute-start | bytes 786440 | tf_op jit(solution)/shard_map/ppermute | solution.py:229
  16.4 9.6 %collective-permute-start.145 = (bf16[256,1024]{1,0:T(8,128)(2,1)S(1)}, bf16[256,1024]{1,0:T(8,128)(2,1)S(1)}, u32[]{:S(2)}, u32[]{:S(2)}) collective-permute-start(bf16[256,1024]{1,0:T(8,128)(2,1)S(1)} %whiten.1.mine_ref.own), channel_id=1, source_target_pairs={{0,1},{1,0},{2,3},{3,2},{4,5},{5,4},{6,7},{7,6},{8,9},{9,8},{10,11... | collective-permute-start | bytes 1572872 | tf_op jit(solution)/shard_map/ppermute | solution.py:159
  18.3 14.9 %collective-permute-start.143 = (bf16[256,1024]{1,0:T(8,128)(2,1)S(1)}, bf16[256,1024]{1,0:T(8,128)(2,1)S(1)}, u32[]{:S(2)}, u32[]{:S(2)}) collective-permute-start(bf16[256,1024]{1,0:T(8,128)(2,1)S(1)} %whiten.1.mine_ref.own), channel_id=1, source_target_pairs={{0,8},{8,0},{16,24},{24,16},{32,40},{40,32},{48,56},{56,48},{64,72... | collective-permute-start | bytes 1572872 | tf_op jit(solution)/shard_map/ppermute | solution.py:175
  21.4 15.8 %collective-permute-start.144 = (bf16[256,1024]{1,0:T(8,128)(2,1)S(1)}, bf16[256,1024]{1,0:T(8,128)(2,1)S(1)}, u32[]{:S(2)}, u32[]{:S(2)}) collective-permute-start(bf16[256,1024]{1,0:T(8,128)(2,1)S(1)} %whiten.1.mine_ref.own), channel_id=1, source_target_pairs={{0,24},{8,16},{16,8},{24,0},{32,56},{40,48},{48,40},{56,32},{64,88... | collective-permute-start | bytes 1572872 | tf_op jit(solution)/shard_map/ppermute | solution.py:175
  31.6 18.6 %copy-start.1 = (bf16[4,256,2048]{2,1,0:T(8,128)(2,1)}, bf16[4,256,2048]{2,1,0:T(8,128)(2,1)S(1)}, u32[]{:S(2)}) copy-start(bf16[4,256,2048]{2,1,0:T(8,128)(2,1)S(1)} %get-tuple-element.391.turned_ref) | copy-start | bytes 12582916
  37.2 9.2 %collective-permute-start.146 = (bf16[128,1024]{1,0:T(8,128)(2,1)S(1)}, bf16[128,1024]{1,0:T(8,128)(2,1)S(1)}, u32[]{:S(2)}, u32[]{:S(2)}) collective-permute-start(bf16[128,1024]{1,0:T(8,128)(2,1)S(1)} %slice.541), channel_id=1, source_target_pairs={{0,24},{8,16},{16,8},{24,0},{32,56},{40,48},{48,40},{56,32},{64,88... | collective-permute-start | bytes 786440 | tf_op jit(solution)/shard_map/ppermute | solution.py:175
  41.0 7.7 %collective-permute-start.147 = (bf16[128,1024]{1,0:T(8,128)(2,1)S(1)}, bf16[128,1024]{1,0:T(8,128)(2,1)S(1)}, u32[]{:S(2)}, u32[]{:S(2)}) collective-permute-start(bf16[128,1024]{1,0:T(8,128)(2,1)S(1)} %slice.542), channel_id=1, source_target_pairs={{0,8},{8,0},{16,24},{24,16},{32,40},{40,32},{48,56},{56,48},{64,72... | collective-permute-start | bytes 786440 | tf_op jit(solution)/shard_map/ppermute | solution.py:175
  50.3 9.9 %collective-permute-start.49 = (bf16[2,1,256,256]{3,2,1,0:T(8,128)(2,1)S(1)}, bf16[2,1,256,256]{3,2,1,0:T(8,128)(2,1)S(1)}, u32[]{:S(2)}, u32[]{:S(2)}) collective-permute-start(bf16[2,1,256,256]{3,2,1,0:T(8,128)(2,1)S(1)} %slice.390), channel_id=1, source_target_pairs={{0,2},{1,3},{2,0},{3,1},{4,6},{5,7},{6,4},{7,5},{8,10},{9,11},{10,... | collective-permute-start | bytes 786440 | tf_op jit(solution)/shard_map/cond/branch_6_fun/ppermute | solution.py:166
  54.3 28.9 %collective-permute-start.48 = (bf16[256,1024]{1,0:T(8,128)(2,1)}, bf16[256,1024]{1,0:T(8,128)(2,1)S(1)}, u32[]{:S(2)}, u32[]{:S(2)}) collective-permute-start(bf16[256,1024]{1,0:T(8,128)(2,1)} %get-tuple-element.259), channel_id=1, source_target_pairs={{0,192},{8,200},{16,208},{24,216},{32,224},{40,232},{48,240},{56,2... | collective-permute-start | bytes 1572872 | tf_op jit(solution)/shard_map/cond/branch_6_fun/ppermute | solution.py:175
  60.2 8.8 %collective-permute-start.50 = (bf16[1,256,256]{2,1,0:T(8,128)(2,1)S(1)}, bf16[1,256,256]{2,1,0:T(8,128)(2,1)S(1)}, u32[]{:S(2)}, u32[]{:S(2)}) collective-permute-start(bf16[1,256,256]{2,1,0:T(8,128)(2,1)S(1)} %fusion.34), channel_id=1, source_target_pairs={{0,4},{1,5},{2,6},{3,7},{4,0},{5,1},{6,2},{7,3},{8,12},{9,13},{10,... | collective-permute-start | bytes 393224 | tf_op jit(solution)/shard_map/cond/branch_6_fun/ppermute | solution.py:168
  84.0 14.8 %collective-permute-start.1 = (bf16[256,1024]{1,0:T(8,128)(2,1)S(1)}, bf16[256,1024]{1,0:T(8,128)(2,1)S(1)}, u32[]{:S(2)}, u32[]{:S(2)}) collective-permute-start(bf16[256,1024]{1,0:T(8,128)(2,1)S(1)} %get-tuple-element.281), channel_id=1, source_target_pairs={{0,32},{8,40},{16,48},{24,56},{32,0},{40,8},{48,16},{56,24},{64,96... | collective-permute-start | bytes 1572872 | tf_op jit(solution)/shard_map/cond/branch_1_fun/ppermute | solution.py:175
  87.2 11.6 %collective-permute-start.2 = (bf16[256,1024]{1,0:T(8,128)(2,1)}, bf16[256,1024]{1,0:T(8,128)(2,1)}, u32[]{:S(2)}, u32[]{:S(2)}) collective-permute-start(bf16[256,1024]{1,0:T(8,128)(2,1)} %get-tuple-element.282), channel_id=1, source_target_pairs={{0,1},{1,0},{2,3},{3,2},{4,5},{5,4},{6,7},{7,6},{8,9},{9,8},{10,11... | collective-permute-start | bytes 1572872 | tf_op jit(solution)/shard_map/cond/branch_1_fun/ppermute | solution.py:159
  99.0 2.2 %copy-start.2 = (bf16[4,256,2048]{2,1,0:T(8,128)(2,1)S(1)}, bf16[4,256,2048]{2,1,0:T(8,128)(2,1)}, u32[]{:S(2)}) copy-start(bf16[4,256,2048]{2,1,0:T(8,128)(2,1)} %copy-done.1) | copy-start | bytes 12582916
  104.4 19.0 %collective-permute-start.131 = (bf16[2,1,256,256]{3,2,1,0:T(8,128)(2,1)S(1)}, bf16[2,1,256,256]{3,2,1,0:T(8,128)(2,1)S(1)}, u32[]{:S(2)}, u32[]{:S(2)}) collective-permute-start(bf16[2,1,256,256]{3,2,1,0:T(8,128)(2,1)S(1)} %slice.505), channel_id=1, source_target_pairs={{0,2},{1,3},{2,0},{3,1},{4,6},{5,7},{6,4},{7,5},{8,10},{9,11},{10,... | collective-permute-start | bytes 786440 | tf_op jit(solution)/shard_map/cond/branch_13_fun/ppermute | solution.py:166
  106.3 48.8 %collective-permute-start.129 = (bf16[256,1024]{1,0:T(8,128)(2,1)S(1)}, bf16[256,1024]{1,0:T(8,128)(2,1)S(1)}, u32[]{:S(2)}, u32[]{:S(2)}) collective-permute-start(bf16[256,1024]{1,0:T(8,128)(2,1)S(1)} %get-tuple-element.350), channel_id=1, source_target_pairs={{0,416},{8,424},{16,432},{24,440},{32,384},{40,392},{48,400},{56,4... | collective-permute-start | bytes 1572872 | tf_op jit(solution)/shard_map/cond/branch_13_fun/ppermute | solution.py:175
  118.6 36.6 %collective-permute-start.130 = (bf16[256,1024]{1,0:T(8,128)(2,1)S(1)}, bf16[256,1024]{1,0:T(8,128)(2,1)}, u32[]{:S(2)}, u32[]{:S(2)}) collective-permute-start(bf16[256,1024]{1,0:T(8,128)(2,1)S(1)} %get-tuple-element.351), channel_id=1, source_target_pairs={{0,1},{1,0},{2,3},{3,2},{4,5},{5,4},{6,7},{7,6},{8,9},{9,8},{10,11... | collective-permute-start | bytes 1572872 | tf_op jit(solution)/shard_map/cond/branch_13_fun/ppermute | solution.py:159
  123.4 31.6 %collective-permute-start.132 = (bf16[1,256,256]{2,1,0:T(8,128)(2,1)S(1)}, bf16[1,256,256]{2,1,0:T(8,128)(2,1)S(1)}, u32[]{:S(2)}, u32[]{:S(2)}) collective-permute-start(bf16[1,256,256]{2,1,0:T(8,128)(2,1)S(1)} %fusion.149), channel_id=1, source_target_pairs={{0,4},{1,5},{2,6},{3,7},{4,0},{5,1},{6,2},{7,3},{8,12},{9,13},{10,... | collective-permute-start | bytes 393224 | tf_op jit(solution)/shard_map/cond/branch_13_fun/ppermute | solution.py:168
  155.2 9.4 %collective-permute-start.150 = (bf16[256,1024]{1,0:T(8,128)(2,1)S(1)}, bf16[256,1024]{1,0:T(8,128)(2,1)S(1)}, u32[]{:S(2)}, u32[]{:S(2)}) collective-permute-start(bf16[256,1024]{1,0:T(8,128)(2,1)S(1)} %get-tuple-element.396.refs_0_), channel_id=1, source_target_pairs={{0,1},{1,0},{2,3},{3,2},{4,5},{5,4},{6,7},{7,6},{8,9},{9,8},{10,11... | collective-permute-start | bytes 1572872 | tf_op jit(solution)/shard_map/ppermute | solution.py:159
  157.5 2.2 %copy-start.3 = (bf16[4,256,2048]{2,1,0:T(8,128)(2,1)S(1)}, bf16[4,256,2048]{2,1,0:T(8,128)(2,1)}, u32[]{:S(2)}) copy-start(bf16[4,256,2048]{2,1,0:T(8,128)(2,1)} %copy-done.1) | copy-start | bytes 12582916
  162.7 9.8 %collective-permute-start.148 = (bf16[2,1,256,256]{3,2,1,0:T(8,128)(2,1)S(1)}, bf16[2,1,256,256]{3,2,1,0:T(8,128)(2,1)S(1)}, u32[]{:S(2)}, u32[]{:S(2)}) collective-permute-start(bf16[2,1,256,256]{3,2,1,0:T(8,128)(2,1)S(1)} %slice.622), channel_id=1, source_target_pairs={{0,2},{1,3},{2,0},{3,1},{4,6},{5,7},{6,4},{7,5},{8,10},{9,11},{10,... | collective-permute-start | bytes 786440 | tf_op jit(solution)/shard_map/ppermute | solution.py:166
  166.5 11.5 %collective-permute-start.151 = (bf16[2,1,256,256]{3,2,1,0:T(8,128)(2,1)S(1)}, bf16[2,1,256,256]{3,2,1,0:T(8,128)(2,1)S(1)}, u32[]{:S(2)}, u32[]{:S(2)}) collective-permute-start(bf16[2,1,256,256]{3,2,1,0:T(8,128)(2,1)S(1)} %slice.627), channel_id=1, source_target_pairs={{0,2},{1,3},{2,0},{3,1},{4,6},{5,7},{6,4},{7,5},{8,10},{9,11},{10,... | collective-permute-start | bytes 786440 | tf_op jit(solution)/shard_map/ppermute | solution.py:166
  172.5 12.3 %collective-permute-start.149 = (bf16[1,256,256]{2,1,0:T(8,128)(2,1)S(1)}, bf16[1,256,256]{2,1,0:T(8,128)(2,1)S(1)}, u32[]{:S(2)}, u32[]{:S(2)}) collective-permute-start(bf16[1,256,256]{2,1,0:T(8,128)(2,1)S(1)} %fusion.168), channel_id=1, source_target_pairs={{0,4},{1,5},{2,6},{3,7},{4,0},{5,1},{6,2},{7,3},{8,12},{9,13},{10,... | collective-permute-start | bytes 393224 | tf_op jit(solution)/shard_map/ppermute | solution.py:168
  178.1 10.9 %collective-permute-start.152 = (bf16[1,256,256]{2,1,0:T(8,128)(2,1)S(1)}, bf16[1,256,256]{2,1,0:T(8,128)(2,1)S(1)}, u32[]{:S(2)}, u32[]{:S(2)}) collective-permute-start(bf16[1,256,256]{2,1,0:T(8,128)(2,1)S(1)} %fusion.169), channel_id=1, source_target_pairs={{0,4},{1,5},{2,6},{3,7},{4,0},{5,1},{6,2},{7,3},{8,12},{9,13},{10,... | collective-permute-start | bytes 393224 | tf_op jit(solution)/shard_map/ppermute | solution.py:168

commit v2 on v1

--- a/solution.py
+++ b/solution.py
@@ -159,14 +159,22 @@
     return lax.ppermute(block, "freq", [(i, i ^ 1) for i in range(size)])
 
 
+def beside_step(partial, size):
+    half = partial.shape[0] // 2
+    route = [(i, i ^ CORES) for i in range(size)]
+    arrived = lax.ppermute(partial[half:], "freq", route).astype(jnp.float32)
+    passing = (partial[1].astype(jnp.float32) + arrived[1]).astype(jnp.bfloat16)
+    return partial[0].astype(jnp.float32) + arrived[0], passing
+
+
+def across_step(kept, passing, size):
+    route = [(i, i ^ (2 * CORES)) for i in range(size)]
+    passed = lax.ppermute(passing, "freq", route).astype(jnp.float32)
+    return (kept + passed).astype(jnp.bfloat16)
+
+
 def scatter(partial, size):
-    kept = partial.shape[0] // 2
-    beside = [(i, i ^ CORES) for i in range(size)]
-    across = [(i, i ^ (2 * CORES)) for i in range(size)]
-    arrived = lax.ppermute(partial[kept:], "freq", beside).astype(jnp.float32)
-    passing = (partial[1].astype(jnp.float32) + arrived[1]).astype(jnp.bfloat16)
-    passed = lax.ppermute(passing, "freq", across).astype(jnp.float32)
-    return (partial[0].astype(jnp.float32) + arrived[0] + passed).astype(jnp.bfloat16)
+    return across_step(*beside_step(partial, size), size)
 
 
 def exchange(block, mask, count):
@@ -175,52 +183,39 @@
     return lax.ppermute(block, "chan", [(i, i ^ mask) for i in range(count)])
 
 
-def far_side(left, right, count):
-    half = left.shape[0] // 2
-    return exchange(left[:half], 3, count), exchange(right[half:], 1, count)
-
-
-def pick_kernel(mask_ref, own, left, right, low_part, high_part, *refs):
+def pick_kernel(top, mask_ref, own, far, *refs):
     outs, sems = refs[:-1], refs[-1]
-    half = own.shape[0] // 2
     for r, out in enumerate(outs):
-        near = mask_ref[r, 0] & (NEAR - 1)
-        lower, upper = out.at[pl.ds(0, half)], out.at[pl.ds(half, half)]
-        for value, block in ((0, own), (1, left), (3, right)):
-
-            @pl.when(near == value)
-            def _(block=block, lower=lower, upper=upper, r=r):
-                pltpu.make_async_copy(block.at[pl.ds(0, half)], lower, sems.at[r, 0]).start()
-                pltpu.make_async_copy(block.at[pl.ds(half, half)], upper, sems.at[r, 1]).start()
-
-        @pl.when(near == 2)
-        def _(lower=lower, upper=upper, r=r):
-            pltpu.make_async_copy(low_part, lower, sems.at[r, 0]).start()
-            pltpu.make_async_copy(high_part, upper, sems.at[r, 1]).start()
+        high = mask_ref[r, 0] & top
+
+        @pl.when(high == 0)
+        def _(out=out, r=r):
+            pltpu.make_async_copy(own, out, sems.at[r]).start()
+
+        @pl.when(high != 0)
+        def _(out=out, r=r):
+            pltpu.make_async_copy(far, out, sems.at[r]).start()
 
     for r, out in enumerate(outs):
-        pltpu.make_async_copy(low_part, out.at[pl.ds(0, half)], sems.at[r, 0]).wait()
-        pltpu.make_async_copy(high_part, out.at[pl.ds(half, half)], sems.at[r, 1]).wait()
-
-
-def pick(partners, own, *pieces):
-    return pl.pallas_call(
-        pick_kernel,
-        in_specs=[pl.BlockSpec(memory_space=pltpu.SMEM)]
-        + [pl.BlockSpec(memory_space=pl.ANY)] * (1 + len(pieces)),
+        pltpu.make_async_copy(own, out, sems.at[r]).wait()
+
+
+def pick(partners, own, far, top):
+    return pl.pallas_call(
+        functools.partial(pick_kernel, top),
+        in_specs=[pl.BlockSpec(memory_space=pltpu.SMEM)] + [pl.BlockSpec(memory_space=pl.ANY)] * 2,
         out_specs=[pl.BlockSpec(memory_space=pl.ANY)] * ROUNDS,
         out_shape=[jax.ShapeDtypeStruct(own.shape, own.dtype)] * ROUNDS,
-        scratch_shapes=[pltpu.SemaphoreType.DMA((ROUNDS, 2))],
+        scratch_shapes=[pltpu.SemaphoreType.DMA((ROUNDS,))],
         compiler_params=pltpu.CompilerParams(vmem_limit_bytes=1 << 20),
         name="pick",
-    )(partners, own, *pieces)
+    )(partners, own, far)
 
 
 def shards(spectra, half_width, partners):
     freq_count = lax.axis_size("freq")
     chan_count = lax.axis_size("chan")
     channels, bin_dev, width = spectra.shape
-    far_count = chan_count // NEAR
     x = spectra.reshape(channels, bin_dev * width)
     edge = HMAX * width
     up = [(i, i + 1) for i in range(freq_count - 1)]
@@ -235,43 +230,48 @@
         keepdims=False,
     )
     white = whiten(x, low, high, half_wide, bin_dev)
-    left, right = exchange(white, 1, chan_count), exchange(white, 3, chan_count)
+    top = chan_count // 2
+    far_white = exchange(white, top, chan_count)
     other = swap_cores(white, freq_count)
     turned, partial = first_pair(white, other, table, width)
-    left, right, partial = lax.optimization_barrier((left, right, partial))
-    picked = pick(partners, white, left, right, *far_side(left, right, chan_count))
-    far = partners[:, 0] >> (NEAR.bit_length() - 1)
-    *picked, partial = lax.optimization_barrier((*picked, partial))
-
-    def first_stage(mask):
-        def run(block, partial):
-            return exchange(block, mask * NEAR, chan_count), scatter(partial, freq_count)
-
-        return run
-
-    def second_stage(mask):
-        def run(block, held):
-            return exchange(block, mask * NEAR, chan_count), swap_cores(held, freq_count)
-
-        return run
-
-    def last_stage(mask):
-        def run(block, held, partial):
-            arriving = exchange(block, mask * NEAR, chan_count)
-            return arriving, swap_cores(held, freq_count), scatter(partial, freq_count)
-
-        return run
-
-    def stage(make, r, *operands):
-        return lax.switch(far[r], [make(k) for k in range(far_count)], *operands)
-
-    block_0, sum_own = stage(first_stage, 0, picked[0], partial)
-    block_1, other_0 = stage(second_stage, 1, picked[1], block_0)
-    partial = next_pairs(turned, block_0, other_0)
-    block_2, other_1, sum_0 = stage(last_stage, 2, picked[2], block_1, partial)
+    far_white, partial = lax.optimization_barrier((far_white, partial))
+    base = pick(partners, white, far_white, top)
+    masks = partners[:, 0]
+    x_of, y_of = masks & (NEAR - 1), (masks & (top - 1)) >> (NEAR.bit_length() - 1)
+    y_count = top // NEAR
+
+    def stage(y_round, y_block, x_round, x_block, beside, *operands):
+        def make(y_mask, x_mask):
+            def run(y_block, x_block, *operands):
+                return (
+                    exchange(y_block, y_mask * NEAR, chan_count),
+                    exchange(x_block, x_mask, chan_count),
+                    beside(*operands),
+                )
+
+            return run
+
+        return lax.switch(
+            y_of[y_round] * NEAR + x_of[x_round],
+            [make(i, j) for i in range(y_count) for j in range(NEAR)],
+            y_block,
+            x_block,
+            *operands,
+        )
+
+    half_0, half_1, _ = stage(0, base[0], 1, base[1], lambda: ())
+    kept, passing = beside_step(partial, freq_count)
+    half_0, half_1, kept, passing = lax.optimization_barrier((half_0, half_1, kept, passing))
+    block_1, half_2, sum_own = stage(
+        1, half_1, 2, base[2], lambda *sums: across_step(*sums, freq_count), kept, passing
+    )
+    block_2, block_0, other_1 = stage(
+        2, half_2, 0, half_0, lambda block: swap_cores(block, freq_count), block_1
+    )
     sum_1 = scatter(next_pairs(turned, block_1, other_1), freq_count)
-    partial = next_pairs(turned, block_2, swap_cores(block_2, freq_count))
-    return jnp.concatenate([sum_own, sum_0, sum_1, scatter(partial, freq_count)])[None]
+    other_0, other_2 = swap_cores(block_0, freq_count), swap_cores(block_2, freq_count)
+    sum_02 = scatter(next_pairs(turned, block_0, other_0, block_2, other_2), freq_count)
+    return jnp.concatenate([sum_own, sum_02[:1], sum_1, sum_02[1:]])[None]
 
 
 def solution(mesh):

time: 191 us -> 201 us (1.052)
  the two profiles are of different devices: /device:TPU:1 before, /device:TPU:15 now
where the time goes in v2:
time: 201 us
  waiting for transfers between devices  88.6 us (44%)
  starting transfers between devices  81.9 us (41%)
  Pallas kernels  14.9 us (7%)
  local copies, waits for them, and re-layouts  8.67 us (4%)
  between operations  3.96 us (2%)
  other arithmetic  2.05 us (1%)
    ppermute x7, waiting for transfers between devices, exchange(): return lax.ppermute(block, 'chan', [(i, i ^ mask) for i in range(count)])  50 us
    ppermute x7, starting transfers between devices, exchange(): return lax.ppermute(block, 'chan', [(i, i ^ mask) for i in range(count)])  36.3 us
    ppermute x3, waiting for transfers between devices, across_step(): passed = lax.ppermute(passing, 'freq', route).astype(jnp.float32)  21.5 us
    ppermute x3, starting transfers between devices, beside_step(): arrived = lax.ppermute(partial[half:], 'freq', route).astype(jnp.float32)  21.3 us
    ppermute x3, waiting for transfers between devices, beside_step(): arrived = lax.ppermute(partial[half:], 'freq', route).astype(jnp.float32)  12.6 us
    ppermute x4, starting transfers between devices, swap_cores(): return lax.ppermute(block, 'freq', [(i, i ^ 1) for i in range(size)])  9.27 us
    ppermute x3, starting transfers between devices, across_step(): passed = lax.ppermute(passing, 'freq', route).astype(jnp.float32)  8.53 us
    unnamed x11, local copies, waits for them, and re-layouts  6.14 us
  transfers between devices with their start and end apart: 19, of which 11 were waited for; matrix products, arithmetic and copies ran while one was open for 2% of the time, Pallas kernels for 5%

profile of v2, /device:TPU:15, one launch (start us, length us, event | category | flops | bytes accessed | tf_op | source)
XLA Modules:
  0.0 200.6 jit_solution(16703115724976628231)
XLA Ops:
  1.2 2.6 %collective-permute-start.221 = (bf16[256,512]{1,0:T(8,128)(2,1)S(1)}, bf16[256,512]{1,0:T(8,128)(2,1)S(1)}, u32[]{:S(2)}, u32[]{:S(2)}) collective-permute-start(bf16[256,512]{1,0:T(8,128)(2,1)S(1)} %get-tuple-element.922), channel_id=1, source_target_pairs={{1,0},{2,1},{3,2},{4,3},{5,4},{6,5},{7,6},{9,8},{10,9},{11,10},{12... | collective-permute-start | bytes 786440 | tf_op jit(solution)/shard_map/ppermute | solution.py:224
  3.8 3.9 %collective-permute-start.220 = (bf16[256,512]{1,0:T(8,128)(2,1)S(1)}, bf16[256,512]{1,0:T(8,128)(2,1)S(1)}, u32[]{:S(2)}, u32[]{:S(2)}) collective-permute-start(bf16[256,512]{1,0:T(8,128)(2,1)S(1)} %get-tuple-element.923), channel_id=1, source_target_pairs={{0,1},{1,2},{2,3},{3,4},{4,5},{5,6},{6,7},{8,9},{9,10},{10,11},{11... | collective-permute-start | bytes 786440 | tf_op jit(solution)/shard_map/ppermute | solution.py:223
  11.1 2.0 %whiten.1.mine_ref.own = bf16[256,1024]{1,0:T(8,128)(2,1)S(1)} custom-call(bf16[256,1024]{1,0:T(8,128)(2,1)S(1)} %bitcast.32, bf16[256,512]{1,0:T(8,128)(2,1)S(1)} %collective-permute-done.220.low_ref, bf16[256,512]{1,0:T(8,128)(2,1)S(1)} %collective-permute-done.221.high_ref, f32[256,128]{1,0:T(8,128)S(1)} %broadcast_in_dim.4.half_ref), custom_call_target="tpu_custom_call" | custom-call | tf_op jit(solution)/shard_map/whiten/pallas_call | solution.py:72
  15.0 9.7 %collective-permute-start.222 = (bf16[256,1024]{1,0:T(8,128)(2,1)S(1)}, bf16[256,1024]{1,0:T(8,128)(2,1)S(1)}, u32[]{:S(2)}, u32[]{:S(2)}) collective-permute-start(bf16[256,1024]{1,0:T(8,128)(2,1)S(1)} %whiten.1.mine_ref.own), channel_id=1, source_target_pairs={{0,256},{8,264},{16,272},{24,280},{32,288},{40,296},{48,304},{56,3... | collective-permute-start | bytes 1572872 | tf_op jit(solution)/shard_map/ppermute | solution.py:183
  25.6 5.6 %first_pair.1 = (bf16[4,256,2048]{2,1,0:T(8,128)(2,1)S(1)}, bf16[4,1,256,256]{3,2,1,0:T(8,128)(2,1)S(1)}) custom-call(bf16[256,1024]{1,0:T(8,128)(2,1)S(1)} %whiten.1.mine_ref.own, bf16[256,1024]{1,0:T(8,128)(2,1)S(1)} %collective-permute-done.223.other_ref, f32[8,2048]{1,0:T(8,128)S(1)} %dynamic-slice_bitcast_fusion.table_ref), custom_call_target="tpu_custom_call" | custom-call | tf_op jit(solution)/shard_map/first_pair/pallas_call | solution.py:128
  31.2 2.0 copy-done.1
  33.2 3.5 %collective-permute-done.222.far = bf16[256,1024]{1,0:T(8,128)(2,1)S(1)} collective-permute-done((bf16[256,1024]{1,0:T(8,128)(2,1)S(1)}, bf16[256,1024]{1,0:T(8,128)(2,1)S(1)}, u32[]{:S(2)}, u32[]{:S(2)}) %collective-permute-start.222) | collective-permute-done | bytes 524320 | tf_op jit(solution)/shard_map/ppermute | solution.py:183
  36.7 16.1 %collective-permute-start.224 = (bf16[2,1,256,256]{3,2,1,0:T(8,128)(2,1)S(1)}, bf16[2,1,256,256]{3,2,1,0:T(8,128)(2,1)S(1)}, u32[]{:S(2)}, u32[]{:S(2)}) collective-permute-start(bf16[2,1,256,256]{3,2,1,0:T(8,128)(2,1)S(1)} %slice.92), channel_id=1, source_target_pairs={{0,2},{1,3},{2,0},{3,1},{4,6},{5,7},{6,4},{7,5},{8,10},{9,11},{10,... | collective-permute-start | bytes 786440 | tf_op jit(solution)/shard_map/ppermute | solution.py:165
  58.5 28.8 %conditional.5 = ((bf16[256,1024]{1,0:T(8,128)(2,1)S(1)}, bf16[256,1024]{1,0:T(8,128)(2,1)})) conditional(s32[]{:T(128)} %bitcast.1, (bf16[256,1024]{1,0:T(8,128)(2,1)S(1)}, bf16[256,1024]{1,0:T(8,128)(2,1)}) %tuple.521, (bf16[256,1024]{1,0:T(8,128)(2,1)}, bf16[256,1024]{1,0:T(8,128)(2,1)S(1)}) %tuple.522, ...), branch_computations={%region_0.1_spmd, %region_1.2_spmd, %region_2.3_spmd, %region_3.4_... | conditional | bytes 6291560 | solution.py:254
  58.6 6.4 %collective-permute-start.36 = (bf16[256,1024]{1,0:T(8,128)(2,1)S(1)}, bf16[256,1024]{1,0:T(8,128)(2,1)S(1)}, u32[]{:S(2)}, u32[]{:S(2)}) collective-permute-start(bf16[256,1024]{1,0:T(8,128)(2,1)S(1)} %get-tuple-element.635), channel_id=1, source_target_pairs={{0,160},{8,168},{16,176},{24,184},{32,128},{40,136},{48,144},{56,1... | collective-permute-start | bytes 1572872 | tf_op jit(solution)/shard_map/cond/branch_23_fun/ppermute | solution.py:183
  65.0 2.1 %collective-permute-start.37 = (bf16[256,1024]{1,0:T(8,128)(2,1)}, bf16[256,1024]{1,0:T(8,128)(2,1)S(1)}, u32[]{:S(2)}, u32[]{:S(2)}) collective-permute-start(bf16[256,1024]{1,0:T(8,128)(2,1)} %get-tuple-element.636), channel_id=1, source_target_pairs={{0,24},{8,16},{16,8},{24,0},{32,56},{40,48},{48,40},{56,32},{64,88... | collective-permute-start | bytes 1572872 | tf_op jit(solution)/shard_map/cond/branch_23_fun/ppermute | solution.py:183
  67.1 19.3 %collective-permute-done.36 = bf16[256,1024]{1,0:T(8,128)(2,1)S(1)} collective-permute-done((bf16[256,1024]{1,0:T(8,128)(2,1)S(1)}, bf16[256,1024]{1,0:T(8,128)(2,1)S(1)}, u32[]{:S(2)}, u32[]{:S(2)}) %collective-permute-start.36) | collective-permute-done | bytes 524320 | tf_op jit(solution)/shard_map/cond/branch_23_fun/ppermute | solution.py:183
  87.4 32.3 %conditional.8 = (bf16[256,1024]{1,0:T(8,128)(2,1)}, bf16[256,1024]{1,0:T(8,128)(2,1)S(1)}, bf16[1,256,256]{2,1,0:T(8,128)(2,1)S(1)}) conditional(s32[]{:T(128)} %bitcast, (bf16[1,256,256]{2,1,0:T(8,128)(2,1)S(1)}, f32[1,256,256]{2,1,0:T(8,128)S(1)}, bf16[256,1024]{1,0:T(8,128)(2,1)}, ...), branch_computations={%region_32.33_spmd, %region_33.34_spmd, %region_34.35_spmd, %regio... | conditional | flops 196608 | bytes 7340176
  87.7 7.1 %collective-permute-start.178 = (bf16[256,1024]{1,0:T(8,128)(2,1)}, bf16[256,1024]{1,0:T(8,128)(2,1)S(1)}, u32[]{:S(2)}, u32[]{:S(2)}) collective-permute-start(bf16[256,1024]{1,0:T(8,128)(2,1)} %get-tuple-element.721), channel_id=1, source_target_pairs={{0,128},{8,136},{16,144},{24,152},{32,160},{40,168},{48,176},{56,1... | collective-permute-start | bytes 1572872 | tf_op jit(solution)/shard_map/cond/branch_17_fun/ppermute | solution.py:183
  94.8 2.5 %collective-permute-start.179 = (bf16[256,1024]{1,0:T(8,128)(2,1)S(1)}, bf16[256,1024]{1,0:T(8,128)(2,1)S(1)}, u32[]{:S(2)}, u32[]{:S(2)}) collective-permute-start(bf16[256,1024]{1,0:T(8,128)(2,1)S(1)} %get-tuple-element.722), channel_id=1, source_target_pairs={{0,8},{8,0},{16,24},{24,16},{32,40},{40,32},{48,56},{56,48},{64,72... | collective-permute-start | bytes 1572872 | tf_op jit(solution)/shard_map/cond/branch_17_fun/ppermute | solution.py:183
  97.2 2.3 %collective-permute-start.180 = (bf16[1,256,256]{2,1,0:T(8,128)(2,1)S(1)}, bf16[1,256,256]{2,1,0:T(8,128)(2,1)S(1)}, u32[]{:S(2)}, u32[]{:S(2)}) collective-permute-start(bf16[1,256,256]{2,1,0:T(8,128)(2,1)S(1)} %get-tuple-element.724), channel_id=1, source_target_pairs={{0,4},{1,5},{2,6},{3,7},{4,0},{5,1},{6,2},{7,3},{8,12},{9,13},{10,... | collective-permute-start | bytes 393224 | tf_op jit(solution)/shard_map/cond/branch_17_fun/ppermute | solution.py:172
  99.6 6.0 %collective-permute-done.180 = bf16[1,256,256]{2,1,0:T(8,128)(2,1)S(1)} collective-permute-done((bf16[1,256,256]{2,1,0:T(8,128)(2,1)S(1)}, bf16[1,256,256]{2,1,0:T(8,128)(2,1)S(1)}, u32[]{:S(2)}, u32[]{:S(2)}) %collective-permute-start.180) | collective-permute-done | bytes 131104 | tf_op jit(solution)/shard_map/cond/branch_17_fun/ppermute | solution.py:172
  105.6 13.3 %collective-permute-done.178 = bf16[256,1024]{1,0:T(8,128)(2,1)S(1)} collective-permute-done((bf16[256,1024]{1,0:T(8,128)(2,1)}, bf16[256,1024]{1,0:T(8,128)(2,1)S(1)}, u32[]{:S(2)}, u32[]{:S(2)}) %collective-permute-start.178) | collective-permute-done | bytes 524320 | tf_op jit(solution)/shard_map/cond/branch_17_fun/ppermute | solution.py:183
  119.7 25.4 %conditional.7 = (bf16[256,1024]{1,0:T(8,128)(2,1)S(1)}, bf16[256,1024]{1,0:T(8,128)(2,1)S(1)}, bf16[256,1024]{1,0:T(8,128)(2,1)}) conditional(s32[]{:T(128)} %bitcast.5, (bf16[256,1024]{1,0:T(8,128)(2,1)}, bf16[256,1024]{1,0:T(8,128)(2,1)S(1)}, bf16[256,1024]{1,0:T(8,128)(2,1)S(1)}) %tuple.528, ...), branch_computations={%region_64.65_spmd, %region_65.66_spmd, %region_66.67_spmd, %regio... | conditional | bytes 8388752 | solution.py:254
  119.8 6.0 %collective-permute-start.94 = (bf16[256,1024]{1,0:T(8,128)(2,1)S(1)}, bf16[256,1024]{1,0:T(8,128)(2,1)S(1)}, u32[]{:S(2)}, u32[]{:S(2)}) collective-permute-start(bf16[256,1024]{1,0:T(8,128)(2,1)S(1)} %get-tuple-element.832), channel_id=1, source_target_pairs={{0,128},{8,136},{16,144},{24,152},{32,160},{40,168},{48,176},{56,1... | collective-permute-start | bytes 1572872 | tf_op jit(solution)/shard_map/cond/branch_17_fun/ppermute | solution.py:183
  125.8 2.5 %collective-permute-start.95 = (bf16[256,1024]{1,0:T(8,128)(2,1)S(1)}, bf16[256,1024]{1,0:T(8,128)(2,1)S(1)}, u32[]{:S(2)}, u32[]{:S(2)}) collective-permute-start(bf16[256,1024]{1,0:T(8,128)(2,1)S(1)} %get-tuple-element.833), channel_id=1, source_target_pairs={{0,8},{8,0},{16,24},{24,16},{32,40},{40,32},{48,56},{56,48},{64,72... | collective-permute-start | bytes 1572872 | tf_op jit(solution)/shard_map/cond/branch_17_fun/ppermute | solution.py:183
  128.2 3.0 %collective-permute-start.96 = (bf16[256,1024]{1,0:T(8,128)(2,1)}, bf16[256,1024]{1,0:T(8,128)(2,1)}, u32[]{:S(2)}, u32[]{:S(2)}) collective-permute-start(bf16[256,1024]{1,0:T(8,128)(2,1)} %get-tuple-element.834), channel_id=1, source_target_pairs={{0,1},{1,0},{2,3},{3,2},{4,5},{5,4},{6,7},{7,6},{8,9},{9,8},{10,11... | collective-permute-start | bytes 1572872 | tf_op jit(solution)/shard_map/cond/branch_17_fun/ppermute | solution.py:159
  131.3 13.8 %collective-permute-done.94 = bf16[256,1024]{1,0:T(8,128)(2,1)S(1)} collective-permute-done((bf16[256,1024]{1,0:T(8,128)(2,1)S(1)}, bf16[256,1024]{1,0:T(8,128)(2,1)S(1)}, u32[]{:S(2)}, u32[]{:S(2)}) %collective-permute-start.94) | collective-permute-done | bytes 524320 | tf_op jit(solution)/shard_map/cond/branch_17_fun/ppermute | solution.py:183
  145.2 2.4 %collective-permute-start.225 = (bf16[256,1024]{1,0:T(8,128)(2,1)S(1)}, bf16[256,1024]{1,0:T(8,128)(2,1)S(1)}, u32[]{:S(2)}, u32[]{:S(2)}) collective-permute-start(bf16[256,1024]{1,0:T(8,128)(2,1)S(1)} %get-tuple-element.912.refs_0_), channel_id=1, source_target_pairs={{0,1},{1,0},{2,3},{3,2},{4,5},{5,4},{6,7},{7,6},{8,9},{9,8},{10,11... | collective-permute-start | bytes 1572872 | tf_op jit(solution)/shard_map/ppermute | solution.py:159
  151.4 2.2 %copy-done.2 = bf16[4,256,2048]{2,1,0:T(8,128)(2,1)S(1)} copy-done((bf16[4,256,2048]{2,1,0:T(8,128)(2,1)S(1)}, bf16[4,256,2048]{2,1,0:T(8,128)(2,1)}, u32[]{:S(2)}) %copy-start.2) | copy-done | bytes 4194328
  153.6 3.0 %next_pairs.2 = bf16[4,2,256,256]{3,2,1,0:T(8,128)(2,1)S(1)} custom-call(bf16[4,256,2048]{2,1,0:T(8,128)(2,1)S(1)} %copy-done.2, bf16[256,1024]{1,0:T(8,128)(2,1)S(1)} %get-tuple-element.912.refs_0_, bf16[256,1024]{1,0:T(8,128)(2,1)S(1)} %collective-permute-done.225.refs_1_, bf16[256,1024]{1,0:T(8,128)(2,1)S(1)} %get-tuple-element.913.refs_2_, ...), custom_call_target="tpu_custom_call" | custom-call | flops 4294967296 | bytes 4194304 | tf_op jit(solution)/shard_map/next_pairs/pallas_call | solution.py:145
  158.6 2.9 %next_pairs.3 = bf16[4,1,256,256]{3,2,1,0:T(8,128)(2,1)S(1)} custom-call(bf16[4,256,2048]{2,1,0:T(8,128)(2,1)S(1)} %copy-done.2, bf16[256,1024]{1,0:T(8,128)(2,1)S(1)} %copy-done.3, bf16[256,1024]{1,0:T(8,128)(2,1)} %get-tuple-element.914.refs_1_), custom_call_target="tpu_custom_call" | custom-call | flops 2147483648 | bytes 4194304 | tf_op jit(solution)/shard_map/next_pairs/pallas_call | solution.py:145
  161.5 3.3 %collective-permute-start.229 = (bf16[2,1,256,256]{3,2,1,0:T(8,128)(2,1)S(1)}, bf16[2,1,256,256]{3,2,1,0:T(8,128)(2,1)S(1)}, u32[]{:S(2)}, u32[]{:S(2)}) collective-permute-start(bf16[2,1,256,256]{3,2,1,0:T(8,128)(2,1)S(1)} %slice.121), channel_id=1, source_target_pairs={{0,2},{1,3},{2,0},{3,1},{4,6},{5,7},{6,4},{7,5},{8,10},{9,11},{10,... | collective-permute-start | bytes 786440 | tf_op jit(solution)/shard_map/ppermute | solution.py:165
  164.9 12.6 %collective-permute-done.229 = bf16[2,1,256,256]{3,2,1,0:T(8,128)(2,1)S(1)} collective-permute-done((bf16[2,1,256,256]{3,2,1,0:T(8,128)(2,1)S(1)}, bf16[2,1,256,256]{3,2,1,0:T(8,128)(2,1)S(1)}, u32[]{:S(2)}, u32[]{:S(2)}) %collective-permute-start.229) | collective-permute-done | bytes 262176 | tf_op jit(solution)/shard_map/ppermute | solution.py:165
  179.7 4.3 %collective-permute-start.228 = (bf16[2,256,256]{2,1,0:T(8,128)(2,1)S(1)}, bf16[2,256,256]{2,1,0:T(8,128)(2,1)S(1)}, u32[]{:S(2)}, u32[]{:S(2)}) collective-permute-start(bf16[2,256,256]{2,1,0:T(8,128)(2,1)S(1)} %fusion.4), channel_id=1, source_target_pairs={{0,4},{1,5},{2,6},{3,7},{4,0},{5,1},{6,2},{7,3},{8,12},{9,13},{10,... | collective-permute-start | bytes 786440 | tf_op jit(solution)/shard_map/ppermute | solution.py:172
  183.9 10.0 %collective-permute-done.230 = bf16[1,256,256]{2,1,0:T(8,128)(2,1)S(1)} collective-permute-done((bf16[1,256,256]{2,1,0:T(8,128)(2,1)S(1)}, bf16[1,256,256]{2,1,0:T(8,128)(2,1)S(1)}, u32[]{:S(2)}, u32[]{:S(2)}) %collective-permute-start.230) | collective-permute-done | bytes 131104 | tf_op jit(solution)/shard_map/ppermute | solution.py:172
  194.0 5.6 %collective-permute-done.228 = bf16[2,256,256]{2,1,0:T(8,128)(2,1)S(1)} collective-permute-done((bf16[2,256,256]{2,1,0:T(8,128)(2,1)S(1)}, bf16[2,256,256]{2,1,0:T(8,128)(2,1)S(1)}, u32[]{:S(2)}, u32[]{:S(2)}) %collective-permute-start.228) | collective-permute-done | bytes 262176 | tf_op jit(solution)/shard_map/ppermute | solution.py:172
  (49 shorter events, 20.2 us)
Async XLA Ops:
  0.0 52.8 %copy-start = (s32[3,64]{1,0:T(4,128)S(1)}, s32[3,64]{1,0:T(4,128)}, u32[]{:S(2)}) copy-start(s32[3,64]{1,0:T(4,128)} %mask_ref.1) | copy-start | bytes 2308
  1.2 8.6 %collective-permute-start.221 = (bf16[256,512]{1,0:T(8,128)(2,1)S(1)}, bf16[256,512]{1,0:T(8,128)(2,1)S(1)}, u32[]{:S(2)}, u32[]{:S(2)}) collective-permute-start(bf16[256,512]{1,0:T(8,128)(2,1)S(1)} %get-tuple-element.922), channel_id=1, source_target_pairs={{1,0},{2,1},{3,2},{4,3},{5,4},{6,5},{7,6},{9,8},{10,9},{11,10},{12... | collective-permute-start | bytes 786440 | tf_op jit(solution)/shard_map/ppermute | solution.py:224
  3.8 7.2 %collective-permute-start.220 = (bf16[256,512]{1,0:T(8,128)(2,1)S(1)}, bf16[256,512]{1,0:T(8,128)(2,1)S(1)}, u32[]{:S(2)}, u32[]{:S(2)}) collective-permute-start(bf16[256,512]{1,0:T(8,128)(2,1)S(1)} %get-tuple-element.923), channel_id=1, source_target_pairs={{0,1},{1,2},{2,3},{3,4},{4,5},{5,6},{6,7},{8,9},{9,10},{10,11},{11... | collective-permute-start | bytes 786440 | tf_op jit(solution)/shard_map/ppermute | solution.py:223
  13.1 12.5 %collective-permute-start.223 = (bf16[256,1024]{1,0:T(8,128)(2,1)S(1)}, bf16[256,1024]{1,0:T(8,128)(2,1)S(1)}, u32[]{:S(2)}, u32[]{:S(2)}) collective-permute-start(bf16[256,1024]{1,0:T(8,128)(2,1)S(1)} %whiten.1.mine_ref.own), channel_id=1, source_target_pairs={{0,1},{1,0},{2,3},{3,2},{4,5},{5,4},{6,7},{7,6},{8,9},{9,8},{10,11... | collective-permute-start | bytes 1572872 | tf_op jit(solution)/shard_map/ppermute | solution.py:159
  15.0 21.7 %collective-permute-start.222 = (bf16[256,1024]{1,0:T(8,128)(2,1)S(1)}, bf16[256,1024]{1,0:T(8,128)(2,1)S(1)}, u32[]{:S(2)}, u32[]{:S(2)}) collective-permute-start(bf16[256,1024]{1,0:T(8,128)(2,1)S(1)} %whiten.1.mine_ref.own), channel_id=1, source_target_pairs={{0,256},{8,264},{16,272},{24,280},{32,288},{40,296},{48,304},{56,3... | collective-permute-start | bytes 1572872 | tf_op jit(solution)/shard_map/ppermute | solution.py:183
  31.2 2.0 copy-start.1
  36.7 50.6 %collective-permute-start.224 = (bf16[2,1,256,256]{3,2,1,0:T(8,128)(2,1)S(1)}, bf16[2,1,256,256]{3,2,1,0:T(8,128)(2,1)S(1)}, u32[]{:S(2)}, u32[]{:S(2)}) collective-permute-start(bf16[2,1,256,256]{3,2,1,0:T(8,128)(2,1)S(1)} %slice.92), channel_id=1, source_target_pairs={{0,2},{1,3},{2,0},{3,1},{4,6},{5,7},{6,4},{7,5},{8,10},{9,11},{10,... | collective-permute-start | bytes 786440 | tf_op jit(solution)/shard_map/ppermute | solution.py:165
  58.6 27.9 %collective-permute-start.36 = (bf16[256,1024]{1,0:T(8,128)(2,1)S(1)}, bf16[256,1024]{1,0:T(8,128)(2,1)S(1)}, u32[]{:S(2)}, u32[]{:S(2)}) collective-permute-start(bf16[256,1024]{1,0:T(8,128)(2,1)S(1)} %get-tuple-element.635), channel_id=1, source_target_pairs={{0,160},{8,168},{16,176},{24,184},{32,128},{40,136},{48,144},{56,1... | collective-permute-start | bytes 1572872 | tf_op jit(solution)/shard_map/cond/branch_23_fun/ppermute | solution.py:183
  65.0 21.5 %collective-permute-start.37 = (bf16[256,1024]{1,0:T(8,128)(2,1)}, bf16[256,1024]{1,0:T(8,128)(2,1)S(1)}, u32[]{:S(2)}, u32[]{:S(2)}) collective-permute-start(bf16[256,1024]{1,0:T(8,128)(2,1)} %get-tuple-element.636), channel_id=1, source_target_pairs={{0,24},{8,16},{16,8},{24,0},{32,56},{40,48},{48,40},{56,32},{64,88... | collective-permute-start | bytes 1572872 | tf_op jit(solution)/shard_map/cond/branch_23_fun/ppermute | solution.py:183
  87.7 31.2 %collective-permute-start.178 = (bf16[256,1024]{1,0:T(8,128)(2,1)}, bf16[256,1024]{1,0:T(8,128)(2,1)S(1)}, u32[]{:S(2)}, u32[]{:S(2)}) collective-permute-start(bf16[256,1024]{1,0:T(8,128)(2,1)} %get-tuple-element.721), channel_id=1, source_target_pairs={{0,128},{8,136},{16,144},{24,152},{32,160},{40,168},{48,176},{56,1... | collective-permute-start | bytes 1572872 | tf_op jit(solution)/shard_map/cond/branch_17_fun/ppermute | solution.py:183
  94.8 24.9 %collective-permute-start.179 = (bf16[256,1024]{1,0:T(8,128)(2,1)S(1)}, bf16[256,1024]{1,0:T(8,128)(2,1)S(1)}, u32[]{:S(2)}, u32[]{:S(2)}) collective-permute-start(bf16[256,1024]{1,0:T(8,128)(2,1)S(1)} %get-tuple-element.722), channel_id=1, source_target_pairs={{0,8},{8,0},{16,24},{24,16},{32,40},{40,32},{48,56},{56,48},{64,72... | collective-permute-start | bytes 1572872 | tf_op jit(solution)/shard_map/cond/branch_17_fun/ppermute | solution.py:183
  97.2 8.3 %collective-permute-start.180 = (bf16[1,256,256]{2,1,0:T(8,128)(2,1)S(1)}, bf16[1,256,256]{2,1,0:T(8,128)(2,1)S(1)}, u32[]{:S(2)}, u32[]{:S(2)}) collective-permute-start(bf16[1,256,256]{2,1,0:T(8,128)(2,1)S(1)} %get-tuple-element.724), channel_id=1, source_target_pairs={{0,4},{1,5},{2,6},{3,7},{4,0},{5,1},{6,2},{7,3},{8,12},{9,13},{10,... | collective-permute-start | bytes 393224 | tf_op jit(solution)/shard_map/cond/branch_17_fun/ppermute | solution.py:172
  119.8 25.3 %collective-permute-start.94 = (bf16[256,1024]{1,0:T(8,128)(2,1)S(1)}, bf16[256,1024]{1,0:T(8,128)(2,1)S(1)}, u32[]{:S(2)}, u32[]{:S(2)}) collective-permute-start(bf16[256,1024]{1,0:T(8,128)(2,1)S(1)} %get-tuple-element.832), channel_id=1, source_target_pairs={{0,128},{8,136},{16,144},{24,152},{32,160},{40,168},{48,176},{56,1... | collective-permute-start | bytes 1572872 | tf_op jit(solution)/shard_map/cond/branch_17_fun/ppermute | solution.py:183
  125.8 19.3 %collective-permute-start.95 = (bf16[256,1024]{1,0:T(8,128)(2,1)S(1)}, bf16[256,1024]{1,0:T(8,128)(2,1)S(1)}, u32[]{:S(2)}, u32[]{:S(2)}) collective-permute-start(bf16[256,1024]{1,0:T(8,128)(2,1)S(1)} %get-tuple-element.833), channel_id=1, source_target_pairs={{0,8},{8,0},{16,24},{24,16},{32,40},{40,32},{48,56},{56,48},{64,72... | collective-permute-start | bytes 1572872 | tf_op jit(solution)/shard_map/cond/branch_17_fun/ppermute | solution.py:183
  128.2 16.9 %collective-permute-start.96 = (bf16[256,1024]{1,0:T(8,128)(2,1)}, bf16[256,1024]{1,0:T(8,128)(2,1)}, u32[]{:S(2)}, u32[]{:S(2)}) collective-permute-start(bf16[256,1024]{1,0:T(8,128)(2,1)} %get-tuple-element.834), channel_id=1, source_target_pairs={{0,1},{1,0},{2,3},{3,2},{4,5},{5,4},{6,7},{7,6},{8,9},{9,8},{10,11... | collective-permute-start | bytes 1572872 | tf_op jit(solution)/shard_map/cond/branch_17_fun/ppermute | solution.py:159
  145.2 4.3 %collective-permute-start.225 = (bf16[256,1024]{1,0:T(8,128)(2,1)S(1)}, bf16[256,1024]{1,0:T(8,128)(2,1)S(1)}, u32[]{:S(2)}, u32[]{:S(2)}) collective-permute-start(bf16[256,1024]{1,0:T(8,128)(2,1)S(1)} %get-tuple-element.912.refs_0_), channel_id=1, source_target_pairs={{0,1},{1,0},{2,3},{3,2},{4,5},{5,4},{6,7},{7,6},{8,9},{9,8},{10,11... | collective-permute-start | bytes 1572872 | tf_op jit(solution)/shard_map/ppermute | solution.py:159
  147.6 3.8 %collective-permute-start.226 = (bf16[256,1024]{1,0:T(8,128)(2,1)S(1)}, bf16[256,1024]{1,0:T(8,128)(2,1)S(1)}, u32[]{:S(2)}, u32[]{:S(2)}) collective-permute-start(bf16[256,1024]{1,0:T(8,128)(2,1)S(1)} %get-tuple-element.913.refs_2_), channel_id=1, source_target_pairs={{0,1},{1,0},{2,3},{3,2},{4,5},{5,4},{6,7},{7,6},{8,9},{9,8},{10,11... | collective-permute-start | bytes 1572872 | tf_op jit(solution)/shard_map/ppermute | solution.py:159
  151.4 2.2 %copy-start.2 = (bf16[4,256,2048]{2,1,0:T(8,128)(2,1)S(1)}, bf16[4,256,2048]{2,1,0:T(8,128)(2,1)}, u32[]{:S(2)}) copy-start(bf16[4,256,2048]{2,1,0:T(8,128)(2,1)} %copy-done.1) | copy-start | bytes 12582916
  153.6 5.0 %copy-start.3 = (bf16[256,1024]{1,0:T(8,128)(2,1)S(1)}, bf16[256,1024]{1,0:T(8,128)(2,1)}, u32[]{:S(2)}) copy-start(bf16[256,1024]{1,0:T(8,128)(2,1)} %get-tuple-element.909.refs_0_) | copy-start | bytes 1572868
  156.6 22.9 %collective-permute-start.227 = (bf16[2,2,256,256]{3,2,1,0:T(8,128)(2,1)S(1)}, bf16[2,2,256,256]{3,2,1,0:T(8,128)(2,1)S(1)}, u32[]{:S(2)}, u32[]{:S(2)}) collective-permute-start(bf16[2,2,256,256]{3,2,1,0:T(8,128)(2,1)S(1)} %slice.115), channel_id=1, source_target_pairs={{0,2},{1,3},{2,0},{3,1},{4,6},{5,7},{6,4},{7,5},{8,10},{9,11},{10,... | collective-permute-start | bytes 1572872 | tf_op jit(solution)/shard_map/ppermute | solution.py:165
  161.5 16.0 %collective-permute-start.229 = (bf16[2,1,256,256]{3,2,1,0:T(8,128)(2,1)S(1)}, bf16[2,1,256,256]{3,2,1,0:T(8,128)(2,1)S(1)}, u32[]{:S(2)}, u32[]{:S(2)}) collective-permute-start(bf16[2,1,256,256]{3,2,1,0:T(8,128)(2,1)S(1)} %slice.121), channel_id=1, source_target_pairs={{0,2},{1,3},{2,0},{3,1},{4,6},{5,7},{6,4},{7,5},{8,10},{9,11},{10,... | collective-permute-start | bytes 786440 | tf_op jit(solution)/shard_map/ppermute | solution.py:165
  177.6 16.4 %collective-permute-start.230 = (bf16[1,256,256]{2,1,0:T(8,128)(2,1)S(1)}, bf16[1,256,256]{2,1,0:T(8,128)(2,1)S(1)}, u32[]{:S(2)}, u32[]{:S(2)}) collective-permute-start(bf16[1,256,256]{2,1,0:T(8,128)(2,1)S(1)} %fusion.12), channel_id=1, source_target_pairs={{0,4},{1,5},{2,6},{3,7},{4,0},{5,1},{6,2},{7,3},{8,12},{9,13},{10,... | collective-permute-start | bytes 393224 | tf_op jit(solution)/shard_map/ppermute | solution.py:172
  179.7 19.9 %collective-permute-start.228 = (bf16[2,256,256]{2,1,0:T(8,128)(2,1)S(1)}, bf16[2,256,256]{2,1,0:T(8,128)(2,1)S(1)}, u32[]{:S(2)}, u32[]{:S(2)}) collective-permute-start(bf16[2,256,256]{2,1,0:T(8,128)(2,1)S(1)} %fusion.4), channel_id=1, source_target_pairs={{0,4},{1,5},{2,6},{3,7},{4,0},{5,1},{6,2},{7,3},{8,12},{9,13},{10,... | collective-permute-start | bytes 786440 | tf_op jit(solution)/shard_map/ppermute | solution.py:172

commit v3 on v2

--- a/solution.py
+++ b/solution.py
@@ -231,16 +231,17 @@
     )
     white = whiten(x, low, high, half_wide, bin_dev)
     top = chan_count // 2
+    y_count = top // NEAR
+    masks = partners[:, 0]
+    x_of, y_of = masks & (NEAR - 1), (masks & (top - 1)) >> (NEAR.bit_length() - 1)
+    index = [y_of[r] * NEAR + x_of[(r + 1) % ROUNDS] for r in range(ROUNDS)]
     far_white = exchange(white, top, chan_count)
-    other = swap_cores(white, freq_count)
+    other, *index = lax.optimization_barrier((swap_cores(white, freq_count), *index))
     turned, partial = first_pair(white, other, table, width)
     far_white, partial = lax.optimization_barrier((far_white, partial))
     base = pick(partners, white, far_white, top)
-    masks = partners[:, 0]
-    x_of, y_of = masks & (NEAR - 1), (masks & (top - 1)) >> (NEAR.bit_length() - 1)
-    y_count = top // NEAR
-
-    def stage(y_round, y_block, x_round, x_block, beside, *operands):
+
+    def stage(y_round, y_block, x_block, beside, *operands):
         def make(y_mask, x_mask):
             def run(y_block, x_block, *operands):
                 return (
@@ -252,25 +253,31 @@
             return run
 
         return lax.switch(
-            y_of[y_round] * NEAR + x_of[x_round],
+            index[y_round],
             [make(i, j) for i in range(y_count) for j in range(NEAR)],
             y_block,
             x_block,
             *operands,
         )
 
-    half_0, half_1, _ = stage(0, base[0], 1, base[1], lambda: ())
+    half_0, half_1, _ = stage(0, base[0], base[1], lambda: ())
     kept, passing = beside_step(partial, freq_count)
     half_0, half_1, kept, passing = lax.optimization_barrier((half_0, half_1, kept, passing))
     block_1, half_2, sum_own = stage(
-        1, half_1, 2, base[2], lambda *sums: across_step(*sums, freq_count), kept, passing
+        1, half_1, base[2], lambda *sums: across_step(*sums, freq_count), kept, passing
     )
     block_2, block_0, other_1 = stage(
-        2, half_2, 0, half_0, lambda block: swap_cores(block, freq_count), block_1
-    )
-    sum_1 = scatter(next_pairs(turned, block_1, other_1), freq_count)
+        2, half_2, half_0, lambda block: swap_cores(block, freq_count), block_1
+    )
+    partial = next_pairs(turned, block_1, other_1)
+    block_0, block_2, partial = lax.optimization_barrier((block_0, block_2, partial))
+    step_1 = beside_step(partial, freq_count)
     other_0, other_2 = swap_cores(block_0, freq_count), swap_cores(block_2, freq_count)
-    sum_02 = scatter(next_pairs(turned, block_0, other_0, block_2, other_2), freq_count)
+    other_0, other_2, *step_1 = lax.optimization_barrier((other_0, other_2, *step_1))
+    sum_1 = across_step(*step_1, freq_count)
+    partial = next_pairs(turned, block_0, other_0, block_2, other_2)
+    *step_02, sum_1 = lax.optimization_barrier((*beside_step(partial, freq_count), sum_1))
+    sum_02 = across_step(*step_02, freq_count)
     return jnp.concatenate([sum_own, sum_02[:1], sum_1, sum_02[1:]])[None]
 
 

time: 201 us -> 191 us (0.950)
  the two profiles are of different devices: /device:TPU:15 before, /device:TPU:17 now
where the time goes in v3:
time: 191 us; the launch traced here: 190 us
  waiting for transfers between devices  98.4 us (52%)
  starting transfers between devices  60.6 us (32%)
  Pallas kernels  15 us (8%)
  local copies, waits for them, and re-layouts  8.65 us (5%)
  between operations  3.99 us (2%)
  other arithmetic  2.75 us (1%)
    ppermute x6, waiting for transfers between devices, exchange(): return lax.ppermute(block, 'chan', [(i, i ^ mask) for i in range(count)])  55.3 us
    ppermute x3, waiting for transfers between devices, across_step(): passed = lax.ppermute(passing, 'freq', route).astype(jnp.float32)  31.6 us
    ppermute x6, starting transfers between devices, exchange(): return lax.ppermute(block, 'chan', [(i, i ^ mask) for i in range(count)])  27.2 us
    ppermute x3, starting transfers between devices, beside_step(): arrived = lax.ppermute(partial[half:], 'freq', route).astype(jnp.float32)  9.46 us
    ppermute x4, starting transfers between devices, swap_cores(): return lax.ppermute(block, 'freq', [(i, i ^ 1) for i in range(size)])  9.44 us
    ppermute x3, waiting for transfers between devices, beside_step(): arrived = lax.ppermute(partial[half:], 'freq', route).astype(jnp.float32)  8.86 us
    ppermute x3, starting transfers between devices, across_step(): passed = lax.ppermute(passing, 'freq', route).astype(jnp.float32)  7.96 us
    unnamed x9, local copies, waits for them, and re-layouts  6.12 us
  transfers between devices with their start and end apart: 18, of which 11 were waited for; matrix products, arithmetic and copies ran while one was open for 2% of the time, Pallas kernels for 4%

profile of v3, /device:TPU:17, one launch (start us, length us, event | category | flops | bytes accessed | tf_op | source)
XLA Modules:
  0.0 189.8 jit_solution(4032021742216237084)
XLA Ops:
  1.2 2.6 %collective-permute-start.221 = (bf16[256,512]{1,0:T(8,128)(2,1)S(1)}, bf16[256,512]{1,0:T(8,128)(2,1)S(1)}, u32[]{:S(2)}, u32[]{:S(2)}) collective-permute-start(bf16[256,512]{1,0:T(8,128)(2,1)S(1)} %get-tuple-element.954), channel_id=1, source_target_pairs={{1,0},{2,1},{3,2},{4,3},{5,4},{6,5},{7,6},{9,8},{10,9},{11,10},{12... | collective-permute-start | bytes 786440 | tf_op jit(solution)/shard_map/ppermute | solution.py:224
  3.8 3.9 %collective-permute-start.220 = (bf16[256,512]{1,0:T(8,128)(2,1)S(1)}, bf16[256,512]{1,0:T(8,128)(2,1)S(1)}, u32[]{:S(2)}, u32[]{:S(2)}) collective-permute-start(bf16[256,512]{1,0:T(8,128)(2,1)S(1)} %get-tuple-element.955), channel_id=1, source_target_pairs={{0,1},{1,2},{2,3},{3,4},{4,5},{5,6},{6,7},{8,9},{9,10},{10,11},{11... | collective-permute-start | bytes 786440 | tf_op jit(solution)/shard_map/ppermute | solution.py:223
  11.1 2.0 %whiten.1.mine_ref.own = bf16[256,1024]{1,0:T(8,128)(2,1)S(1)} custom-call(bf16[256,1024]{1,0:T(8,128)(2,1)S(1)} %bitcast.24, bf16[256,512]{1,0:T(8,128)(2,1)S(1)} %collective-permute-done.220.low_ref, bf16[256,512]{1,0:T(8,128)(2,1)S(1)} %collective-permute-done.221.high_ref, f32[256,128]{1,0:T(8,128)S(1)} %broadcast_in_dim.4.half_ref), custom_call_target="tpu_custom_call" | custom-call | tf_op jit(solution)/shard_map/whiten/pallas_call | solution.py:72
  13.1 9.7 %collective-permute-start.223 = (bf16[256,1024]{1,0:T(8,128)(2,1)S(1)}, bf16[256,1024]{1,0:T(8,128)(2,1)S(1)}, u32[]{:S(2)}, u32[]{:S(2)}) collective-permute-start(bf16[256,1024]{1,0:T(8,128)(2,1)S(1)} %whiten.1.mine_ref.own), channel_id=1, source_target_pairs={{0,256},{8,264},{16,272},{24,280},{32,288},{40,296},{48,304},{56,3... | collective-permute-start | bytes 1572872 | tf_op jit(solution)/shard_map/ppermute | solution.py:183
  22.8 1.9 %collective-permute-start.222 = (bf16[256,1024]{1,0:T(8,128)(2,1)S(1)}, bf16[256,1024]{1,0:T(8,128)(2,1)S(1)}, u32[]{:S(2)}, u32[]{:S(2)}) collective-permute-start(bf16[256,1024]{1,0:T(8,128)(2,1)S(1)} %whiten.1.mine_ref.own), channel_id=1, source_target_pairs={{0,1},{1,0},{2,3},{3,2},{4,5},{5,4},{6,7},{7,6},{8,9},{9,8},{10,11... | collective-permute-start | bytes 1572872 | tf_op jit(solution)/shard_map/ppermute | solution.py:159
  30.6 5.6 %first_pair.1 = (bf16[4,256,2048]{2,1,0:T(8,128)(2,1)S(1)}, bf16[4,1,256,256]{3,2,1,0:T(8,128)(2,1)S(1)}) custom-call(bf16[256,1024]{1,0:T(8,128)(2,1)S(1)} %whiten.1.mine_ref.own, bf16[256,1024]{1,0:T(8,128)(2,1)S(1)} %collective-permute-done.222.other_ref, f32[8,2048]{1,0:T(8,128)S(1)} %dynamic-slice_bitcast_fusion.table_ref), custom_call_target="tpu_custom_call" | custom-call | tf_op jit(solution)/shard_map/first_pair/pallas_call | solution.py:128
  36.2 2.0 %copy-done.1 = bf16[4,256,2048]{2,1,0:T(8,128)(2,1)} copy-done((bf16[4,256,2048]{2,1,0:T(8,128)(2,1)}, bf16[4,256,2048]{2,1,0:T(8,128)(2,1)S(1)}, u32[]{:S(2)}) %copy-start.1) | copy-done | bytes 4194328
  38.1 5.4 %collective-permute-done.223.far = bf16[256,1024]{1,0:T(8,128)(2,1)S(1)} collective-permute-done((bf16[256,1024]{1,0:T(8,128)(2,1)S(1)}, bf16[256,1024]{1,0:T(8,128)(2,1)S(1)}, u32[]{:S(2)}, u32[]{:S(2)}) %collective-permute-start.223) | collective-permute-done | bytes 524320 | tf_op jit(solution)/shard_map/ppermute | solution.py:183
  43.5 5.0 %collective-permute-start.224 = (bf16[2,1,256,256]{3,2,1,0:T(8,128)(2,1)S(1)}, bf16[2,1,256,256]{3,2,1,0:T(8,128)(2,1)S(1)}, u32[]{:S(2)}, u32[]{:S(2)}) collective-permute-start(bf16[2,1,256,256]{3,2,1,0:T(8,128)(2,1)S(1)} %slice.94), channel_id=1, source_target_pairs={{0,2},{1,3},{2,0},{3,1},{4,6},{5,7},{6,4},{7,5},{8,10},{9,11},{10,... | collective-permute-start | bytes 786440 | tf_op jit(solution)/shard_map/ppermute | solution.py:165
  50.0 30.8 %conditional.5 = ((bf16[256,1024]{1,0:T(8,128)(2,1)S(1)}, bf16[256,1024]{1,0:T(8,128)(2,1)})) conditional(s32[]{:T(128)} %clamp.10, (bf16[256,1024]{1,0:T(8,128)(2,1)S(1)}, bf16[256,1024]{1,0:T(8,128)(2,1)}) %tuple.526, (bf16[256,1024]{1,0:T(8,128)(2,1)}, bf16[256,1024]{1,0:T(8,128)(2,1)S(1)}) %tuple.527, ...), branch_computations={%region_0.1_spmd, %region_1.2_spmd, %region_2.3_spmd, %region_3.4_... | conditional | bytes 6291560 | solution.py:255
  50.1 4.9 %collective-permute-start.36 = (bf16[256,1024]{1,0:T(8,128)(2,1)S(1)}, bf16[256,1024]{1,0:T(8,128)(2,1)S(1)}, u32[]{:S(2)}, u32[]{:S(2)}) collective-permute-start(bf16[256,1024]{1,0:T(8,128)(2,1)S(1)} %get-tuple-element.635), channel_id=1, source_target_pairs={{0,160},{8,168},{16,176},{24,184},{32,128},{40,136},{48,144},{56,1... | collective-permute-start | bytes 1572872 | tf_op jit(solution)/shard_map/cond/branch_23_fun/ppermute | solution.py:183
  54.9 4.4 %collective-permute-start.37 = (bf16[256,1024]{1,0:T(8,128)(2,1)}, bf16[256,1024]{1,0:T(8,128)(2,1)S(1)}, u32[]{:S(2)}, u32[]{:S(2)}) collective-permute-start(bf16[256,1024]{1,0:T(8,128)(2,1)} %get-tuple-element.636), channel_id=1, source_target_pairs={{0,24},{8,16},{16,8},{24,0},{32,56},{40,48},{48,40},{56,32},{64,88... | collective-permute-start | bytes 1572872 | tf_op jit(solution)/shard_map/cond/branch_23_fun/ppermute | solution.py:183
  59.3 20.6 %collective-permute-done.36 = bf16[256,1024]{1,0:T(8,128)(2,1)S(1)} collective-permute-done((bf16[256,1024]{1,0:T(8,128)(2,1)S(1)}, bf16[256,1024]{1,0:T(8,128)(2,1)S(1)}, u32[]{:S(2)}, u32[]{:S(2)}) %collective-permute-start.36) | collective-permute-done | bytes 524320 | tf_op jit(solution)/shard_map/cond/branch_23_fun/ppermute | solution.py:183
  80.9 25.7 %conditional.8 = (bf16[256,1024]{1,0:T(8,128)(2,1)}, bf16[256,1024]{1,0:T(8,128)(2,1)S(1)}, bf16[1,256,256]{2,1,0:T(8,128)(2,1)S(1)}) conditional(s32[]{:T(128)} %clamp.9, (bf16[1,256,256]{2,1,0:T(8,128)(2,1)S(1)}, f32[1,256,256]{2,1,0:T(8,128)S(1)}, bf16[256,1024]{1,0:T(8,128)(2,1)}, ...), branch_computations={%region_32.33_spmd, %region_33.34_spmd, %region_34.35_spmd, %regio... | conditional | flops 196608 | bytes 7340176
  82.9 4.4 %collective-permute-start.163 = (bf16[256,1024]{1,0:T(8,128)(2,1)S(1)}, bf16[256,1024]{1,0:T(8,128)(2,1)S(1)}, u32[]{:S(2)}, u32[]{:S(2)}) collective-permute-start(bf16[256,1024]{1,0:T(8,128)(2,1)S(1)} %get-tuple-element.698), channel_id=1, source_target_pairs={{0,24},{8,16},{16,8},{24,0},{32,56},{40,48},{48,40},{56,32},{64,88... | collective-permute-start | bytes 1572872 | tf_op jit(solution)/shard_map/cond/branch_11_fun/ppermute | solution.py:183
  87.3 1.9 %collective-permute-start.164 = (bf16[1,256,256]{2,1,0:T(8,128)(2,1)S(1)}, bf16[1,256,256]{2,1,0:T(8,128)(2,1)S(1)}, u32[]{:S(2)}, u32[]{:S(2)}) collective-permute-start(bf16[1,256,256]{2,1,0:T(8,128)(2,1)S(1)} %get-tuple-element.700), channel_id=1, source_target_pairs={{0,4},{1,5},{2,6},{3,7},{4,0},{5,1},{6,2},{7,3},{8,12},{9,13},{10,... | collective-permute-start | bytes 393224 | tf_op jit(solution)/shard_map/cond/branch_11_fun/ppermute | solution.py:172
  89.2 8.8 %collective-permute-done.164 = bf16[1,256,256]{2,1,0:T(8,128)(2,1)S(1)} collective-permute-done((bf16[1,256,256]{2,1,0:T(8,128)(2,1)S(1)}, bf16[1,256,256]{2,1,0:T(8,128)(2,1)S(1)}, u32[]{:S(2)}, u32[]{:S(2)}) %collective-permute-start.164) | collective-permute-done | bytes 131104 | tf_op jit(solution)/shard_map/cond/branch_11_fun/ppermute | solution.py:172
  98.1 7.5 %collective-permute-done.162 = bf16[256,1024]{1,0:T(8,128)(2,1)S(1)} collective-permute-done((bf16[256,1024]{1,0:T(8,128)(2,1)}, bf16[256,1024]{1,0:T(8,128)(2,1)S(1)}, u32[]{:S(2)}, u32[]{:S(2)}) %collective-permute-start.162) | collective-permute-done | bytes 524320 | tf_op jit(solution)/shard_map/cond/branch_11_fun/ppermute | solution.py:183
  106.6 26.3 %conditional.7 = (bf16[256,1024]{1,0:T(8,128)(2,1)S(1)}, bf16[256,1024]{1,0:T(8,128)(2,1)S(1)}, bf16[256,1024]{1,0:T(8,128)(2,1)}) conditional(s32[]{:T(128)} %clamp.11, (bf16[256,1024]{1,0:T(8,128)(2,1)}, bf16[256,1024]{1,0:T(8,128)(2,1)S(1)}, bf16[256,1024]{1,0:T(8,128)(2,1)S(1)}) %tuple.533, ...), branch_computations={%region_64.65_spmd, %region_65.66_spmd, %region_66.67_spmd, %regio... | conditional | bytes 8388752 | solution.py:255
  108.6 2.4 %collective-permute-start.82 = (bf16[256,1024]{1,0:T(8,128)(2,1)}, bf16[256,1024]{1,0:T(8,128)(2,1)}, u32[]{:S(2)}, u32[]{:S(2)}) collective-permute-start(bf16[256,1024]{1,0:T(8,128)(2,1)} %get-tuple-element.819), channel_id=1, source_target_pairs={{0,1},{1,0},{2,3},{3,2},{4,5},{5,4},{6,7},{7,6},{8,9},{9,8},{10,11... | collective-permute-start | bytes 1572872 | tf_op jit(solution)/shard_map/cond/branch_12_fun/ppermute | solution.py:159
  111.0 21.8 %collective-permute-done.81 = bf16[256,1024]{1,0:T(8,128)(2,1)S(1)} collective-permute-done((bf16[256,1024]{1,0:T(8,128)(2,1)S(1)}, bf16[256,1024]{1,0:T(8,128)(2,1)S(1)}, u32[]{:S(2)}, u32[]{:S(2)}) %collective-permute-start.81) | collective-permute-done | bytes 524320 | tf_op jit(solution)/shard_map/cond/branch_12_fun/ppermute | solution.py:183
  132.9 2.2 %copy-done.2 = bf16[4,256,2048]{2,1,0:T(8,128)(2,1)S(1)} copy-done((bf16[4,256,2048]{2,1,0:T(8,128)(2,1)S(1)}, bf16[4,256,2048]{2,1,0:T(8,128)(2,1)}, u32[]{:S(2)}) %copy-start.2) | copy-done | bytes 4194328
  135.1 3.1 %next_pairs.2 = bf16[4,1,256,256]{3,2,1,0:T(8,128)(2,1)S(1)} custom-call(bf16[4,256,2048]{2,1,0:T(8,128)(2,1)S(1)} %copy-done.2, bf16[256,1024]{1,0:T(8,128)(2,1)} %get-tuple-element.927.refs_0_, bf16[256,1024]{1,0:T(8,128)(2,1)} %get-tuple-element.932.refs_1_), custom_call_target="tpu_custom_call" | custom-call | flops 2147483648 | bytes 4194304 | tf_op jit(solution)/shard_map/next_pairs/pallas_call | solution.py:145
  138.2 3.2 %collective-permute-start.225 = (bf16[256,1024]{1,0:T(8,128)(2,1)S(1)}, bf16[256,1024]{1,0:T(8,128)(2,1)S(1)}, u32[]{:S(2)}, u32[]{:S(2)}) collective-permute-start(bf16[256,1024]{1,0:T(8,128)(2,1)S(1)} %get-tuple-element.933.refs_0_), channel_id=1, source_target_pairs={{0,1},{1,0},{2,3},{3,2},{4,5},{5,4},{6,7},{7,6},{8,9},{9,8},{10,11... | collective-permute-start | bytes 1572872 | tf_op jit(solution)/shard_map/ppermute | solution.py:159
  143.4 2.2 %collective-permute-start.227 = (bf16[2,1,256,256]{3,2,1,0:T(8,128)(2,1)S(1)}, bf16[2,1,256,256]{3,2,1,0:T(8,128)(2,1)S(1)}, u32[]{:S(2)}, u32[]{:S(2)}) collective-permute-start(bf16[2,1,256,256]{3,2,1,0:T(8,128)(2,1)S(1)} %slice.99), channel_id=1, source_target_pairs={{0,2},{1,3},{2,0},{3,1},{4,6},{5,7},{6,4},{7,5},{8,10},{9,11},{10,... | collective-permute-start | bytes 786440 | tf_op jit(solution)/shard_map/ppermute | solution.py:165
  145.6 7.0 %collective-permute-done.227 = bf16[2,1,256,256]{3,2,1,0:T(8,128)(2,1)S(1)} collective-permute-done((bf16[2,1,256,256]{3,2,1,0:T(8,128)(2,1)S(1)}, bf16[2,1,256,256]{3,2,1,0:T(8,128)(2,1)S(1)}, u32[]{:S(2)}, u32[]{:S(2)}) %collective-permute-start.227) | collective-permute-done | bytes 262176 | tf_op jit(solution)/shard_map/ppermute | solution.py:165
  152.7 3.0 %next_pairs.3 = bf16[4,2,256,256]{3,2,1,0:T(8,128)(2,1)S(1)} custom-call(bf16[4,256,2048]{2,1,0:T(8,128)(2,1)S(1)} %copy-done.2, bf16[256,1024]{1,0:T(8,128)(2,1)S(1)} %get-tuple-element.933.refs_0_, bf16[256,1024]{1,0:T(8,128)(2,1)S(1)} %collective-permute-done.225.refs_1_, bf16[256,1024]{1,0:T(8,128)(2,1)S(1)} %get-tuple-element.934.refs_2_, ...), custom_call_target="tpu_custom_call" | custom-call | flops 4294967296 | bytes 4194304 | tf_op jit(solution)/shard_map/next_pairs/pallas_call | solution.py:145
  155.8 2.2 %collective-permute-start.228 = (bf16[2,2,256,256]{3,2,1,0:T(8,128)(2,1)S(1)}, bf16[2,2,256,256]{3,2,1,0:T(8,128)(2,1)S(1)}, u32[]{:S(2)}, u32[]{:S(2)}) collective-permute-start(bf16[2,2,256,256]{3,2,1,0:T(8,128)(2,1)S(1)} %slice.117), channel_id=1, source_target_pairs={{0,2},{1,3},{2,0},{3,1},{4,6},{5,7},{6,4},{7,5},{8,10},{9,11},{10,... | collective-permute-start | bytes 1572872 | tf_op jit(solution)/shard_map/ppermute | solution.py:165
  158.0 3.2 %collective-permute-start.229 = (bf16[1,256,256]{2,1,0:T(8,128)(2,1)S(1)}, bf16[1,256,256]{2,1,0:T(8,128)(2,1)S(1)}, u32[]{:S(2)}, u32[]{:S(2)}) collective-permute-start(bf16[1,256,256]{2,1,0:T(8,128)(2,1)S(1)} %get-tuple-element.939), channel_id=1, source_target_pairs={{0,4},{1,5},{2,6},{3,7},{4,0},{5,1},{6,2},{7,3},{8,12},{9,13},{10,... | collective-permute-start | bytes 393224 | tf_op jit(solution)/shard_map/ppermute | solution.py:172
  161.2 9.5 %collective-permute-done.229 = bf16[1,256,256]{2,1,0:T(8,128)(2,1)S(1)} collective-permute-done((bf16[1,256,256]{2,1,0:T(8,128)(2,1)S(1)}, bf16[1,256,256]{2,1,0:T(8,128)(2,1)S(1)}, u32[]{:S(2)}, u32[]{:S(2)}) %collective-permute-start.229) | collective-permute-done | bytes 131104 | tf_op jit(solution)/shard_map/ppermute | solution.py:172
  172.7 2.9 %collective-permute-start.230 = (bf16[2,256,256]{2,1,0:T(8,128)(2,1)S(1)}, bf16[2,256,256]{2,1,0:T(8,128)(2,1)S(1)}, u32[]{:S(2)}, u32[]{:S(2)}) collective-permute-start(bf16[2,256,256]{2,1,0:T(8,128)(2,1)S(1)} %get-tuple-element.941), channel_id=1, source_target_pairs={{0,4},{1,5},{2,6},{3,7},{4,0},{5,1},{6,2},{7,3},{8,12},{9,13},{10,... | collective-permute-start | bytes 786440 | tf_op jit(solution)/shard_map/ppermute | solution.py:172
  175.6 13.3 %collective-permute-done.230 = bf16[2,256,256]{2,1,0:T(8,128)(2,1)S(1)} collective-permute-done((bf16[2,256,256]{2,1,0:T(8,128)(2,1)S(1)}, bf16[2,256,256]{2,1,0:T(8,128)(2,1)S(1)}, u32[]{:S(2)}, u32[]{:S(2)}) %collective-permute-start.230) | collective-permute-done | bytes 262176 | tf_op jit(solution)/shard_map/ppermute | solution.py:172
  (44 shorter events, 18.9 us)
Async XLA Ops:
  0.0 48.5 %copy-start = (s32[3,64]{1,0:T(4,128)S(1)}, s32[3,64]{1,0:T(4,128)}, u32[]{:S(2)}) copy-start(s32[3,64]{1,0:T(4,128)} %mask_ref.1) | copy-start | bytes 2308
  1.2 8.6 %collective-permute-start.221 = (bf16[256,512]{1,0:T(8,128)(2,1)S(1)}, bf16[256,512]{1,0:T(8,128)(2,1)S(1)}, u32[]{:S(2)}, u32[]{:S(2)}) collective-permute-start(bf16[256,512]{1,0:T(8,128)(2,1)S(1)} %get-tuple-element.954), channel_id=1, source_target_pairs={{1,0},{2,1},{3,2},{4,3},{5,4},{6,5},{7,6},{9,8},{10,9},{11,10},{12... | collective-permute-start | bytes 786440 | tf_op jit(solution)/shard_map/ppermute | solution.py:224
  3.8 7.2 %collective-permute-start.220 = (bf16[256,512]{1,0:T(8,128)(2,1)S(1)}, bf16[256,512]{1,0:T(8,128)(2,1)S(1)}, u32[]{:S(2)}, u32[]{:S(2)}) collective-permute-start(bf16[256,512]{1,0:T(8,128)(2,1)S(1)} %get-tuple-element.955), channel_id=1, source_target_pairs={{0,1},{1,2},{2,3},{3,4},{4,5},{5,6},{6,7},{8,9},{9,10},{10,11},{11... | collective-permute-start | bytes 786440 | tf_op jit(solution)/shard_map/ppermute | solution.py:223
  13.1 30.4 %collective-permute-start.223 = (bf16[256,1024]{1,0:T(8,128)(2,1)S(1)}, bf16[256,1024]{1,0:T(8,128)(2,1)S(1)}, u32[]{:S(2)}, u32[]{:S(2)}) collective-permute-start(bf16[256,1024]{1,0:T(8,128)(2,1)S(1)} %whiten.1.mine_ref.own), channel_id=1, source_target_pairs={{0,256},{8,264},{16,272},{24,280},{32,288},{40,296},{48,304},{56,3... | collective-permute-start | bytes 1572872 | tf_op jit(solution)/shard_map/ppermute | solution.py:183
  22.8 7.8 %collective-permute-start.222 = (bf16[256,1024]{1,0:T(8,128)(2,1)S(1)}, bf16[256,1024]{1,0:T(8,128)(2,1)S(1)}, u32[]{:S(2)}, u32[]{:S(2)}) collective-permute-start(bf16[256,1024]{1,0:T(8,128)(2,1)S(1)} %whiten.1.mine_ref.own), channel_id=1, source_target_pairs={{0,1},{1,0},{2,3},{3,2},{4,5},{5,4},{6,7},{7,6},{8,9},{9,8},{10,11... | collective-permute-start | bytes 1572872 | tf_op jit(solution)/shard_map/ppermute | solution.py:159
  36.2 2.0 %copy-start.1 = (bf16[4,256,2048]{2,1,0:T(8,128)(2,1)}, bf16[4,256,2048]{2,1,0:T(8,128)(2,1)S(1)}, u32[]{:S(2)}) copy-start(bf16[4,256,2048]{2,1,0:T(8,128)(2,1)S(1)} %get-tuple-element.925.turned_ref) | copy-start | bytes 12582916
  43.5 37.3 %collective-permute-start.224 = (bf16[2,1,256,256]{3,2,1,0:T(8,128)(2,1)S(1)}, bf16[2,1,256,256]{3,2,1,0:T(8,128)(2,1)S(1)}, u32[]{:S(2)}, u32[]{:S(2)}) collective-permute-start(bf16[2,1,256,256]{3,2,1,0:T(8,128)(2,1)S(1)} %slice.94), channel_id=1, source_target_pairs={{0,2},{1,3},{2,0},{3,1},{4,6},{5,7},{6,4},{7,5},{8,10},{9,11},{10,... | collective-permute-start | bytes 786440 | tf_op jit(solution)/shard_map/ppermute | solution.py:165
  50.1 29.9 %collective-permute-start.36 = (bf16[256,1024]{1,0:T(8,128)(2,1)S(1)}, bf16[256,1024]{1,0:T(8,128)(2,1)S(1)}, u32[]{:S(2)}, u32[]{:S(2)}) collective-permute-start(bf16[256,1024]{1,0:T(8,128)(2,1)S(1)} %get-tuple-element.635), channel_id=1, source_target_pairs={{0,160},{8,168},{16,176},{24,184},{32,128},{40,136},{48,144},{56,1... | collective-permute-start | bytes 1572872 | tf_op jit(solution)/shard_map/cond/branch_23_fun/ppermute | solution.py:183
  54.9 25.1 %collective-permute-start.37 = (bf16[256,1024]{1,0:T(8,128)(2,1)}, bf16[256,1024]{1,0:T(8,128)(2,1)S(1)}, u32[]{:S(2)}, u32[]{:S(2)}) collective-permute-start(bf16[256,1024]{1,0:T(8,128)(2,1)} %get-tuple-element.636), channel_id=1, source_target_pairs={{0,24},{8,16},{16,8},{24,0},{32,56},{40,48},{48,40},{56,32},{64,88... | collective-permute-start | bytes 1572872 | tf_op jit(solution)/shard_map/cond/branch_23_fun/ppermute | solution.py:183
  81.0 24.6 %collective-permute-start.162 = (bf16[256,1024]{1,0:T(8,128)(2,1)}, bf16[256,1024]{1,0:T(8,128)(2,1)S(1)}, u32[]{:S(2)}, u32[]{:S(2)}) collective-permute-start(bf16[256,1024]{1,0:T(8,128)(2,1)} %get-tuple-element.697), channel_id=1, source_target_pairs={{0,64},{8,72},{16,80},{24,88},{32,96},{40,104},{48,112},{56,120},{... | collective-permute-start | bytes 1572872 | tf_op jit(solution)/shard_map/cond/branch_11_fun/ppermute | solution.py:183
  82.9 23.5 %collective-permute-start.163 = (bf16[256,1024]{1,0:T(8,128)(2,1)S(1)}, bf16[256,1024]{1,0:T(8,128)(2,1)S(1)}, u32[]{:S(2)}, u32[]{:S(2)}) collective-permute-start(bf16[256,1024]{1,0:T(8,128)(2,1)S(1)} %get-tuple-element.698), channel_id=1, source_target_pairs={{0,24},{8,16},{16,8},{24,0},{32,56},{40,48},{48,40},{56,32},{64,88... | collective-permute-start | bytes 1572872 | tf_op jit(solution)/shard_map/cond/branch_11_fun/ppermute | solution.py:183
  87.3 10.7 %collective-permute-start.164 = (bf16[1,256,256]{2,1,0:T(8,128)(2,1)S(1)}, bf16[1,256,256]{2,1,0:T(8,128)(2,1)S(1)}, u32[]{:S(2)}, u32[]{:S(2)}) collective-permute-start(bf16[1,256,256]{2,1,0:T(8,128)(2,1)S(1)} %get-tuple-element.700), channel_id=1, source_target_pairs={{0,4},{1,5},{2,6},{3,7},{4,0},{5,1},{6,2},{7,3},{8,12},{9,13},{10,... | collective-permute-start | bytes 393224 | tf_op jit(solution)/shard_map/cond/branch_11_fun/ppermute | solution.py:172
  106.7 26.2 %collective-permute-start.81 = (bf16[256,1024]{1,0:T(8,128)(2,1)S(1)}, bf16[256,1024]{1,0:T(8,128)(2,1)S(1)}, u32[]{:S(2)}, u32[]{:S(2)}) collective-permute-start(bf16[256,1024]{1,0:T(8,128)(2,1)S(1)} %get-tuple-element.817), channel_id=1, source_target_pairs={{0,96},{8,104},{16,112},{24,120},{32,64},{40,72},{48,80},{56,88},{... | collective-permute-start | bytes 1572872 | tf_op jit(solution)/shard_map/cond/branch_12_fun/ppermute | solution.py:183
  108.6 24.3 %collective-permute-start.82 = (bf16[256,1024]{1,0:T(8,128)(2,1)}, bf16[256,1024]{1,0:T(8,128)(2,1)}, u32[]{:S(2)}, u32[]{:S(2)}) collective-permute-start(bf16[256,1024]{1,0:T(8,128)(2,1)} %get-tuple-element.819), channel_id=1, source_target_pairs={{0,1},{1,0},{2,3},{3,2},{4,5},{5,4},{6,7},{7,6},{8,9},{9,8},{10,11... | collective-permute-start | bytes 1572872 | tf_op jit(solution)/shard_map/cond/branch_12_fun/ppermute | solution.py:159
  132.9 2.2 %copy-start.2 = (bf16[4,256,2048]{2,1,0:T(8,128)(2,1)S(1)}, bf16[4,256,2048]{2,1,0:T(8,128)(2,1)}, u32[]{:S(2)}) copy-start(bf16[4,256,2048]{2,1,0:T(8,128)(2,1)} %copy-done.1) | copy-start | bytes 12582916
  138.2 14.6 %collective-permute-start.225 = (bf16[256,1024]{1,0:T(8,128)(2,1)S(1)}, bf16[256,1024]{1,0:T(8,128)(2,1)S(1)}, u32[]{:S(2)}, u32[]{:S(2)}) collective-permute-start(bf16[256,1024]{1,0:T(8,128)(2,1)S(1)} %get-tuple-element.933.refs_0_), channel_id=1, source_target_pairs={{0,1},{1,0},{2,3},{3,2},{4,5},{5,4},{6,7},{7,6},{8,9},{9,8},{10,11... | collective-permute-start | bytes 1572872 | tf_op jit(solution)/shard_map/ppermute | solution.py:159
  141.4 11.3 %collective-permute-start.226 = (bf16[256,1024]{1,0:T(8,128)(2,1)S(1)}, bf16[256,1024]{1,0:T(8,128)(2,1)S(1)}, u32[]{:S(2)}, u32[]{:S(2)}) collective-permute-start(bf16[256,1024]{1,0:T(8,128)(2,1)S(1)} %get-tuple-element.934.refs_2_), channel_id=1, source_target_pairs={{0,1},{1,0},{2,3},{3,2},{4,5},{5,4},{6,7},{7,6},{8,9},{9,8},{10,11... | collective-permute-start | bytes 1572872 | tf_op jit(solution)/shard_map/ppermute | solution.py:159
  143.4 9.3 %collective-permute-start.227 = (bf16[2,1,256,256]{3,2,1,0:T(8,128)(2,1)S(1)}, bf16[2,1,256,256]{3,2,1,0:T(8,128)(2,1)S(1)}, u32[]{:S(2)}, u32[]{:S(2)}) collective-permute-start(bf16[2,1,256,256]{3,2,1,0:T(8,128)(2,1)S(1)} %slice.99), channel_id=1, source_target_pairs={{0,2},{1,3},{2,0},{3,1},{4,6},{5,7},{6,4},{7,5},{8,10},{9,11},{10,... | collective-permute-start | bytes 786440 | tf_op jit(solution)/shard_map/ppermute | solution.py:165
  155.8 16.8 %collective-permute-start.228 = (bf16[2,2,256,256]{3,2,1,0:T(8,128)(2,1)S(1)}, bf16[2,2,256,256]{3,2,1,0:T(8,128)(2,1)S(1)}, u32[]{:S(2)}, u32[]{:S(2)}) collective-permute-start(bf16[2,2,256,256]{3,2,1,0:T(8,128)(2,1)S(1)} %slice.117), channel_id=1, source_target_pairs={{0,2},{1,3},{2,0},{3,1},{4,6},{5,7},{6,4},{7,5},{8,10},{9,11},{10,... | collective-permute-start | bytes 1572872 | tf_op jit(solution)/shard_map/ppermute | solution.py:165
  158.0 12.7 %collective-permute-start.229 = (bf16[1,256,256]{2,1,0:T(8,128)(2,1)S(1)}, bf16[1,256,256]{2,1,0:T(8,128)(2,1)S(1)}, u32[]{:S(2)}, u32[]{:S(2)}) collective-permute-start(bf16[1,256,256]{2,1,0:T(8,128)(2,1)S(1)} %get-tuple-element.939), channel_id=1, source_target_pairs={{0,4},{1,5},{2,6},{3,7},{4,0},{5,1},{6,2},{7,3},{8,12},{9,13},{10,... | collective-permute-start | bytes 393224 | tf_op jit(solution)/shard_map/ppermute | solution.py:172
  172.7 16.1 %collective-permute-start.230 = (bf16[2,256,256]{2,1,0:T(8,128)(2,1)S(1)}, bf16[2,256,256]{2,1,0:T(8,128)(2,1)S(1)}, u32[]{:S(2)}, u32[]{:S(2)}) collective-permute-start(bf16[2,256,256]{2,1,0:T(8,128)(2,1)S(1)} %get-tuple-element.941), channel_id=1, source_target_pairs={{0,4},{1,5},{2,6},{3,7},{4,0},{5,1},{6,2},{7,3},{8,12},{9,13},{10,... | collective-permute-start | bytes 786440 | tf_op jit(solution)/shard_map/ppermute | solution.py:172

commit v4 on v3

--- a/solution.py
+++ b/solution.py
@@ -269,16 +269,9 @@
     block_2, block_0, other_1 = stage(
         2, half_2, half_0, lambda block: swap_cores(block, freq_count), block_1
     )
-    partial = next_pairs(turned, block_1, other_1)
-    block_0, block_2, partial = lax.optimization_barrier((block_0, block_2, partial))
-    step_1 = beside_step(partial, freq_count)
     other_0, other_2 = swap_cores(block_0, freq_count), swap_cores(block_2, freq_count)
-    other_0, other_2, *step_1 = lax.optimization_barrier((other_0, other_2, *step_1))
-    sum_1 = across_step(*step_1, freq_count)
-    partial = next_pairs(turned, block_0, other_0, block_2, other_2)
-    *step_02, sum_1 = lax.optimization_barrier((*beside_step(partial, freq_count), sum_1))
-    sum_02 = across_step(*step_02, freq_count)
-    return jnp.concatenate([sum_own, sum_02[:1], sum_1, sum_02[1:]])[None]
+    partial = next_pairs(turned, block_0, other_0, block_1, other_1, block_2, other_2)
+    return jnp.concatenate([sum_own, scatter(partial, freq_count)])[None]
 
 
 def solution(mesh):

time: 191 us -> 189 us (0.990)
  the two profiles are of different devices: /device:TPU:17 before, /device:TPU:13 now
where the time goes in v4:
time: 189 us
  waiting for transfers between devices  100 us (53%)
  starting transfers between devices  59.8 us (32%)
  Pallas kernels  14.2 us (8%)
  local copies, waits for them, and re-layouts  8.68 us (5%)
  between operations  4.05 us (2%)
    ppermute x7, waiting for transfers between devices, exchange(): return lax.ppermute(block, 'chan', [(i, i ^ mask) for i in range(count)])  50 us
    ppermute x7, starting transfers between devices, exchange(): return lax.ppermute(block, 'chan', [(i, i ^ mask) for i in range(count)])  29.7 us
    ppermute x2, waiting for transfers between devices, across_step(): passed = lax.ppermute(passing, 'freq', route).astype(jnp.float32)  26.3 us
    ppermute x2, waiting for transfers between devices, beside_step(): arrived = lax.ppermute(partial[half:], 'freq', route).astype(jnp.float32)  18.7 us
    ppermute x4, starting transfers between devices, swap_cores(): return lax.ppermute(block, 'freq', [(i, i ^ 1) for i in range(size)])  12.6 us
    ppermute x2, starting transfers between devices, beside_step(): arrived = lax.ppermute(partial[half:], 'freq', route).astype(jnp.float32)  7.22 us
    unnamed x11, local copies, waits for them, and re-layouts  6.13 us
    pallas_call x1, Pallas kernels, first_pair(): pl.pallas_call(functools.partial(first_kernel, width), out_shape=[jax.Sha...  5.57 us
  transfers between devices with their start and end apart: 17, of which 12 were waited for; matrix products, arithmetic and copies ran while one was open for 2% of the time, Pallas kernels for 4%

profile of v4, /device:TPU:13, one launch (start us, length us, event | category | flops | bytes accessed | tf_op | source)
XLA Modules:
  0.0 188.8 jit_solution(6509781923863605668)
XLA Ops:
  1.2 2.6 %collective-permute-start.221 = (bf16[256,512]{1,0:T(8,128)(2,1)S(1)}, bf16[256,512]{1,0:T(8,128)(2,1)S(1)}, u32[]{:S(2)}, u32[]{:S(2)}) collective-permute-start(bf16[256,512]{1,0:T(8,128)(2,1)S(1)} %get-tuple-element.937), channel_id=1, source_target_pairs={{1,0},{2,1},{3,2},{4,3},{5,4},{6,5},{7,6},{9,8},{10,9},{11,10},{12... | collective-permute-start | bytes 786440 | tf_op jit(solution)/shard_map/ppermute | solution.py:224
  3.8 3.9 %collective-permute-start.220 = (bf16[256,512]{1,0:T(8,128)(2,1)S(1)}, bf16[256,512]{1,0:T(8,128)(2,1)S(1)}, u32[]{:S(2)}, u32[]{:S(2)}) collective-permute-start(bf16[256,512]{1,0:T(8,128)(2,1)S(1)} %get-tuple-element.938), channel_id=1, source_target_pairs={{0,1},{1,2},{2,3},{3,4},{4,5},{5,6},{6,7},{8,9},{9,10},{10,11},{11... | collective-permute-start | bytes 786440 | tf_op jit(solution)/shard_map/ppermute | solution.py:223
  7.7 2.1 %collective-permute-done.221.high_ref = bf16[256,512]{1,0:T(8,128)(2,1)S(1)} collective-permute-done((bf16[256,512]{1,0:T(8,128)(2,1)S(1)}, bf16[256,512]{1,0:T(8,128)(2,1)S(1)}, u32[]{:S(2)}, u32[]{:S(2)}) %collective-permute-start.221) | collective-permute-done | bytes 262176 | tf_op jit(solution)/shard_map/ppermute | solution.py:224
  11.1 2.0 %whiten.1.mine_ref.own = bf16[256,1024]{1,0:T(8,128)(2,1)S(1)} custom-call(bf16[256,1024]{1,0:T(8,128)(2,1)S(1)} %bitcast.24, bf16[256,512]{1,0:T(8,128)(2,1)S(1)} %collective-permute-done.220.low_ref, bf16[256,512]{1,0:T(8,128)(2,1)S(1)} %collective-permute-done.221.high_ref, f32[256,128]{1,0:T(8,128)S(1)} %broadcast_in_dim.4.half_ref), custom_call_target="tpu_custom_call" | custom-call | tf_op jit(solution)/shard_map/whiten/pallas_call | solution.py:72
  13.1 9.7 %collective-permute-start.223 = (bf16[256,1024]{1,0:T(8,128)(2,1)S(1)}, bf16[256,1024]{1,0:T(8,128)(2,1)S(1)}, u32[]{:S(2)}, u32[]{:S(2)}) collective-permute-start(bf16[256,1024]{1,0:T(8,128)(2,1)S(1)} %whiten.1.mine_ref.own), channel_id=1, source_target_pairs={{0,256},{8,264},{16,272},{24,280},{32,288},{40,296},{48,304},{56,3... | collective-permute-start | bytes 1572872 | tf_op jit(solution)/shard_map/ppermute | solution.py:183
  22.8 1.9 %collective-permute-start.222 = (bf16[256,1024]{1,0:T(8,128)(2,1)S(1)}, bf16[256,1024]{1,0:T(8,128)(2,1)S(1)}, u32[]{:S(2)}, u32[]{:S(2)}) collective-permute-start(bf16[256,1024]{1,0:T(8,128)(2,1)S(1)} %whiten.1.mine_ref.own), channel_id=1, source_target_pairs={{0,1},{1,0},{2,3},{3,2},{4,5},{5,4},{6,7},{7,6},{8,9},{9,8},{10,11... | collective-permute-start | bytes 1572872 | tf_op jit(solution)/shard_map/ppermute | solution.py:159
  30.0 5.6 %first_pair.1 = (bf16[4,256,2048]{2,1,0:T(8,128)(2,1)S(1)}, bf16[4,1,256,256]{3,2,1,0:T(8,128)(2,1)S(1)}) custom-call(bf16[256,1024]{1,0:T(8,128)(2,1)S(1)} %whiten.1.mine_ref.own, bf16[256,1024]{1,0:T(8,128)(2,1)S(1)} %collective-permute-done.222.other_ref, f32[8,2048]{1,0:T(8,128)S(1)} %dynamic-slice_bitcast_fusion.table_ref), custom_call_target="tpu_custom_call" | custom-call | tf_op jit(solution)/shard_map/first_pair/pallas_call | solution.py:128
  35.6 2.0 %copy-done.1 = bf16[4,256,2048]{2,1,0:T(8,128)(2,1)} copy-done((bf16[4,256,2048]{2,1,0:T(8,128)(2,1)}, bf16[4,256,2048]{2,1,0:T(8,128)(2,1)S(1)}, u32[]{:S(2)}) %copy-start.1) | copy-done | bytes 4194328
  37.6 5.9 %collective-permute-done.223.far = bf16[256,1024]{1,0:T(8,128)(2,1)S(1)} collective-permute-done((bf16[256,1024]{1,0:T(8,128)(2,1)S(1)}, bf16[256,1024]{1,0:T(8,128)(2,1)S(1)}, u32[]{:S(2)}, u32[]{:S(2)}) %collective-permute-start.223) | collective-permute-done | bytes 524320 | tf_op jit(solution)/shard_map/ppermute | solution.py:183
  43.6 5.0 %collective-permute-start.224 = (bf16[2,1,256,256]{3,2,1,0:T(8,128)(2,1)S(1)}, bf16[2,1,256,256]{3,2,1,0:T(8,128)(2,1)S(1)}, u32[]{:S(2)}, u32[]{:S(2)}) collective-permute-start(bf16[2,1,256,256]{3,2,1,0:T(8,128)(2,1)S(1)} %slice.73), channel_id=1, source_target_pairs={{0,2},{1,3},{2,0},{3,1},{4,6},{5,7},{6,4},{7,5},{8,10},{9,11},{10,... | collective-permute-start | bytes 786440 | tf_op jit(solution)/shard_map/ppermute | solution.py:165
  50.0 17.4 %conditional.5 = ((bf16[256,1024]{1,0:T(8,128)(2,1)S(1)}, bf16[256,1024]{1,0:T(8,128)(2,1)})) conditional(s32[]{:T(128)} %clamp.10, (bf16[256,1024]{1,0:T(8,128)(2,1)S(1)}, bf16[256,1024]{1,0:T(8,128)(2,1)}) %tuple.524, (bf16[256,1024]{1,0:T(8,128)(2,1)}, bf16[256,1024]{1,0:T(8,128)(2,1)S(1)}) %tuple.525, ...), branch_computations={%region_0.1_spmd, %region_1.2_spmd, %region_2.3_spmd, %region_3.4_... | conditional | bytes 6291560 | solution.py:255
  50.1 2.1 %collective-permute-start.4 = (bf16[256,1024]{1,0:T(8,128)(2,1)S(1)}, bf16[256,1024]{1,0:T(8,128)(2,1)S(1)}, u32[]{:S(2)}, u32[]{:S(2)}) collective-permute-start(bf16[256,1024]{1,0:T(8,128)(2,1)S(1)} %get-tuple-element.603), channel_id=1, source_target_pairs={{0,32},{8,40},{16,48},{24,56},{32,0},{40,8},{48,16},{56,24},{64,96... | collective-permute-start | bytes 1572872 | tf_op jit(solution)/shard_map/cond/branch_5_fun/ppermute | solution.py:183
  52.1 2.8 %collective-permute-start.5 = (bf16[256,1024]{1,0:T(8,128)(2,1)}, bf16[256,1024]{1,0:T(8,128)(2,1)S(1)}, u32[]{:S(2)}, u32[]{:S(2)}) collective-permute-start(bf16[256,1024]{1,0:T(8,128)(2,1)} %get-tuple-element.604), channel_id=1, source_target_pairs={{0,8},{8,0},{16,24},{24,16},{32,40},{40,32},{48,56},{56,48},{64,72... | collective-permute-start | bytes 1572872 | tf_op jit(solution)/shard_map/cond/branch_5_fun/ppermute | solution.py:183
  55.0 9.6 %collective-permute-done.4 = bf16[256,1024]{1,0:T(8,128)(2,1)S(1)} collective-permute-done((bf16[256,1024]{1,0:T(8,128)(2,1)S(1)}, bf16[256,1024]{1,0:T(8,128)(2,1)S(1)}, u32[]{:S(2)}, u32[]{:S(2)}) %collective-permute-start.4) | collective-permute-done | bytes 524320 | tf_op jit(solution)/shard_map/cond/branch_5_fun/ppermute | solution.py:183
  64.6 1.9 %collective-permute-done.5 = bf16[256,1024]{1,0:T(8,128)(2,1)S(1)} collective-permute-done((bf16[256,1024]{1,0:T(8,128)(2,1)}, bf16[256,1024]{1,0:T(8,128)(2,1)S(1)}, u32[]{:S(2)}, u32[]{:S(2)}) %collective-permute-start.5) | collective-permute-done | bytes 524320 | tf_op jit(solution)/shard_map/cond/branch_5_fun/ppermute | solution.py:183
  67.5 39.5 %conditional.8 = (bf16[256,1024]{1,0:T(8,128)(2,1)}, bf16[256,1024]{1,0:T(8,128)(2,1)S(1)}, f32[1,256,256]{2,1,0:T(8,128)S(1)}, f32[1,256,256]{2,1,0:T(8,128)S(1)}) conditional(s32[]{:T(128)} %clamp.9, (bf16[1,256,256]{2,1,0:T(8,128)(2,1)S(1)}, bf16[256,1024]{1,0:T(8,128)(2,1)}, bf16[256,1024]{1,0:T(8,128)(2,1)S(1)}, ...), branch_computations={%region_32.33_spmd, %region_33.34_spmd, %region_34.35_spmd, %regio... | conditional | flops 65536 | bytes 7209112
  67.5 4.3 %collective-permute-start.89 = (bf16[256,1024]{1,0:T(8,128)(2,1)}, bf16[256,1024]{1,0:T(8,128)(2,1)S(1)}, u32[]{:S(2)}, u32[]{:S(2)}) collective-permute-start(bf16[256,1024]{1,0:T(8,128)(2,1)} %get-tuple-element.717), channel_id=1, source_target_pairs={{0,96},{8,104},{16,112},{24,120},{32,64},{40,72},{48,80},{56,88},{... | collective-permute-start | bytes 1572872 | tf_op jit(solution)/shard_map/cond/branch_15_fun/ppermute | solution.py:183
  71.9 2.2 %collective-permute-start.90 = (bf16[256,1024]{1,0:T(8,128)(2,1)S(1)}, bf16[256,1024]{1,0:T(8,128)(2,1)S(1)}, u32[]{:S(2)}, u32[]{:S(2)}) collective-permute-start(bf16[256,1024]{1,0:T(8,128)(2,1)S(1)} %get-tuple-element.718), channel_id=1, source_target_pairs={{0,24},{8,16},{16,8},{24,0},{32,56},{40,48},{48,40},{56,32},{64,88... | collective-permute-start | bytes 1572872 | tf_op jit(solution)/shard_map/cond/branch_15_fun/ppermute | solution.py:183
  76.0 6.1 %collective-permute-done.91 = bf16[1,256,256]{2,1,0:T(8,128)(2,1)S(1)} collective-permute-done((bf16[1,256,256]{2,1,0:T(8,128)(2,1)S(1)}, bf16[1,256,256]{2,1,0:T(8,128)(2,1)S(1)}, u32[]{:S(2)}, u32[]{:S(2)}) %collective-permute-start.91) | collective-permute-done | bytes 131104 | tf_op jit(solution)/shard_map/cond/branch_15_fun/ppermute | solution.py:172
  82.1 23.8 %collective-permute-done.89 = bf16[256,1024]{1,0:T(8,128)(2,1)S(1)} collective-permute-done((bf16[256,1024]{1,0:T(8,128)(2,1)}, bf16[256,1024]{1,0:T(8,128)(2,1)S(1)}, u32[]{:S(2)}, u32[]{:S(2)}) %collective-permute-start.89) | collective-permute-done | bytes 524320 | tf_op jit(solution)/shard_map/cond/branch_15_fun/ppermute | solution.py:183
  106.9 21.5 %conditional.7 = (bf16[256,1024]{1,0:T(8,128)(2,1)S(1)}, bf16[256,1024]{1,0:T(8,128)(2,1)S(1)}, bf16[256,1024]{1,0:T(8,128)(2,1)}) conditional(s32[]{:T(128)} %clamp.11, (bf16[256,1024]{1,0:T(8,128)(2,1)}, bf16[256,1024]{1,0:T(8,128)(2,1)S(1)}, bf16[256,1024]{1,0:T(8,128)(2,1)S(1)}) %tuple.531, ...), branch_computations={%region_64.65_spmd, %region_65.66_spmd, %region_66.67_spmd, %regio... | conditional | bytes 8388752 | solution.py:255
  107.0 6.4 %collective-permute-start.181 = (bf16[256,1024]{1,0:T(8,128)(2,1)S(1)}, bf16[256,1024]{1,0:T(8,128)(2,1)S(1)}, u32[]{:S(2)}, u32[]{:S(2)}) collective-permute-start(bf16[256,1024]{1,0:T(8,128)(2,1)S(1)} %get-tuple-element.839), channel_id=1, source_target_pairs={{0,128},{8,136},{16,144},{24,152},{32,160},{40,168},{48,176},{56,1... | collective-permute-start | bytes 1572872 | tf_op jit(solution)/shard_map/cond/branch_18_fun/ppermute | solution.py:183
  113.4 2.1 %collective-permute-start.182 = (bf16[256,1024]{1,0:T(8,128)(2,1)S(1)}, bf16[256,1024]{1,0:T(8,128)(2,1)S(1)}, u32[]{:S(2)}, u32[]{:S(2)}) collective-permute-start(bf16[256,1024]{1,0:T(8,128)(2,1)S(1)} %get-tuple-element.840), channel_id=1, source_target_pairs={{0,16},{8,24},{16,0},{24,8},{32,48},{40,56},{48,32},{56,40},{64,80... | collective-permute-start | bytes 1572872 | tf_op jit(solution)/shard_map/cond/branch_18_fun/ppermute | solution.py:183
  115.6 4.0 %collective-permute-start.183 = (bf16[256,1024]{1,0:T(8,128)(2,1)}, bf16[256,1024]{1,0:T(8,128)(2,1)}, u32[]{:S(2)}, u32[]{:S(2)}) collective-permute-start(bf16[256,1024]{1,0:T(8,128)(2,1)} %get-tuple-element.841), channel_id=1, source_target_pairs={{0,1},{1,0},{2,3},{3,2},{4,5},{5,4},{6,7},{7,6},{8,9},{9,8},{10,11... | collective-permute-start | bytes 1572872 | tf_op jit(solution)/shard_map/cond/branch_18_fun/ppermute | solution.py:159
  119.6 5.1 %collective-permute-done.181 = bf16[256,1024]{1,0:T(8,128)(2,1)S(1)} collective-permute-done((bf16[256,1024]{1,0:T(8,128)(2,1)S(1)}, bf16[256,1024]{1,0:T(8,128)(2,1)S(1)}, u32[]{:S(2)}, u32[]{:S(2)}) %collective-permute-start.181) | collective-permute-done | bytes 524320 | tf_op jit(solution)/shard_map/cond/branch_18_fun/ppermute | solution.py:183
  124.7 3.6 %collective-permute-done.182 = bf16[256,1024]{1,0:T(8,128)(2,1)S(1)} collective-permute-done((bf16[256,1024]{1,0:T(8,128)(2,1)S(1)}, bf16[256,1024]{1,0:T(8,128)(2,1)S(1)}, u32[]{:S(2)}, u32[]{:S(2)}) %collective-permute-start.182) | collective-permute-done | bytes 524320 | tf_op jit(solution)/shard_map/cond/branch_18_fun/ppermute | solution.py:183
  128.4 4.7 %collective-permute-start.225 = (bf16[256,1024]{1,0:T(8,128)(2,1)S(1)}, bf16[256,1024]{1,0:T(8,128)(2,1)S(1)}, u32[]{:S(2)}, u32[]{:S(2)}) collective-permute-start(bf16[256,1024]{1,0:T(8,128)(2,1)S(1)} %get-tuple-element.926.refs_0_), channel_id=1, source_target_pairs={{0,1},{1,0},{2,3},{3,2},{4,5},{5,4},{6,7},{7,6},{8,9},{9,8},{10,11... | collective-permute-start | bytes 1572872 | tf_op jit(solution)/shard_map/ppermute | solution.py:159
  136.9 2.2 %copy-done.2 = bf16[4,256,2048]{2,1,0:T(8,128)(2,1)S(1)} copy-done((bf16[4,256,2048]{2,1,0:T(8,128)(2,1)S(1)}, bf16[4,256,2048]{2,1,0:T(8,128)(2,1)}, u32[]{:S(2)}) %copy-start.2) | copy-done | bytes 4194328
  139.1 5.2 %next_pairs.1 = bf16[4,3,256,256]{3,2,1,0:T(8,128)(2,1)S(1)} custom-call(bf16[4,256,2048]{2,1,0:T(8,128)(2,1)S(1)} %copy-done.2, bf16[256,1024]{1,0:T(8,128)(2,1)S(1)} %get-tuple-element.926.refs_0_, bf16[256,1024]{1,0:T(8,128)(2,1)S(1)} %collective-permute-done.225.refs_1_, bf16[256,1024]{1,0:T(8,128)(2,1)} %get-tuple-element.923.refs_2_, ...), custom_call_target="tpu_custom_call" | custom-call | flops 6442450944 | bytes 4194304 | tf_op jit(solution)/shard_map/next_pairs/pallas_call | solution.py:145
  144.4 2.2 %collective-permute-start.227 = (bf16[2,3,256,256]{3,2,1,0:T(8,128)(2,1)S(1)}, bf16[2,3,256,256]{3,2,1,0:T(8,128)(2,1)S(1)}, u32[]{:S(2)}, u32[]{:S(2)}) collective-permute-start(bf16[2,3,256,256]{3,2,1,0:T(8,128)(2,1)S(1)} %slice.87), channel_id=1, source_target_pairs={{0,2},{1,3},{2,0},{3,1},{4,6},{5,7},{6,4},{7,5},{8,10},{9,11},{10,... | collective-permute-start | bytes 2359304 | tf_op jit(solution)/shard_map/ppermute | solution.py:165
  146.7 18.7 %collective-permute-done.227 = bf16[2,3,256,256]{3,2,1,0:T(8,128)(2,1)S(1)} collective-permute-done((bf16[2,3,256,256]{3,2,1,0:T(8,128)(2,1)S(1)}, bf16[2,3,256,256]{3,2,1,0:T(8,128)(2,1)S(1)}, u32[]{:S(2)}, u32[]{:S(2)}) %collective-permute-start.227) | collective-permute-done | bytes 786464 | tf_op jit(solution)/shard_map/ppermute | solution.py:165
  167.6 20.2 %collective-permute-done.228 = bf16[3,256,256]{2,1,0:T(8,128)(2,1)S(1)} collective-permute-done((bf16[3,256,256]{2,1,0:T(8,128)(2,1)S(1)}, bf16[3,256,256]{2,1,0:T(8,128)(2,1)S(1)}, u32[]{:S(2)}, u32[]{:S(2)}) %collective-permute-start.228) | collective-permute-done | bytes 393248 | tf_op jit(solution)/shard_map/ppermute | solution.py:172
  (40 shorter events, 16.1 us)
Async XLA Ops:
  0.0 7.7 %copy-start.3 = (s32[256]{0:T(256)S(1)}, s32[256]{0:T(256)}, u32[]{:S(2)}) copy-start(s32[256]{0:T(256)} %param.101) | copy-start | bytes 3076
  1.2 23.6 %copy-start = (s32[3,64]{1,0:T(4,128)S(1)}, s32[3,64]{1,0:T(4,128)}, u32[]{:S(2)}) copy-start(s32[3,64]{1,0:T(4,128)} %mask_ref.1) | copy-start | bytes 2308
  1.2 8.6 %collective-permute-start.221 = (bf16[256,512]{1,0:T(8,128)(2,1)S(1)}, bf16[256,512]{1,0:T(8,128)(2,1)S(1)}, u32[]{:S(2)}, u32[]{:S(2)}) collective-permute-start(bf16[256,512]{1,0:T(8,128)(2,1)S(1)} %get-tuple-element.937), channel_id=1, source_target_pairs={{1,0},{2,1},{3,2},{4,3},{5,4},{6,5},{7,6},{9,8},{10,9},{11,10},{12... | collective-permute-start | bytes 786440 | tf_op jit(solution)/shard_map/ppermute | solution.py:224
  3.8 7.2 %collective-permute-start.220 = (bf16[256,512]{1,0:T(8,128)(2,1)S(1)}, bf16[256,512]{1,0:T(8,128)(2,1)S(1)}, u32[]{:S(2)}, u32[]{:S(2)}) collective-permute-start(bf16[256,512]{1,0:T(8,128)(2,1)S(1)} %get-tuple-element.938), channel_id=1, source_target_pairs={{0,1},{1,2},{2,3},{3,4},{4,5},{5,6},{6,7},{8,9},{9,10},{10,11},{11... | collective-permute-start | bytes 786440 | tf_op jit(solution)/shard_map/ppermute | solution.py:223
  13.1 30.4 %collective-permute-start.223 = (bf16[256,1024]{1,0:T(8,128)(2,1)S(1)}, bf16[256,1024]{1,0:T(8,128)(2,1)S(1)}, u32[]{:S(2)}, u32[]{:S(2)}) collective-permute-start(bf16[256,1024]{1,0:T(8,128)(2,1)S(1)} %whiten.1.mine_ref.own), channel_id=1, source_target_pairs={{0,256},{8,264},{16,272},{24,280},{32,288},{40,296},{48,304},{56,3... | collective-permute-start | bytes 1572872 | tf_op jit(solution)/shard_map/ppermute | solution.py:183
  22.8 7.2 %collective-permute-start.222 = (bf16[256,1024]{1,0:T(8,128)(2,1)S(1)}, bf16[256,1024]{1,0:T(8,128)(2,1)S(1)}, u32[]{:S(2)}, u32[]{:S(2)}) collective-permute-start(bf16[256,1024]{1,0:T(8,128)(2,1)S(1)} %whiten.1.mine_ref.own), channel_id=1, source_target_pairs={{0,1},{1,0},{2,3},{3,2},{4,5},{5,4},{6,7},{7,6},{8,9},{9,8},{10,11... | collective-permute-start | bytes 1572872 | tf_op jit(solution)/shard_map/ppermute | solution.py:159
  35.6 2.0 %copy-start.1 = (bf16[4,256,2048]{2,1,0:T(8,128)(2,1)}, bf16[4,256,2048]{2,1,0:T(8,128)(2,1)S(1)}, u32[]{:S(2)}) copy-start(bf16[4,256,2048]{2,1,0:T(8,128)(2,1)S(1)} %get-tuple-element.921.turned_ref) | copy-start | bytes 12582916
  43.6 23.8 %collective-permute-start.224 = (bf16[2,1,256,256]{3,2,1,0:T(8,128)(2,1)S(1)}, bf16[2,1,256,256]{3,2,1,0:T(8,128)(2,1)S(1)}, u32[]{:S(2)}, u32[]{:S(2)}) collective-permute-start(bf16[2,1,256,256]{3,2,1,0:T(8,128)(2,1)S(1)} %slice.73), channel_id=1, source_target_pairs={{0,2},{1,3},{2,0},{3,1},{4,6},{5,7},{6,4},{7,5},{8,10},{9,11},{10,... | collective-permute-start | bytes 786440 | tf_op jit(solution)/shard_map/ppermute | solution.py:165
  50.1 14.5 %collective-permute-start.4 = (bf16[256,1024]{1,0:T(8,128)(2,1)S(1)}, bf16[256,1024]{1,0:T(8,128)(2,1)S(1)}, u32[]{:S(2)}, u32[]{:S(2)}) collective-permute-start(bf16[256,1024]{1,0:T(8,128)(2,1)S(1)} %get-tuple-element.603), channel_id=1, source_target_pairs={{0,32},{8,40},{16,48},{24,56},{32,0},{40,8},{48,16},{56,24},{64,96... | collective-permute-start | bytes 1572872 | tf_op jit(solution)/shard_map/cond/branch_5_fun/ppermute | solution.py:183
  52.1 14.4 %collective-permute-start.5 = (bf16[256,1024]{1,0:T(8,128)(2,1)}, bf16[256,1024]{1,0:T(8,128)(2,1)S(1)}, u32[]{:S(2)}, u32[]{:S(2)}) collective-permute-start(bf16[256,1024]{1,0:T(8,128)(2,1)} %get-tuple-element.604), channel_id=1, source_target_pairs={{0,8},{8,0},{16,24},{24,16},{32,40},{40,32},{48,56},{56,48},{64,72... | collective-permute-start | bytes 1572872 | tf_op jit(solution)/shard_map/cond/branch_5_fun/ppermute | solution.py:183
  67.5 38.4 %collective-permute-start.89 = (bf16[256,1024]{1,0:T(8,128)(2,1)}, bf16[256,1024]{1,0:T(8,128)(2,1)S(1)}, u32[]{:S(2)}, u32[]{:S(2)}) collective-permute-start(bf16[256,1024]{1,0:T(8,128)(2,1)} %get-tuple-element.717), channel_id=1, source_target_pairs={{0,96},{8,104},{16,112},{24,120},{32,64},{40,72},{48,80},{56,88},{... | collective-permute-start | bytes 1572872 | tf_op jit(solution)/shard_map/cond/branch_15_fun/ppermute | solution.py:183
  71.9 34.8 %collective-permute-start.90 = (bf16[256,1024]{1,0:T(8,128)(2,1)S(1)}, bf16[256,1024]{1,0:T(8,128)(2,1)S(1)}, u32[]{:S(2)}, u32[]{:S(2)}) collective-permute-start(bf16[256,1024]{1,0:T(8,128)(2,1)S(1)} %get-tuple-element.718), channel_id=1, source_target_pairs={{0,24},{8,16},{16,8},{24,0},{32,56},{40,48},{48,40},{56,32},{64,88... | collective-permute-start | bytes 1572872 | tf_op jit(solution)/shard_map/cond/branch_15_fun/ppermute | solution.py:183
  74.0 8.0 %collective-permute-start.91 = (bf16[1,256,256]{2,1,0:T(8,128)(2,1)S(1)}, bf16[1,256,256]{2,1,0:T(8,128)(2,1)S(1)}, u32[]{:S(2)}, u32[]{:S(2)}) collective-permute-start(bf16[1,256,256]{2,1,0:T(8,128)(2,1)S(1)} %get-tuple-element.720), channel_id=1, source_target_pairs={{0,4},{1,5},{2,6},{3,7},{4,0},{5,1},{6,2},{7,3},{8,12},{9,13},{10,... | collective-permute-start | bytes 393224 | tf_op jit(solution)/shard_map/cond/branch_15_fun/ppermute | solution.py:172
  107.0 17.7 %collective-permute-start.181 = (bf16[256,1024]{1,0:T(8,128)(2,1)S(1)}, bf16[256,1024]{1,0:T(8,128)(2,1)S(1)}, u32[]{:S(2)}, u32[]{:S(2)}) collective-permute-start(bf16[256,1024]{1,0:T(8,128)(2,1)S(1)} %get-tuple-element.839), channel_id=1, source_target_pairs={{0,128},{8,136},{16,144},{24,152},{32,160},{40,168},{48,176},{56,1... | collective-permute-start | bytes 1572872 | tf_op jit(solution)/shard_map/cond/branch_18_fun/ppermute | solution.py:183
  113.4 15.0 %collective-permute-start.182 = (bf16[256,1024]{1,0:T(8,128)(2,1)S(1)}, bf16[256,1024]{1,0:T(8,128)(2,1)S(1)}, u32[]{:S(2)}, u32[]{:S(2)}) collective-permute-start(bf16[256,1024]{1,0:T(8,128)(2,1)S(1)} %get-tuple-element.840), channel_id=1, source_target_pairs={{0,16},{8,24},{16,0},{24,8},{32,48},{40,56},{48,32},{56,40},{64,80... | collective-permute-start | bytes 1572872 | tf_op jit(solution)/shard_map/cond/branch_18_fun/ppermute | solution.py:183
  115.6 12.9 %collective-permute-start.183 = (bf16[256,1024]{1,0:T(8,128)(2,1)}, bf16[256,1024]{1,0:T(8,128)(2,1)}, u32[]{:S(2)}, u32[]{:S(2)}) collective-permute-start(bf16[256,1024]{1,0:T(8,128)(2,1)} %get-tuple-element.841), channel_id=1, source_target_pairs={{0,1},{1,0},{2,3},{3,2},{4,5},{5,4},{6,7},{7,6},{8,9},{9,8},{10,11... | collective-permute-start | bytes 1572872 | tf_op jit(solution)/shard_map/cond/branch_18_fun/ppermute | solution.py:159
  128.4 6.6 %collective-permute-start.225 = (bf16[256,1024]{1,0:T(8,128)(2,1)S(1)}, bf16[256,1024]{1,0:T(8,128)(2,1)S(1)}, u32[]{:S(2)}, u32[]{:S(2)}) collective-permute-start(bf16[256,1024]{1,0:T(8,128)(2,1)S(1)} %get-tuple-element.926.refs_0_), channel_id=1, source_target_pairs={{0,1},{1,0},{2,3},{3,2},{4,5},{5,4},{6,7},{7,6},{8,9},{9,8},{10,11... | collective-permute-start | bytes 1572872 | tf_op jit(solution)/shard_map/ppermute | solution.py:159
  133.1 3.8 %collective-permute-start.226 = (bf16[256,1024]{1,0:T(8,128)(2,1)S(1)}, bf16[256,1024]{1,0:T(8,128)(2,1)S(1)}, u32[]{:S(2)}, u32[]{:S(2)}) collective-permute-start(bf16[256,1024]{1,0:T(8,128)(2,1)S(1)} %get-tuple-element.928.refs_4_), channel_id=1, source_target_pairs={{0,1},{1,0},{2,3},{3,2},{4,5},{5,4},{6,7},{7,6},{8,9},{9,8},{10,11... | collective-permute-start | bytes 1572872 | tf_op jit(solution)/shard_map/ppermute | solution.py:159
  136.9 2.2 %copy-start.2 = (bf16[4,256,2048]{2,1,0:T(8,128)(2,1)S(1)}, bf16[4,256,2048]{2,1,0:T(8,128)(2,1)}, u32[]{:S(2)}) copy-start(bf16[4,256,2048]{2,1,0:T(8,128)(2,1)} %copy-done.1) | copy-start | bytes 12582916
  144.4 20.9 %collective-permute-start.227 = (bf16[2,3,256,256]{3,2,1,0:T(8,128)(2,1)S(1)}, bf16[2,3,256,256]{3,2,1,0:T(8,128)(2,1)S(1)}, u32[]{:S(2)}, u32[]{:S(2)}) collective-permute-start(bf16[2,3,256,256]{3,2,1,0:T(8,128)(2,1)S(1)} %slice.87), channel_id=1, source_target_pairs={{0,2},{1,3},{2,0},{3,1},{4,6},{5,7},{6,4},{7,5},{8,10},{9,11},{10,... | collective-permute-start | bytes 2359304 | tf_op jit(solution)/shard_map/ppermute | solution.py:165
  165.6 22.2 %collective-permute-start.228 = (bf16[3,256,256]{2,1,0:T(8,128)(2,1)S(1)}, bf16[3,256,256]{2,1,0:T(8,128)(2,1)S(1)}, u32[]{:S(2)}, u32[]{:S(2)}) collective-permute-start(bf16[3,256,256]{2,1,0:T(8,128)(2,1)S(1)} %fusion.4), channel_id=1, source_target_pairs={{0,4},{1,5},{2,6},{3,7},{4,0},{5,1},{6,2},{7,3},{8,12},{9,13},{10,... | collective-permute-start | bytes 1179656 | tf_op jit(solution)/shard_map/ppermute | solution.py:172

commit v5 on v4

--- a/solution.py
+++ b/solution.py
@@ -174,7 +174,11 @@
 
 
 def scatter(partial, size):
-    return across_step(*beside_step(partial, size), size)
+    total = partial[0].astype(jnp.float32)
+    for k in range(1, partial.shape[0]):
+        route = [(i, i ^ (ORDER[k] * CORES)) for i in range(size)]
+        total = total + lax.ppermute(partial[k], "freq", route).astype(jnp.float32)
+    return total.astype(jnp.bfloat16)
 
 
 def exchange(block, mask, count):

time: 189 us -> 181 us (0.958)
  the two profiles are of different devices: /device:TPU:13 before, /device:TPU:75 now
where the time goes in v5:
time: 181 us; the launch traced here: 180 us
  waiting for transfers between devices  93.2 us (51%)
  starting transfers between devices  59 us (33%)
  Pallas kernels  14.2 us (8%)
  local copies, waits for them, and re-layouts  7.88 us (4%)
  between operations  4.04 us (2%)
    ppermute x5, waiting for transfers between devices, exchange(): return lax.ppermute(block, 'chan', [(i, i ^ mask) for i in range(count)])  52.8 us
    ppermute x3, waiting for transfers between devices, scatter(): total = total + lax.ppermute(partial[k], 'freq', route).astype(jnp.float32)  29.7 us
    ppermute x5, starting transfers between devices, exchange(): return lax.ppermute(block, 'chan', [(i, i ^ mask) for i in range(count)])  25.2 us
    ppermute x4, starting transfers between devices, swap_cores(): return lax.ppermute(block, 'freq', [(i, i ^ 1) for i in range(size)])  13.4 us
    ppermute x3, starting transfers between devices, scatter(): total = total + lax.ppermute(partial[k], 'freq', route).astype(jnp.float32)  9.27 us
    unnamed x11, local copies, waits for them, and re-layouts  6.12 us
    ppermute x1, waiting for transfers between devices, across_step(): passed = lax.ppermute(passing, 'freq', route).astype(jnp.float32)  5.58 us
    pallas_call x1, Pallas kernels, first_pair(): pl.pallas_call(functools.partial(first_kernel, width), out_shape=[jax.Sha...  5.57 us
  transfers between devices with their start and end apart: 16, of which 11 were waited for; matrix products, arithmetic and copies ran while one was open for 1% of the time, Pallas kernels for 4%

profile of v5, /device:TPU:75, one launch (start us, length us, event | category | flops | bytes accessed | tf_op | source)
XLA Modules:
  0.0 180.0 jit_solution(11907762829054289854)
XLA Ops:
  1.2 2.6 %collective-permute-start.221 = (bf16[256,512]{1,0:T(8,128)(2,1)S(1)}, bf16[256,512]{1,0:T(8,128)(2,1)S(1)}, u32[]{:S(2)}, u32[]{:S(2)}) collective-permute-start(bf16[256,512]{1,0:T(8,128)(2,1)S(1)} %get-tuple-element.940), channel_id=1, source_target_pairs={{1,0},{2,1},{3,2},{4,3},{5,4},{6,5},{7,6},{9,8},{10,9},{11,10},{12... | collective-permute-start | bytes 786440 | tf_op jit(solution)/shard_map/ppermute | solution.py:228
  3.8 3.9 %collective-permute-start.220 = (bf16[256,512]{1,0:T(8,128)(2,1)S(1)}, bf16[256,512]{1,0:T(8,128)(2,1)S(1)}, u32[]{:S(2)}, u32[]{:S(2)}) collective-permute-start(bf16[256,512]{1,0:T(8,128)(2,1)S(1)} %get-tuple-element.941), channel_id=1, source_target_pairs={{0,1},{1,2},{2,3},{3,4},{4,5},{5,6},{6,7},{8,9},{9,10},{10,11},{11... | collective-permute-start | bytes 786440 | tf_op jit(solution)/shard_map/ppermute | solution.py:227
  7.7 2.4 %collective-permute-done.221.high_ref = bf16[256,512]{1,0:T(8,128)(2,1)S(1)} collective-permute-done((bf16[256,512]{1,0:T(8,128)(2,1)S(1)}, bf16[256,512]{1,0:T(8,128)(2,1)S(1)}, u32[]{:S(2)}, u32[]{:S(2)}) %collective-permute-start.221) | collective-permute-done | bytes 262176 | tf_op jit(solution)/shard_map/ppermute | solution.py:228
  11.1 2.0 %whiten.1.mine_ref.own = bf16[256,1024]{1,0:T(8,128)(2,1)S(1)} custom-call(bf16[256,1024]{1,0:T(8,128)(2,1)S(1)} %bitcast.27, bf16[256,512]{1,0:T(8,128)(2,1)S(1)} %collective-permute-done.220.low_ref, bf16[256,512]{1,0:T(8,128)(2,1)S(1)} %collective-permute-done.221.high_ref, f32[256,128]{1,0:T(8,128)S(1)} %broadcast_in_dim.4.half_ref), custom_call_target="tpu_custom_call" | custom-call | tf_op jit(solution)/shard_map/whiten/pallas_call | solution.py:72
  13.1 8.8 %collective-permute-start.223 = (bf16[256,1024]{1,0:T(8,128)(2,1)S(1)}, bf16[256,1024]{1,0:T(8,128)(2,1)S(1)}, u32[]{:S(2)}, u32[]{:S(2)}) collective-permute-start(bf16[256,1024]{1,0:T(8,128)(2,1)S(1)} %whiten.1.mine_ref.own), channel_id=1, source_target_pairs={{0,256},{8,264},{16,272},{24,280},{32,288},{40,296},{48,304},{56,3... | collective-permute-start | bytes 1572872 | tf_op jit(solution)/shard_map/ppermute | solution.py:187
  21.9 3.6 %collective-permute-start.222 = (bf16[256,1024]{1,0:T(8,128)(2,1)S(1)}, bf16[256,1024]{1,0:T(8,128)(2,1)S(1)}, u32[]{:S(2)}, u32[]{:S(2)}) collective-permute-start(bf16[256,1024]{1,0:T(8,128)(2,1)S(1)} %whiten.1.mine_ref.own), channel_id=1, source_target_pairs={{0,1},{1,0},{2,3},{3,2},{4,5},{5,4},{6,7},{7,6},{8,9},{9,8},{10,11... | collective-permute-start | bytes 1572872 | tf_op jit(solution)/shard_map/ppermute | solution.py:159
  30.8 5.6 %first_pair.1 = (bf16[4,256,2048]{2,1,0:T(8,128)(2,1)S(1)}, bf16[4,1,256,256]{3,2,1,0:T(8,128)(2,1)S(1)}) custom-call(bf16[256,1024]{1,0:T(8,128)(2,1)S(1)} %whiten.1.mine_ref.own, bf16[256,1024]{1,0:T(8,128)(2,1)S(1)} %collective-permute-done.222.other_ref, f32[8,2048]{1,0:T(8,128)S(1)} %dynamic-slice_bitcast_fusion.table_ref), custom_call_target="tpu_custom_call" | custom-call | tf_op jit(solution)/shard_map/first_pair/pallas_call | solution.py:128
  36.4 2.0 %copy-done.1 = bf16[4,256,2048]{2,1,0:T(8,128)(2,1)} copy-done((bf16[4,256,2048]{2,1,0:T(8,128)(2,1)}, bf16[4,256,2048]{2,1,0:T(8,128)(2,1)S(1)}, u32[]{:S(2)}) %copy-start.1) | copy-done | bytes 4194328
  38.3 6.2 %collective-permute-done.223.far = bf16[256,1024]{1,0:T(8,128)(2,1)S(1)} collective-permute-done((bf16[256,1024]{1,0:T(8,128)(2,1)S(1)}, bf16[256,1024]{1,0:T(8,128)(2,1)S(1)}, u32[]{:S(2)}, u32[]{:S(2)}) %collective-permute-start.223) | collective-permute-done | bytes 524320 | tf_op jit(solution)/shard_map/ppermute | solution.py:187
  44.5 1.9 %collective-permute-start.224 = (bf16[2,1,256,256]{3,2,1,0:T(8,128)(2,1)S(1)}, bf16[2,1,256,256]{3,2,1,0:T(8,128)(2,1)S(1)}, u32[]{:S(2)}, u32[]{:S(2)}) collective-permute-start(bf16[2,1,256,256]{3,2,1,0:T(8,128)(2,1)S(1)} %slice.70), channel_id=1, source_target_pairs={{0,2},{1,3},{2,0},{3,1},{4,6},{5,7},{6,4},{7,5},{8,10},{9,11},{10,... | collective-permute-start | bytes 786440 | tf_op jit(solution)/shard_map/ppermute | solution.py:165
  47.9 28.9 %conditional.5 = ((bf16[256,1024]{1,0:T(8,128)(2,1)S(1)}, bf16[256,1024]{1,0:T(8,128)(2,1)})) conditional(s32[]{:T(128)} %clamp.10, (bf16[256,1024]{1,0:T(8,128)(2,1)S(1)}, bf16[256,1024]{1,0:T(8,128)(2,1)}) %tuple.524, (bf16[256,1024]{1,0:T(8,128)(2,1)}, bf16[256,1024]{1,0:T(8,128)(2,1)S(1)}) %tuple.525, ...), branch_computations={%region_0.1_spmd, %region_1.2_spmd, %region_2.3_spmd, %region_3.4_... | conditional | bytes 6291560 | solution.py:259
  48.0 5.0 %collective-permute-start.38 = (bf16[256,1024]{1,0:T(8,128)(2,1)S(1)}, bf16[256,1024]{1,0:T(8,128)(2,1)S(1)}, u32[]{:S(2)}, u32[]{:S(2)}) collective-permute-start(bf16[256,1024]{1,0:T(8,128)(2,1)S(1)} %get-tuple-element.641), channel_id=1, source_target_pairs={{0,192},{8,200},{16,208},{24,216},{32,224},{40,232},{48,240},{56,2... | collective-permute-start | bytes 1572872 | tf_op jit(solution)/shard_map/cond/branch_24_fun/ppermute | solution.py:187
  53.0 23.8 %collective-permute-done.38 = bf16[256,1024]{1,0:T(8,128)(2,1)S(1)} collective-permute-done((bf16[256,1024]{1,0:T(8,128)(2,1)S(1)}, bf16[256,1024]{1,0:T(8,128)(2,1)S(1)}, u32[]{:S(2)}, u32[]{:S(2)}) %collective-permute-start.38) | collective-permute-done | bytes 524320 | tf_op jit(solution)/shard_map/cond/branch_24_fun/ppermute | solution.py:187
  76.9 18.2 %conditional.8 = (bf16[256,1024]{1,0:T(8,128)(2,1)}, bf16[256,1024]{1,0:T(8,128)(2,1)S(1)}, f32[1,256,256]{2,1,0:T(8,128)S(1)}, f32[1,256,256]{2,1,0:T(8,128)S(1)}) conditional(s32[]{:T(128)} %clamp.9, (bf16[1,256,256]{2,1,0:T(8,128)(2,1)S(1)}, bf16[256,1024]{1,0:T(8,128)(2,1)}, bf16[256,1024]{1,0:T(8,128)(2,1)S(1)}, ...), branch_computations={%region_32.33_spmd, %region_33.34_spmd, %region_34.35_spmd, %regio... | conditional | flops 65536 | bytes 7209112
  77.0 1.9 %collective-permute-start.64 = (bf16[256,1024]{1,0:T(8,128)(2,1)}, bf16[256,1024]{1,0:T(8,128)(2,1)S(1)}, u32[]{:S(2)}, u32[]{:S(2)}) collective-permute-start(bf16[256,1024]{1,0:T(8,128)(2,1)} %get-tuple-element.681), channel_id=1, source_target_pairs={{0,32},{8,40},{16,48},{24,56},{32,0},{40,8},{48,16},{56,24},{64,96... | collective-permute-start | bytes 1572872 | tf_op jit(solution)/shard_map/cond/branch_6_fun/ppermute | solution.py:187
  78.9 3.8 %collective-permute-start.65 = (bf16[256,1024]{1,0:T(8,128)(2,1)S(1)}, bf16[256,1024]{1,0:T(8,128)(2,1)S(1)}, u32[]{:S(2)}, u32[]{:S(2)}) collective-permute-start(bf16[256,1024]{1,0:T(8,128)(2,1)S(1)} %get-tuple-element.682), channel_id=1, source_target_pairs={{0,16},{8,24},{16,0},{24,8},{32,48},{40,56},{48,32},{56,40},{64,80... | collective-permute-start | bytes 1572872 | tf_op jit(solution)/shard_map/cond/branch_6_fun/ppermute | solution.py:187
  82.7 2.7 %collective-permute-start.66 = (bf16[1,256,256]{2,1,0:T(8,128)(2,1)S(1)}, bf16[1,256,256]{2,1,0:T(8,128)(2,1)S(1)}, u32[]{:S(2)}, u32[]{:S(2)}) collective-permute-start(bf16[1,256,256]{2,1,0:T(8,128)(2,1)S(1)} %get-tuple-element.684), channel_id=1, source_target_pairs={{0,4},{1,5},{2,6},{3,7},{4,0},{5,1},{6,2},{7,3},{8,12},{9,13},{10,... | collective-permute-start | bytes 393224 | tf_op jit(solution)/shard_map/cond/branch_6_fun/ppermute | solution.py:172
  85.4 5.6 %collective-permute-done.66 = bf16[1,256,256]{2,1,0:T(8,128)(2,1)S(1)} collective-permute-done((bf16[1,256,256]{2,1,0:T(8,128)(2,1)S(1)}, bf16[1,256,256]{2,1,0:T(8,128)(2,1)S(1)}, u32[]{:S(2)}, u32[]{:S(2)}) %collective-permute-start.66) | collective-permute-done | bytes 131104 | tf_op jit(solution)/shard_map/cond/branch_6_fun/ppermute | solution.py:172
  92.6 2.3 %collective-permute-done.65 = bf16[256,1024]{1,0:T(8,128)(2,1)S(1)} collective-permute-done((bf16[256,1024]{1,0:T(8,128)(2,1)S(1)}, bf16[256,1024]{1,0:T(8,128)(2,1)S(1)}, u32[]{:S(2)}, u32[]{:S(2)}) %collective-permute-start.65) | collective-permute-done | bytes 524320 | tf_op jit(solution)/shard_map/cond/branch_6_fun/ppermute | solution.py:187
  95.1 30.0 %conditional.7 = (bf16[256,1024]{1,0:T(8,128)(2,1)S(1)}, bf16[256,1024]{1,0:T(8,128)(2,1)S(1)}, bf16[256,1024]{1,0:T(8,128)(2,1)}) conditional(s32[]{:T(128)} %clamp.11, (bf16[256,1024]{1,0:T(8,128)(2,1)}, bf16[256,1024]{1,0:T(8,128)(2,1)S(1)}, bf16[256,1024]{1,0:T(8,128)(2,1)S(1)}) %tuple.531, ...), branch_computations={%region_64.65_spmd, %region_65.66_spmd, %region_66.67_spmd, %regio... | conditional | bytes 8388752 | solution.py:259
  95.2 5.7 %collective-permute-start.176 = (bf16[256,1024]{1,0:T(8,128)(2,1)S(1)}, bf16[256,1024]{1,0:T(8,128)(2,1)S(1)}, u32[]{:S(2)}, u32[]{:S(2)}) collective-permute-start(bf16[256,1024]{1,0:T(8,128)(2,1)S(1)} %get-tuple-element.833), channel_id=1, source_target_pairs={{0,128},{8,136},{16,144},{24,152},{32,160},{40,168},{48,176},{56,1... | collective-permute-start | bytes 1572872 | tf_op jit(solution)/shard_map/cond/branch_16_fun/ppermute | solution.py:187
  100.8 4.4 %collective-permute-start.177 = (bf16[256,1024]{1,0:T(8,128)(2,1)}, bf16[256,1024]{1,0:T(8,128)(2,1)}, u32[]{:S(2)}, u32[]{:S(2)}) collective-permute-start(bf16[256,1024]{1,0:T(8,128)(2,1)} %get-tuple-element.835), channel_id=1, source_target_pairs={{0,1},{1,0},{2,3},{3,2},{4,5},{5,4},{6,7},{7,6},{8,9},{9,8},{10,11... | collective-permute-start | bytes 1572872 | tf_op jit(solution)/shard_map/cond/branch_16_fun/ppermute | solution.py:159
  105.2 19.8 %collective-permute-done.176 = bf16[256,1024]{1,0:T(8,128)(2,1)S(1)} collective-permute-done((bf16[256,1024]{1,0:T(8,128)(2,1)S(1)}, bf16[256,1024]{1,0:T(8,128)(2,1)S(1)}, u32[]{:S(2)}, u32[]{:S(2)}) %collective-permute-start.176) | collective-permute-done | bytes 524320 | tf_op jit(solution)/shard_map/cond/branch_16_fun/ppermute | solution.py:187
  125.1 3.5 %collective-permute-start.225 = (bf16[256,1024]{1,0:T(8,128)(2,1)S(1)}, bf16[256,1024]{1,0:T(8,128)(2,1)S(1)}, u32[]{:S(2)}, u32[]{:S(2)}) collective-permute-start(bf16[256,1024]{1,0:T(8,128)(2,1)S(1)} %get-tuple-element.926.refs_0_), channel_id=1, source_target_pairs={{0,1},{1,0},{2,3},{3,2},{4,5},{5,4},{6,7},{7,6},{8,9},{9,8},{10,11... | collective-permute-start | bytes 1572872 | tf_op jit(solution)/shard_map/ppermute | solution.py:159
  128.6 1.9 %collective-permute-start.226 = (bf16[256,1024]{1,0:T(8,128)(2,1)S(1)}, bf16[256,1024]{1,0:T(8,128)(2,1)S(1)}, u32[]{:S(2)}, u32[]{:S(2)}) collective-permute-start(bf16[256,1024]{1,0:T(8,128)(2,1)S(1)} %get-tuple-element.928.refs_4_), channel_id=1, source_target_pairs={{0,1},{1,0},{2,3},{3,2},{4,5},{5,4},{6,7},{7,6},{8,9},{9,8},{10,11... | collective-permute-start | bytes 1572872 | tf_op jit(solution)/shard_map/ppermute | solution.py:159
  132.4 2.2 %copy-done.2 = bf16[4,256,2048]{2,1,0:T(8,128)(2,1)S(1)} copy-done((bf16[4,256,2048]{2,1,0:T(8,128)(2,1)S(1)}, bf16[4,256,2048]{2,1,0:T(8,128)(2,1)}, u32[]{:S(2)}) %copy-start.2) | copy-done | bytes 4194328
  134.6 5.2 %next_pairs.1 = bf16[4,3,256,256]{3,2,1,0:T(8,128)(2,1)S(1)} custom-call(bf16[4,256,2048]{2,1,0:T(8,128)(2,1)S(1)} %copy-done.2, bf16[256,1024]{1,0:T(8,128)(2,1)S(1)} %get-tuple-element.926.refs_0_, bf16[256,1024]{1,0:T(8,128)(2,1)S(1)} %collective-permute-done.225.refs_1_, bf16[256,1024]{1,0:T(8,128)(2,1)} %get-tuple-element.923.refs_2_, ...), custom_call_target="tpu_custom_call" | custom-call | flops 6442450944 | bytes 4194304 | tf_op jit(solution)/shard_map/next_pairs/pallas_call | solution.py:145
  140.0 2.3 %collective-permute-start.227 = (bf16[3,256,256]{2,1,0:T(8,128)(2,1)S(1)}, bf16[3,256,256]{2,1,0:T(8,128)(2,1)S(1)}, u32[]{:S(2)}, u32[]{:S(2)}) collective-permute-start(bf16[3,256,256]{2,1,0:T(8,128)(2,1)S(1)} %get-tuple-element.935), channel_id=1, source_target_pairs={{0,4},{1,5},{2,6},{3,7},{4,0},{5,1},{6,2},{7,3},{8,12},{9,13},{10,... | collective-permute-start | bytes 1179656 | tf_op jit(solution)/shard_map/ppermute | solution.py:180
  142.3 3.8 %collective-permute-start.229 = (bf16[3,256,256]{2,1,0:T(8,128)(2,1)S(1)}, bf16[3,256,256]{2,1,0:T(8,128)(2,1)S(1)}, u32[]{:S(2)}, u32[]{:S(2)}) collective-permute-start(bf16[3,256,256]{2,1,0:T(8,128)(2,1)S(1)} %get-tuple-element.936), channel_id=1, source_target_pairs={{0,6},{1,7},{2,4},{3,5},{4,2},{5,3},{6,0},{7,1},{8,14},{9,15},{10,... | collective-permute-start | bytes 1179656 | tf_op jit(solution)/shard_map/ppermute | solution.py:180
  146.1 3.2 %collective-permute-start.228 = (bf16[3,256,256]{2,1,0:T(8,128)(2,1)S(1)}, bf16[3,256,256]{2,1,0:T(8,128)(2,1)S(1)}, u32[]{:S(2)}, u32[]{:S(2)}) collective-permute-start(bf16[3,256,256]{2,1,0:T(8,128)(2,1)S(1)} %get-tuple-element.937), channel_id=1, source_target_pairs={{0,2},{1,3},{2,0},{3,1},{4,6},{5,7},{6,4},{7,5},{8,10},{9,11},{10,... | collective-permute-start | bytes 1179656 | tf_op jit(solution)/shard_map/ppermute | solution.py:180
  149.3 18.3 %collective-permute-done.227 = bf16[3,256,256]{2,1,0:T(8,128)(2,1)S(1)} collective-permute-done((bf16[3,256,256]{2,1,0:T(8,128)(2,1)S(1)}, bf16[3,256,256]{2,1,0:T(8,128)(2,1)S(1)}, u32[]{:S(2)}, u32[]{:S(2)}) %collective-permute-start.227) | collective-permute-done | bytes 393248 | tf_op jit(solution)/shard_map/ppermute | solution.py:180
  167.6 11.3 %collective-permute-done.229 = bf16[3,256,256]{2,1,0:T(8,128)(2,1)S(1)} collective-permute-done((bf16[3,256,256]{2,1,0:T(8,128)(2,1)S(1)}, bf16[3,256,256]{2,1,0:T(8,128)(2,1)S(1)}, u32[]{:S(2)}, u32[]{:S(2)}) %collective-permute-start.229) | collective-permute-done | bytes 393248 | tf_op jit(solution)/shard_map/ppermute | solution.py:180
  (34 shorter events, 9.9 us)
Async XLA Ops:
  0.0 7.7 %copy-start.3 = (s32[256]{0:T(256)S(1)}, s32[256]{0:T(256)}, u32[]{:S(2)}) copy-start(s32[256]{0:T(256)} %param.101) | copy-start | bytes 3076
  1.2 24.4 %copy-start = (s32[3,64]{1,0:T(4,128)S(1)}, s32[3,64]{1,0:T(4,128)}, u32[]{:S(2)}) copy-start(s32[3,64]{1,0:T(4,128)} %mask_ref.1) | copy-start | bytes 2308
  1.2 8.9 %collective-permute-start.221 = (bf16[256,512]{1,0:T(8,128)(2,1)S(1)}, bf16[256,512]{1,0:T(8,128)(2,1)S(1)}, u32[]{:S(2)}, u32[]{:S(2)}) collective-permute-start(bf16[256,512]{1,0:T(8,128)(2,1)S(1)} %get-tuple-element.940), channel_id=1, source_target_pairs={{1,0},{2,1},{3,2},{4,3},{5,4},{6,5},{7,6},{9,8},{10,9},{11,10},{12... | collective-permute-start | bytes 786440 | tf_op jit(solution)/shard_map/ppermute | solution.py:228
  3.8 7.2 %collective-permute-start.220 = (bf16[256,512]{1,0:T(8,128)(2,1)S(1)}, bf16[256,512]{1,0:T(8,128)(2,1)S(1)}, u32[]{:S(2)}, u32[]{:S(2)}) collective-permute-start(bf16[256,512]{1,0:T(8,128)(2,1)S(1)} %get-tuple-element.941), channel_id=1, source_target_pairs={{0,1},{1,2},{2,3},{3,4},{4,5},{5,6},{6,7},{8,9},{9,10},{10,11},{11... | collective-permute-start | bytes 786440 | tf_op jit(solution)/shard_map/ppermute | solution.py:227
  13.1 31.4 %collective-permute-start.223 = (bf16[256,1024]{1,0:T(8,128)(2,1)S(1)}, bf16[256,1024]{1,0:T(8,128)(2,1)S(1)}, u32[]{:S(2)}, u32[]{:S(2)}) collective-permute-start(bf16[256,1024]{1,0:T(8,128)(2,1)S(1)} %whiten.1.mine_ref.own), channel_id=1, source_target_pairs={{0,256},{8,264},{16,272},{24,280},{32,288},{40,296},{48,304},{56,3... | collective-permute-start | bytes 1572872 | tf_op jit(solution)/shard_map/ppermute | solution.py:187
  21.9 8.9 %collective-permute-start.222 = (bf16[256,1024]{1,0:T(8,128)(2,1)S(1)}, bf16[256,1024]{1,0:T(8,128)(2,1)S(1)}, u32[]{:S(2)}, u32[]{:S(2)}) collective-permute-start(bf16[256,1024]{1,0:T(8,128)(2,1)S(1)} %whiten.1.mine_ref.own), channel_id=1, source_target_pairs={{0,1},{1,0},{2,3},{3,2},{4,5},{5,4},{6,7},{7,6},{8,9},{9,8},{10,11... | collective-permute-start | bytes 1572872 | tf_op jit(solution)/shard_map/ppermute | solution.py:159
  36.4 2.0 %copy-start.1 = (bf16[4,256,2048]{2,1,0:T(8,128)(2,1)}, bf16[4,256,2048]{2,1,0:T(8,128)(2,1)S(1)}, u32[]{:S(2)}) copy-start(bf16[4,256,2048]{2,1,0:T(8,128)(2,1)S(1)} %get-tuple-element.921.turned_ref) | copy-start | bytes 12582916
  44.5 32.3 %collective-permute-start.224 = (bf16[2,1,256,256]{3,2,1,0:T(8,128)(2,1)S(1)}, bf16[2,1,256,256]{3,2,1,0:T(8,128)(2,1)S(1)}, u32[]{:S(2)}, u32[]{:S(2)}) collective-permute-start(bf16[2,1,256,256]{3,2,1,0:T(8,128)(2,1)S(1)} %slice.70), channel_id=1, source_target_pairs={{0,2},{1,3},{2,0},{3,1},{4,6},{5,7},{6,4},{7,5},{8,10},{9,11},{10,... | collective-permute-start | bytes 786440 | tf_op jit(solution)/shard_map/ppermute | solution.py:165
  48.0 28.8 %collective-permute-start.38 = (bf16[256,1024]{1,0:T(8,128)(2,1)S(1)}, bf16[256,1024]{1,0:T(8,128)(2,1)S(1)}, u32[]{:S(2)}, u32[]{:S(2)}) collective-permute-start(bf16[256,1024]{1,0:T(8,128)(2,1)S(1)} %get-tuple-element.641), channel_id=1, source_target_pairs={{0,192},{8,200},{16,208},{24,216},{32,224},{40,232},{48,240},{56,2... | collective-permute-start | bytes 1572872 | tf_op jit(solution)/shard_map/cond/branch_24_fun/ppermute | solution.py:187
  77.0 14.8 %collective-permute-start.64 = (bf16[256,1024]{1,0:T(8,128)(2,1)}, bf16[256,1024]{1,0:T(8,128)(2,1)S(1)}, u32[]{:S(2)}, u32[]{:S(2)}) collective-permute-start(bf16[256,1024]{1,0:T(8,128)(2,1)} %get-tuple-element.681), channel_id=1, source_target_pairs={{0,32},{8,40},{16,48},{24,56},{32,0},{40,8},{48,16},{56,24},{64,96... | collective-permute-start | bytes 1572872 | tf_op jit(solution)/shard_map/cond/branch_6_fun/ppermute | solution.py:187
  78.9 15.9 %collective-permute-start.65 = (bf16[256,1024]{1,0:T(8,128)(2,1)S(1)}, bf16[256,1024]{1,0:T(8,128)(2,1)S(1)}, u32[]{:S(2)}, u32[]{:S(2)}) collective-permute-start(bf16[256,1024]{1,0:T(8,128)(2,1)S(1)} %get-tuple-element.682), channel_id=1, source_target_pairs={{0,16},{8,24},{16,0},{24,8},{32,48},{40,56},{48,32},{56,40},{64,80... | collective-permute-start | bytes 1572872 | tf_op jit(solution)/shard_map/cond/branch_6_fun/ppermute | solution.py:187
  82.7 8.3 %collective-permute-start.66 = (bf16[1,256,256]{2,1,0:T(8,128)(2,1)S(1)}, bf16[1,256,256]{2,1,0:T(8,128)(2,1)S(1)}, u32[]{:S(2)}, u32[]{:S(2)}) collective-permute-start(bf16[1,256,256]{2,1,0:T(8,128)(2,1)S(1)} %get-tuple-element.684), channel_id=1, source_target_pairs={{0,4},{1,5},{2,6},{3,7},{4,0},{5,1},{6,2},{7,3},{8,12},{9,13},{10,... | collective-permute-start | bytes 393224 | tf_op jit(solution)/shard_map/cond/branch_6_fun/ppermute | solution.py:172
  95.2 29.9 %collective-permute-start.176 = (bf16[256,1024]{1,0:T(8,128)(2,1)S(1)}, bf16[256,1024]{1,0:T(8,128)(2,1)S(1)}, u32[]{:S(2)}, u32[]{:S(2)}) collective-permute-start(bf16[256,1024]{1,0:T(8,128)(2,1)S(1)} %get-tuple-element.833), channel_id=1, source_target_pairs={{0,128},{8,136},{16,144},{24,152},{32,160},{40,168},{48,176},{56,1... | collective-permute-start | bytes 1572872 | tf_op jit(solution)/shard_map/cond/branch_16_fun/ppermute | solution.py:187
  100.8 24.2 %collective-permute-start.177 = (bf16[256,1024]{1,0:T(8,128)(2,1)}, bf16[256,1024]{1,0:T(8,128)(2,1)}, u32[]{:S(2)}, u32[]{:S(2)}) collective-permute-start(bf16[256,1024]{1,0:T(8,128)(2,1)} %get-tuple-element.835), channel_id=1, source_target_pairs={{0,1},{1,0},{2,3},{3,2},{4,5},{5,4},{6,7},{7,6},{8,9},{9,8},{10,11... | collective-permute-start | bytes 1572872 | tf_op jit(solution)/shard_map/cond/branch_16_fun/ppermute | solution.py:159
  125.1 5.4 %collective-permute-start.225 = (bf16[256,1024]{1,0:T(8,128)(2,1)S(1)}, bf16[256,1024]{1,0:T(8,128)(2,1)S(1)}, u32[]{:S(2)}, u32[]{:S(2)}) collective-permute-start(bf16[256,1024]{1,0:T(8,128)(2,1)S(1)} %get-tuple-element.926.refs_0_), channel_id=1, source_target_pairs={{0,1},{1,0},{2,3},{3,2},{4,5},{5,4},{6,7},{7,6},{8,9},{9,8},{10,11... | collective-permute-start | bytes 1572872 | tf_op jit(solution)/shard_map/ppermute | solution.py:159
  128.6 3.8 %collective-permute-start.226 = (bf16[256,1024]{1,0:T(8,128)(2,1)S(1)}, bf16[256,1024]{1,0:T(8,128)(2,1)S(1)}, u32[]{:S(2)}, u32[]{:S(2)}) collective-permute-start(bf16[256,1024]{1,0:T(8,128)(2,1)S(1)} %get-tuple-element.928.refs_4_), channel_id=1, source_target_pairs={{0,1},{1,0},{2,3},{3,2},{4,5},{5,4},{6,7},{7,6},{8,9},{9,8},{10,11... | collective-permute-start | bytes 1572872 | tf_op jit(solution)/shard_map/ppermute | solution.py:159
  132.4 2.2 %copy-start.2 = (bf16[4,256,2048]{2,1,0:T(8,128)(2,1)S(1)}, bf16[4,256,2048]{2,1,0:T(8,128)(2,1)}, u32[]{:S(2)}) copy-start(bf16[4,256,2048]{2,1,0:T(8,128)(2,1)} %copy-done.1) | copy-start | bytes 12582916
  140.0 27.7 %collective-permute-start.227 = (bf16[3,256,256]{2,1,0:T(8,128)(2,1)S(1)}, bf16[3,256,256]{2,1,0:T(8,128)(2,1)S(1)}, u32[]{:S(2)}, u32[]{:S(2)}) collective-permute-start(bf16[3,256,256]{2,1,0:T(8,128)(2,1)S(1)} %get-tuple-element.935), channel_id=1, source_target_pairs={{0,4},{1,5},{2,6},{3,7},{4,0},{5,1},{6,2},{7,3},{8,12},{9,13},{10,... | collective-permute-start | bytes 1179656 | tf_op jit(solution)/shard_map/ppermute | solution.py:180
  142.3 36.7 %collective-permute-start.229 = (bf16[3,256,256]{2,1,0:T(8,128)(2,1)S(1)}, bf16[3,256,256]{2,1,0:T(8,128)(2,1)S(1)}, u32[]{:S(2)}, u32[]{:S(2)}) collective-permute-start(bf16[3,256,256]{2,1,0:T(8,128)(2,1)S(1)} %get-tuple-element.936), channel_id=1, source_target_pairs={{0,6},{1,7},{2,4},{3,5},{4,2},{5,3},{6,0},{7,1},{8,14},{9,15},{10,... | collective-permute-start | bytes 1179656 | tf_op jit(solution)/shard_map/ppermute | solution.py:180
  146.1 32.9 %collective-permute-start.228 = (bf16[3,256,256]{2,1,0:T(8,128)(2,1)S(1)}, bf16[3,256,256]{2,1,0:T(8,128)(2,1)S(1)}, u32[]{:S(2)}, u32[]{:S(2)}) collective-permute-start(bf16[3,256,256]{2,1,0:T(8,128)(2,1)S(1)} %get-tuple-element.937), channel_id=1, source_target_pairs={{0,2},{1,3},{2,0},{3,1},{4,6},{5,7},{6,4},{7,5},{8,10},{9,11},{10,... | collective-permute-start | bytes 1179656 | tf_op jit(solution)/shard_map/ppermute | solution.py:180
